TPU v7x, 32 devices: a whole 2x2x4 slice. The times are simulated.
32 devices in a mesh: parts: 1, chan: 16 (over z, y, core), tm: 2 (over x), freq: 1.
Axes of the slice: x: 2, y: 2, z: 4, core: 2. Of those that a mesh axis runs over, the one named last changes fastest.
Arguments:
- spectra: bfloat16 [2, 512, 16, 2048], P(None, 'freq', 'tm', ('parts', 'chan')), may hold values from -6 to 6
- owners: int32 [4], P('parts'), may hold values from 0 to 15
- source_rows: int32 [4, 16], P('parts'), may hold values from 0 to 127
Outputs:
- correlations: float32 [4, 16, 2048, 128], P(None, ('tm', 'freq'), ('parts', 'chan'))
All inputs are finite; a program needn't handle non-finite values.
Results may differ from a plain program's by a relative error of at most 0.0037.
Values may be sent and summed in bfloat16 or wider, within the bound.
No kernel may reach another device: no remote copies, remote signals or barrier semaphores. Data moves between devices by JAX's collectives and lax.ppermute only.
A program may use at most 64 MiB of HBM per device.

v0:
```python
import functools
import math

import jax
import jax.numpy as jnp
import numpy as np
from jax import lax
from jax.experimental import pallas as pl
from jax.experimental.pallas import tpu as pltpu
from jax.sharding import PartitionSpec as P

WINDOW_LEN = 4096
FIRST_BIN = 64
LAGS = 128
RANK = 64
BLOCK = 8
WATER = 0.5
VMEM_LIMIT = 48 * 1024 * 1024

CORE_MASK = 1
HOP_MASKS = (4, 2, 6)
CHUNKS = 8


def chunk_id(index):
    core = index & 1
    second = (index >> 1) & 1
    third = ((index >> 2) ^ (index >> 3)) & 1
    return core * 4 + second * 2 + third


def lag_basis(bins):
    k = FIRST_BIN + np.arange(bins)
    shifts = np.arange(LAGS) - LAGS // 2
    angle = 2.0 * np.pi * np.mod(k[:, None] * shifts[None, :], WINDOW_LEN) / WINDOW_LEN
    table = np.stack([np.cos(angle), -np.sin(angle)])
    _, _, rows = np.linalg.svd(table.reshape(2 * bins, LAGS), full_matrices=False)
    basis = rows[:RANK]
    return np.einsum("ofl,rl->ofr", table, basis), basis


def pick_kernel(shards, side, owners_in, rows_in, spectra, out, owners, rows, staged, sems):
    total = out.shape[3]
    steps = owners.shape[0]
    me = lax.axis_index("chan")
    mine = lax.axis_index("tm") * lax.axis_size("freq") + lax.axis_index("freq")
    place = chunk_id(me)
    scalars = [
        pltpu.make_async_copy(owners_in, owners, sems.at[4]),
        pltpu.make_async_copy(rows_in, rows, sems.at[5]),
    ]
    for copy in scalars:
        copy.start()
    keep = total // (steps * shards)
    fc = staged.shape[2]
    copies = []
    for j in range(4):
        at = pl.multiple_of((place ^ (side + j)) * fc, fc)
        copy = pltpu.make_async_copy(spectra.at[:, pl.ds(at, fc)], staged.at[j], sems.at[j])
        copy.start()
        copies.append(copy)
    for copy in scalars:
        copy.wait()
    sub = lax.broadcasted_iota(jnp.int32, (8, 128), 0)
    lane = lax.broadcasted_iota(jnp.int32, (8, 128), 1)
    hot = []
    for first in range(0, total, 8):
        want = jnp.full((8, 128), -1, jnp.int32)
        for i in range(8):
            d, rest = divmod(first + i, steps * keep)
            t, k = divmod(rest, keep)
            row = jnp.where(owners[t] == me, rows[t, (mine ^ d) * keep + k], -1)
            want = jnp.where(sub == i, row, want)
        hot.append(jnp.where(want == lane, 1.0, 0.0))
    hot = jnp.concatenate(hot, axis=0).astype(jnp.bfloat16)
    for j in range(4):
        copies[j].wait()
        for k in range(2):
            block = staged[j, k].reshape(-1, staged.shape[4])
            got = lax.dot_general(
                hot, block, (((1,), (1,)), ((), ())), preferred_element_type=jnp.float32
            ).astype(jnp.bfloat16)
            for g in range(out.shape[1]):
                out[j, g, k] = got[:, g * 128 : (g + 1) * 128]


def pick(owners, rows, spectra, shards, side):
    bins, win, chans = spectra.shape[1:]
    total = rows.size
    gc = bins * win // 128 // CHUNKS
    return pl.pallas_call(
        functools.partial(pick_kernel, shards, side),
        in_specs=[pl.BlockSpec(memory_space=pl.ANY)] * 3,
        out_specs=pl.BlockSpec(memory_space=pltpu.VMEM),
        out_shape=jax.ShapeDtypeStruct((4, gc, 2, total, 128), jnp.bfloat16),
        scratch_shapes=[
            pltpu.SMEM(owners.shape, jnp.int32),
            pltpu.SMEM(rows.shape, jnp.int32),
            pltpu.VMEM((4, 2, bins // CHUNKS, win, chans), jnp.bfloat16),
            pltpu.SemaphoreType.DMA((6,)),
        ],
        compiler_params=pltpu.CompilerParams(vmem_limit_bytes=VMEM_LIMIT),
        cost_estimate=pl.CostEstimate(
            flops=2 * bins * win * chans * total, bytes_accessed=2 << 20, transcendentals=0
        ),
        name="pick_sources",
    )(owners, rows, spectra)


def whiten_pair(real, imag):
    real = real.astype(jnp.float32)
    imag = imag.astype(jnp.float32)
    size = jnp.sqrt(real * real + imag * imag) + WATER
    return (real / size).astype(jnp.bfloat16), (imag / size).astype(jnp.bfloat16)


def whiten_kernel(meta, spectra, out):
    gc = out.shape[1]
    gf = spectra.shape[1] // gc
    for g in range(gc):
        real = spectra[0, g * gf : (g + 1) * gf].reshape(128, 128)
        imag = spectra[1, g * gf : (g + 1) * gf].reshape(128, 128)
        out[0, g, 0], out[0, g, 1] = whiten_pair(real, imag)


def whiten(meta, spectra):
    bins, win, chans = spectra.shape[1:]
    gc = bins * win // 128 // CHUNKS
    return pl.pallas_call(
        whiten_kernel,
        grid_spec=pltpu.PrefetchScalarGridSpec(
            num_scalar_prefetch=1,
            grid=(CHUNKS,),
            in_specs=[pl.BlockSpec((2, bins // CHUNKS, win, chans), lambda p, meta: (0, meta[0] ^ p, 0, 0))],
            out_specs=pl.BlockSpec((1, gc, 2, 128, 128), lambda p, meta: (p, 0, 0, 0, 0)),
        ),
        out_shape=jax.ShapeDtypeStruct((CHUNKS, gc, 2, 128, 128), jnp.bfloat16),
        compiler_params=pltpu.CompilerParams(vmem_limit_bytes=VMEM_LIMIT),
        cost_estimate=pl.CostEstimate(flops=1 << 24, bytes_accessed=4 << 20, transcendentals=1 << 20),
        name="whiten_block",
    )(meta, spectra)


def cross_kernel(places, first, begun, meta, *refs):
    sources, refs = refs[: len(places)], refs[len(places) :]
    if begun is not None:
        start, *refs = refs
    white, table, out, cross = refs
    count = out.shape[1] // 128
    gc = white.shape[1]
    gf = table.shape[2] // (2 * gc)
    win = 128 // gf
    row = lax.broadcasted_iota(jnp.int32, (gf, 128), 0)
    lane = lax.broadcasted_iota(jnp.int32, (gf, 128), 1)
    mask = jnp.where(lane // win == row, 1.0, 0.0).astype(jnp.bfloat16)
    for i, p in enumerate(places):
        for g in range(gc):
            wr = white[p, g, 0]
            wi = white[p, g, 1]
            right = jnp.concatenate(
                [jnp.concatenate([wr, wi], axis=1), jnp.concatenate([wi, -wr], axis=1)], axis=0
            )
            low = first // 16 * 16
            high = min(-(-(first + count) // 16) * 16, sources[i].shape[2])
            real = sources[i][g, 0, low:high].astype(jnp.float32)[first - low : first - low + count]
            imag = sources[i][g, 1, low:high].astype(jnp.float32)[first - low : first - low + count]
            step = math.gcd(8, count)
            for s0 in range(0, count, step):
                rows = []
                for s in range(s0, s0 + step):
                    lr = jnp.broadcast_to(real[s : s + 1], (gf, 128)).astype(jnp.bfloat16) * mask
                    li = jnp.broadcast_to(imag[s : s + 1], (gf, 128)).astype(jnp.bfloat16) * mask
                    rows.append(jnp.concatenate([lr, li], axis=1))
                left = jnp.concatenate(rows, axis=0)
                both = jnp.dot(left, right, preferred_element_type=jnp.float32).astype(jnp.bfloat16)
                for o in range(2):
                    at = (i * 2 + o) * gc * gf + g * gf
                    for s in range(step):
                        cross[at : at + gf, (s0 + s) * 128 : (s0 + s + 1) * 128] = both[
                            s * gf : (s + 1) * gf, o * 128 : (o + 1) * 128
                        ]
    left = jnp.concatenate([table[meta[0] ^ p] for p in places], axis=1)
    wide = math.gcd(4, count) * 128
    for n in range(count * 128 // wide):
        got = jnp.dot(left, cross[:, n * wide : (n + 1) * wide], preferred_element_type=jnp.float32)
        if begun is not None:
            got = got + start[:, begun * 128 + n * wide : begun * 128 + (n + 1) * wide]
        out[:, n * wide : (n + 1) * wide] = got.astype(out.dtype)


def coefficients(meta, chunks, places, start, white, table, first, count, dtype):
    gc = white.shape[1]
    operands = [chunks[p] for p in places] + ([] if start is None else [start[0]]) + [white, table]
    begun = None if start is None else start[1]
    return pl.pallas_call(
        functools.partial(cross_kernel, places, first, begun),
        in_specs=[pl.BlockSpec(memory_space=pltpu.SMEM)] + [pl.BlockSpec(memory_space=pltpu.VMEM)] * len(operands),
        out_specs=pl.BlockSpec(memory_space=pltpu.VMEM),
        out_shape=jax.ShapeDtypeStruct((RANK, count * 128), dtype),
        scratch_shapes=[pltpu.VMEM((len(places) * table.shape[2], count * 128), jnp.bfloat16)],
        compiler_params=pltpu.CompilerParams(vmem_limit_bytes=VMEM_LIMIT),
        cost_estimate=pl.CostEstimate(
            flops=len(places) * gc * count * 16 * 256 * 256 * 3, bytes_accessed=2 << 20, transcendentals=0
        ),
        name="cross_coefficients",
    )(meta, *operands)


def lags_kernel(own, *refs):
    *others, basis, out, staged, sems = refs
    blocks = sems.shape[0]
    size = out.shape[0] // blocks
    copies = []
    for i in range(blocks):
        for s in range(size):
            at = slice(s * 128, (s + 1) * 128)
            value = own[:, (i * size + s) * 128 : (i * size + s + 1) * 128]
            for other in others[i::blocks]:
                value = value + other[:, at].astype(jnp.float32)
            high = value.astype(jnp.bfloat16)
            low = (value - high.astype(jnp.float32)).astype(jnp.bfloat16)
            left = jnp.concatenate([high, low, high], axis=0)
            staged[i * size + s] = lax.dot_general(
                left, basis[...], (((0,), (0,)), ((), ())), preferred_element_type=jnp.float32
            )
        at = pl.ds(i * size, size)
        copy = pltpu.make_async_copy(staged.at[at], out.at[at], sems.at[i])
        copy.start()
        copies.append(copy)
    for copy in copies:
        copy.wait()


def to_lags(own, others, basis):
    count = own.shape[1] // 128
    operands = [own, *[block for blocks in others for block in blocks], basis]
    shape = (count, 128, LAGS)
    return pl.pallas_call(
        lags_kernel,
        in_specs=[pl.BlockSpec(memory_space=pltpu.VMEM)] * len(operands),
        out_specs=pl.BlockSpec(memory_space=pl.ANY),
        out_shape=jax.ShapeDtypeStruct(shape, jnp.float32),
        scratch_shapes=[pltpu.VMEM(shape, jnp.float32), pltpu.SemaphoreType.DMA((len(others[0]),))],
        compiler_params=pltpu.CompilerParams(vmem_limit_bytes=VMEM_LIMIT),
        cost_estimate=pl.CostEstimate(flops=count * 128 * 128 * 192 * 2, bytes_accessed=1 << 20, transcendentals=0),
        name="lags",
    )(*operands)


def per_device(size, spectra, owners, source_rows):
    bins = spectra.shape[1]
    steps, count = source_rows.shape
    shards = lax.axis_size("tm") * lax.axis_size("freq")
    keep = count // shards
    me = lax.axis_index("chan").astype(jnp.int32)
    meta = chunk_id(me).reshape(1)

    def across(block, mask):
        return lax.ppermute(block, "chan", [(i, i ^ mask) for i in range(size)])

    all_bins = bins * lax.axis_size("freq")
    table, basis = lag_basis(all_bins)
    windows = spectra.shape[2] * lax.axis_size("tm")
    table = jnp.asarray((table / windows).astype(jnp.bfloat16))
    if all_bins != bins:
        table = lax.dynamic_slice_in_dim(table, lax.axis_index("freq") * bins, bins, 1)
    table = jnp.transpose(table.reshape(2, CHUNKS, bins // CHUNKS, RANK), (1, 3, 0, 2)).reshape(CHUNKS, RANK, -1)
    high = basis.astype(jnp.bfloat16)
    low = (basis - high.astype(np.float64)).astype(jnp.bfloat16)
    basis = jnp.asarray(np.concatenate([high, high, low], axis=0))

    inputs = [pltpu.with_memory_space_constraint(x, pltpu.HBM) for x in (owners, source_rows, spectra)]
    away = pick(*inputs, shards, 4)
    home = pick(*inputs, shards, 0)
    half = home + across(away, CORE_MASK)
    half, spectra = lax.optimization_barrier((half, spectra))
    total = half[0]
    arrived = [across(half[j + 1], mask) for j, mask in enumerate(HOP_MASKS)]
    white = whiten(meta, spectra)
    arrived, white = lax.optimization_barrier((arrived, white))
    for part in arrived:
        total = total + part
    for mask in [12] * (size >= 16) + [16 << i for i in range(10) if 16 << i < size]:
        total = total + across(total, mask)
    own = jnp.stack(whiten_pair(total[:, 0], total[:, 1]), axis=1)
    arrived = [across(own, mask) for mask in HOP_MASKS]
    beside = across(own, CORE_MASK)
    begun = coefficients(
        meta, {0: own, 4: beside}, (0, 4), None, white, table, 0, source_rows.size, jnp.float32
    )
    *arrived, begun = lax.optimization_barrier((*arrived, begun))
    chunks = {}
    for j, chunk in enumerate(arrived):
        chunks[j + 1] = chunk
        chunks[j + 5] = across(chunk, CORE_MASK)
    every = steps * keep
    block = min(BLOCK, every)
    firsts = range(0, every, block)
    outer = every * (shards - 1)
    near = coefficients(meta, chunks, (1, 2, 3), (begun, every), white, table, every, outer, jnp.float32)
    sent = {}
    for first in firsts:
        for d in range(1, shards):
            at = d * every + first
            part = coefficients(
                meta, chunks, (5, 6, 7), (near, at - every), white, table, at, block, jnp.bfloat16
            )
            sent[first, d] = lax.ppermute(part, ("tm", "freq"), [(i, i ^ d) for i in range(shards)])
    kept = coefficients(meta, chunks, (1, 2, 3, 5, 6, 7), (begun, 0), white, table, 0, every, jnp.float32)
    others = [[sent[first, d] for first in firsts] for d in range(1, shards)]
    return to_lags(kept, others, basis).reshape(steps, keep, 128, LAGS)


def solution(mesh):
    placed = (P(None, "freq", "tm", ("parts", "chan")), P("parts"), P("parts", None))
    return jax.shard_map(
        functools.partial(per_device, mesh.shape["chan"]),
        mesh=mesh,
        in_specs=placed,
        out_specs=P(None, ("tm", "freq"), ("parts", "chan"), None),
        check_vma=False,
    )
```

profile of v0, /device:TPU:0, one launch (start us, length us, event | category | flops | bytes accessed | tf_op | source)
XLA Modules:
  0.0 52.2 jit_solution(4374916906382846354)
XLA Ops:
  0.0 1.8 %pick_sources.3 = bf16[4,4,2,64,128]{4,3,2,1,0:T(8,128)(2,1)S(1)} custom-call(s32[4]{0:T(128)} %owners_in.3, s32[4,16]{1,0:T(4,128)} %rows_in.3, bf16[2,512,8,128]{3,2,1,0:T(8,128)(2,1)} %spectra.4), custom_call_target="tpu_custom_call" | custom-call | flops 67108864 | bytes 2097152 | tf_op jit(solution)/shard_map/pick_sources/pallas_call | solution.py:91
  1.9 0.5 collective-permute-start
  2.4 1.9 %pick_sources.2 = bf16[4,4,2,64,128]{4,3,2,1,0:T(8,128)(2,1)S(1)} custom-call(s32[4]{0:T(128)} %owners_in.3, s32[4,16]{1,0:T(4,128)} %rows_in.3, bf16[2,512,8,128]{3,2,1,0:T(8,128)(2,1)} %spectra.4), custom_call_target="tpu_custom_call" | custom-call | flops 67108864 | bytes 2097152 | tf_op jit(solution)/shard_map/pick_sources/pallas_call | solution.py:91
  4.3 0.2 add.36
  4.6 2.7 %collective-permute-start.1 = (bf16[4,2,64,128]{3,2,1,0:T(8,128)(2,1)S(1)}, bf16[4,2,64,128]{3,2,1,0:T(8,128)(2,1)S(1)}, u32[]{:S(2)}, u32[]{:S(2)}) collective-permute-start(bf16[4,2,64,128]{3,2,1,0:T(8,128)(2,1)S(1)} %get-tuple-element.27), channel_id=1, source_target_pairs={{0,8},{2,10},{4,12},{6,14},{8,0},{10,2},{12,4},{14,6},{16,24},{18,... | collective-permute-start | bytes 393224 | tf_op jit(solution)/shard_map/ppermute | solution.py:259
  7.3 1.5 %collective-permute-start.2 = (bf16[4,2,64,128]{3,2,1,0:T(8,128)(2,1)S(1)}, bf16[4,2,64,128]{3,2,1,0:T(8,128)(2,1)S(1)}, u32[]{:S(2)}, u32[]{:S(2)}) collective-permute-start(bf16[4,2,64,128]{3,2,1,0:T(8,128)(2,1)S(1)} %get-tuple-element.26), channel_id=1, source_target_pairs={{0,4},{2,6},{4,0},{6,2},{8,12},{10,14},{12,8},{14,10},{16,20},{18,... | collective-permute-start | bytes 393224 | tf_op jit(solution)/shard_map/ppermute | solution.py:259
  8.8 1.5 %whiten_block.1.refs_2_.refs_7_.refs_4_ = bf16[8,4,2,128,128]{4,3,2,1,0:T(8,128)(2,1)S(1)} custom-call(s32[1]{0:T(128)} %bitcast.meta, bf16[2,512,8,128]{3,2,1,0:T(8,128)(2,1)S(1)} %copy-done), custom_call_target="tpu_custom_call" | custom-call | flops 16777216 | bytes 4194304 | tf_op jit(solution)/shard_map/whiten_block/pallas_call | solution.py:129
  10.4 1.0 %collective-permute-done.1 = bf16[4,2,64,128]{3,2,1,0:T(8,128)(2,1)S(1)} collective-permute-done((bf16[4,2,64,128]{3,2,1,0:T(8,128)(2,1)S(1)}, bf16[4,2,64,128]{3,2,1,0:T(8,128)(2,1)S(1)}, u32[]{:S(2)}, u32[]{:S(2)}) %collective-permute-start.1) | collective-permute-done | bytes 131104 | tf_op jit(solution)/shard_map/ppermute | solution.py:259
  11.4 4.2 %collective-permute-done.2 = bf16[4,2,64,128]{3,2,1,0:T(8,128)(2,1)S(1)} collective-permute-done((bf16[4,2,64,128]{3,2,1,0:T(8,128)(2,1)S(1)}, bf16[4,2,64,128]{3,2,1,0:T(8,128)(2,1)S(1)}, u32[]{:S(2)}, u32[]{:S(2)}) %collective-permute-start.2) | collective-permute-done | bytes 131104 | tf_op jit(solution)/shard_map/ppermute | solution.py:259
  15.6 3.3 %collective-permute-start.4 = (bf16[4,2,64,128]{3,2,1,0:T(8,128)(2,1)S(1)}, bf16[4,2,64,128]{3,2,1,0:T(8,128)(2,1)S(1)}, u32[]{:S(2)}, u32[]{:S(2)}) collective-permute-start(bf16[4,2,64,128]{3,2,1,0:T(8,128)(2,1)S(1)} %fusion.5), channel_id=1, source_target_pairs={{0,24},{2,26},{4,28},{6,30},{8,16},{10,18},{12,20},{14,22},{16,8},... | collective-permute-start | bytes 393224 | tf_op jit(solution)/shard_map/ppermute | solution.py:259
  18.9 3.6 %collective-permute-done.4 = bf16[4,2,64,128]{3,2,1,0:T(8,128)(2,1)S(1)} collective-permute-done((bf16[4,2,64,128]{3,2,1,0:T(8,128)(2,1)S(1)}, bf16[4,2,64,128]{3,2,1,0:T(8,128)(2,1)S(1)}, u32[]{:S(2)}, u32[]{:S(2)}) %collective-permute-start.4) | collective-permute-done | bytes 131104 | tf_op jit(solution)/shard_map/ppermute | solution.py:259
  22.5 0.1 fusion.3
  22.7 2.2 %collective-permute-start.5 = (bf16[4,2,64,128]{3,2,1,0:T(8,128)(2,1)S(1)}, bf16[4,2,64,128]{3,2,1,0:T(8,128)(2,1)S(1)}, u32[]{:S(2)}, u32[]{:S(2)}) collective-permute-start(bf16[4,2,64,128]{3,2,1,0:T(8,128)(2,1)S(1)} %pad_maximum_fusion.refs_0_), channel_id=1, source_target_pairs={{0,8},{2,10},{4,12},{6,14},{8,0},{10,2},{12,4},{14,6},{16,24},{18,... | collective-permute-start | bytes 393224 | tf_op jit(solution)/shard_map/ppermute | solution.py:259
  25.0 1.4 %collective-permute-start.6 = (bf16[4,2,64,128]{3,2,1,0:T(8,128)(2,1)S(1)}, bf16[4,2,64,128]{3,2,1,0:T(8,128)(2,1)S(1)}, u32[]{:S(2)}, u32[]{:S(2)}) collective-permute-start(bf16[4,2,64,128]{3,2,1,0:T(8,128)(2,1)S(1)} %pad_maximum_fusion.refs_0_), channel_id=1, source_target_pairs={{0,4},{2,6},{4,0},{6,2},{8,12},{10,14},{12,8},{14,10},{16,20},{18,... | collective-permute-start | bytes 393224 | tf_op jit(solution)/shard_map/ppermute | solution.py:259
  26.3 0.2 collective-permute-start.7
  26.5 2.0 %cross_coefficients.7.refs_6_.refs_3_ = f32[64,8192]{1,0:T(8,128)S(1)} custom-call(s32[1]{0:T(128)} %bitcast.meta, bf16[4,2,64,128]{3,2,1,0:T(8,128)(2,1)S(1)} %pad_maximum_fusion.refs_0_, bf16[4,2,64,128]{3,2,1,0:T(8,128)(2,1)S(1)} %collective-permute-done.8.refs_1_, bf16[8,4,2,128,128]{4,3,2,1,0:T(8,128)(2,1)S(1)} %whiten_block.1.refs_2_.refs_7_.refs_4_, ...), custom_call_target="tpu_custom_call" | custom-call | flops 1610612736 | bytes 2097152 | tf_op jit(solution)/shard_map/cross_coefficients/pallas_call | solution.py:195
  28.5 0.6 %collective-permute-done.5.refs_0_ = bf16[4,2,64,128]{3,2,1,0:T(8,128)(2,1)S(1)} collective-permute-done((bf16[4,2,64,128]{3,2,1,0:T(8,128)(2,1)S(1)}, bf16[4,2,64,128]{3,2,1,0:T(8,128)(2,1)S(1)}, u32[]{:S(2)}, u32[]{:S(2)}) %collective-permute-start.5) | collective-permute-done | bytes 131104 | tf_op jit(solution)/shard_map/ppermute | solution.py:259
  29.1 4.2 %collective-permute-done.6.refs_1_ = bf16[4,2,64,128]{3,2,1,0:T(8,128)(2,1)S(1)} collective-permute-done((bf16[4,2,64,128]{3,2,1,0:T(8,128)(2,1)S(1)}, bf16[4,2,64,128]{3,2,1,0:T(8,128)(2,1)S(1)}, u32[]{:S(2)}, u32[]{:S(2)}) %collective-permute-start.6) | collective-permute-done | bytes 131104 | tf_op jit(solution)/shard_map/ppermute | solution.py:259
  33.3 0.5 collective-permute-start.11
  33.9 1.6 %cross_coefficients.9.refs_3_ = f32[64,4096]{1,0:T(8,128)S(1)} custom-call(s32[1]{0:T(128)} %bitcast.meta, bf16[4,2,64,128]{3,2,1,0:T(8,128)(2,1)S(1)} %collective-permute-done.5.refs_0_, bf16[4,2,64,128]{3,2,1,0:T(8,128)(2,1)S(1)} %collective-permute-done.6.refs_1_, bf16[4,2,64,128]{3,2,1,0:T(8,128)(2,1)S(1)} %collective-permute-done.7.refs_2_, ...), custom_call_target="tpu_custom_call" | custom-call | flops 1207959552 | bytes 2097152 | tf_op jit(solution)/shard_map/cross_coefficients/pallas_call | solution.py:195
  35.5 0.6 %cross_coefficients.13 = bf16[64,1024]{1,0:T(8,128)(2,1)S(1)} custom-call(s32[1]{0:T(128)} %bitcast.meta, bf16[4,2,64,128]{3,2,1,0:T(8,128)(2,1)S(1)} %collective-permute-done.9.refs_3_.refs_0_, bf16[4,2,64,128]{3,2,1,0:T(8,128)(2,1)S(1)} %collective-permute-done.10.refs_4_.refs_1_, bf16[4,2,64,128]{3,2,1,0:T(8,128)(2,1)S(1)} %collective-permute-done.11.refs_5_.refs_2_, ...), custom_call_target="tpu_custom_call" | custom-call | flops 301989888 | bytes 2097152 | tf_op jit(solution)/shard_map/cross_coefficients/pallas_call | solution.py:195
  36.1 1.6 %collective-permute-start.15 = (bf16[64,1024]{1,0:T(8,128)(2,1)S(1)}, bf16[64,1024]{1,0:T(8,128)(2,1)S(1)}, u32[]{:S(2)}, u32[]{:S(2)}) collective-permute-start(bf16[64,1024]{1,0:T(8,128)(2,1)S(1)} %cross_coefficients.13), channel_id=1, source_target_pairs={{0,1},{1,0},{2,3},{3,2},{4,5},{5,4},{6,7},{7,6},{8,9},{9,8},{10,11... | collective-permute-start | bytes 393224 | tf_op jit(solution)/shard_map/ppermute | solution.py:308
  37.6 0.6 %cross_coefficients.12 = bf16[64,1024]{1,0:T(8,128)(2,1)S(1)} custom-call(s32[1]{0:T(128)} %bitcast.meta, bf16[4,2,64,128]{3,2,1,0:T(8,128)(2,1)S(1)} %collective-permute-done.9.refs_3_.refs_0_, bf16[4,2,64,128]{3,2,1,0:T(8,128)(2,1)S(1)} %collective-permute-done.10.refs_4_.refs_1_, bf16[4,2,64,128]{3,2,1,0:T(8,128)(2,1)S(1)} %collective-permute-done.11.refs_5_.refs_2_, ...), custom_call_target="tpu_custom_call" | custom-call | flops 301989888 | bytes 2097152 | tf_op jit(solution)/shard_map/cross_coefficients/pallas_call | solution.py:195
  38.2 0.6 %collective-permute-start.14 = (bf16[64,1024]{1,0:T(8,128)(2,1)S(1)}, bf16[64,1024]{1,0:T(8,128)(2,1)S(1)}, u32[]{:S(2)}, u32[]{:S(2)}) collective-permute-start(bf16[64,1024]{1,0:T(8,128)(2,1)S(1)} %cross_coefficients.12), channel_id=1, source_target_pairs={{0,1},{1,0},{2,3},{3,2},{4,5},{5,4},{6,7},{7,6},{8,9},{9,8},{10,11... | collective-permute-start | bytes 393224 | tf_op jit(solution)/shard_map/ppermute | solution.py:308
  38.8 0.6 %cross_coefficients.11 = bf16[64,1024]{1,0:T(8,128)(2,1)S(1)} custom-call(s32[1]{0:T(128)} %bitcast.meta, bf16[4,2,64,128]{3,2,1,0:T(8,128)(2,1)S(1)} %collective-permute-done.9.refs_3_.refs_0_, bf16[4,2,64,128]{3,2,1,0:T(8,128)(2,1)S(1)} %collective-permute-done.10.refs_4_.refs_1_, bf16[4,2,64,128]{3,2,1,0:T(8,128)(2,1)S(1)} %collective-permute-done.11.refs_5_.refs_2_, ...), custom_call_target="tpu_custom_call" | custom-call | flops 301989888 | bytes 2097152 | tf_op jit(solution)/shard_map/cross_coefficients/pallas_call | solution.py:195
  39.4 1.5 %collective-permute-start.13 = (bf16[64,1024]{1,0:T(8,128)(2,1)S(1)}, bf16[64,1024]{1,0:T(8,128)(2,1)S(1)}, u32[]{:S(2)}, u32[]{:S(2)}) collective-permute-start(bf16[64,1024]{1,0:T(8,128)(2,1)S(1)} %cross_coefficients.11), channel_id=1, source_target_pairs={{0,1},{1,0},{2,3},{3,2},{4,5},{5,4},{6,7},{7,6},{8,9},{9,8},{10,11... | collective-permute-start | bytes 393224 | tf_op jit(solution)/shard_map/ppermute | solution.py:308
  41.0 0.6 %cross_coefficients.10 = bf16[64,1024]{1,0:T(8,128)(2,1)S(1)} custom-call(s32[1]{0:T(128)} %bitcast.meta, bf16[4,2,64,128]{3,2,1,0:T(8,128)(2,1)S(1)} %collective-permute-done.9.refs_3_.refs_0_, bf16[4,2,64,128]{3,2,1,0:T(8,128)(2,1)S(1)} %collective-permute-done.10.refs_4_.refs_1_, bf16[4,2,64,128]{3,2,1,0:T(8,128)(2,1)S(1)} %collective-permute-done.11.refs_5_.refs_2_, ...), custom_call_target="tpu_custom_call" | custom-call | flops 301989888 | bytes 2097152 | tf_op jit(solution)/shard_map/cross_coefficients/pallas_call | solution.py:195
  41.6 0.6 %collective-permute-start.12 = (bf16[64,1024]{1,0:T(8,128)(2,1)S(1)}, bf16[64,1024]{1,0:T(8,128)(2,1)S(1)}, u32[]{:S(2)}, u32[]{:S(2)}) collective-permute-start(bf16[64,1024]{1,0:T(8,128)(2,1)S(1)} %cross_coefficients.10), channel_id=1, source_target_pairs={{0,1},{1,0},{2,3},{3,2},{4,5},{5,4},{6,7},{7,6},{8,9},{9,8},{10,11... | collective-permute-start | bytes 393224 | tf_op jit(solution)/shard_map/ppermute | solution.py:308
  42.2 3.0 %cross_coefficients.8.own = f32[64,4096]{1,0:T(8,128)S(1)} custom-call(s32[1]{0:T(128)} %bitcast.meta, bf16[4,2,64,128]{3,2,1,0:T(8,128)(2,1)S(1)} %collective-permute-done.5.refs_0_, bf16[4,2,64,128]{3,2,1,0:T(8,128)(2,1)S(1)} %collective-permute-done.6.refs_1_, bf16[4,2,64,128]{3,2,1,0:T(8,128)(2,1)S(1)} %collective-permute-done.7.refs_2_, ...), custom_call_target="tpu_custom_call" | custom-call | flops 2415919104 | bytes 2097152 | tf_op jit(solution)/shard_map/cross_coefficients/pallas_call | solution.py:195
  45.3 2.8 %collective-permute-done.13.refs_1_ = bf16[64,1024]{1,0:T(8,128)(2,1)S(1)} collective-permute-done((bf16[64,1024]{1,0:T(8,128)(2,1)S(1)}, bf16[64,1024]{1,0:T(8,128)(2,1)S(1)}, u32[]{:S(2)}, u32[]{:S(2)}) %collective-permute-start.13) | collective-permute-done | bytes 131104 | tf_op jit(solution)/shard_map/ppermute | solution.py:308
  48.1 2.4 %collective-permute-done.12.refs_0_ = bf16[64,1024]{1,0:T(8,128)(2,1)S(1)} collective-permute-done((bf16[64,1024]{1,0:T(8,128)(2,1)S(1)}, bf16[64,1024]{1,0:T(8,128)(2,1)S(1)}, u32[]{:S(2)}, u32[]{:S(2)}) %collective-permute-start.12) | collective-permute-done | bytes 131104 | tf_op jit(solution)/shard_map/ppermute | solution.py:308
  50.5 1.7 %lags.1 = f32[32,128,128]{2,1,0:T(8,128)} custom-call(f32[64,4096]{1,0:T(8,128)S(1)} %cross_coefficients.8.own, bf16[64,1024]{1,0:T(8,128)(2,1)S(1)} %collective-permute-done.12.refs_0_, bf16[64,1024]{1,0:T(8,128)(2,1)S(1)} %collective-permute-done.13.refs_1_, bf16[64,1024]{1,0:T(8,128)(2,1)S(1)} %collective-permute-done.14.refs_2_, ...), custom_call_target="tpu_custom_call" | custom-call | flops 201326592 | bytes 1048576 | tf_op jit(solution)/shard_map/lags/pallas_call | solution.py:238
  (23 shorter events, 0.3 us)
Async XLA Ops:
  1.9 7.0 %copy-start = (bf16[2,512,8,128]{3,2,1,0:T(8,128)(2,1)S(1)}, bf16[2,512,8,128]{3,2,1,0:T(8,128)(2,1)}, u32[]{:S(2)}) copy-start(bf16[2,512,8,128]{3,2,1,0:T(8,128)(2,1)} %spectra.4) | copy-start | bytes 6291460
  1.9 2.5 %collective-permute-start = (bf16[4,4,2,64,128]{4,3,2,1,0:T(8,128)(2,1)S(1)}, bf16[4,4,2,64,128]{4,3,2,1,0:T(8,128)(2,1)S(1)}, u32[]{:S(2)}, u32[]{:S(2)}) collective-permute-start(bf16[4,4,2,64,128]{4,3,2,1,0:T(8,128)(2,1)S(1)} %pick_sources.3), channel_id=1, source_target_pairs={{0,2},{2,0},{4,6},{6,4},{8,10},{10,8},{12,14},{14,12},{16,18},{18,... | collective-permute-start | bytes 1572872 | tf_op jit(solution)/shard_map/ppermute | solution.py:259
  4.6 6.8 %collective-permute-start.1 = (bf16[4,2,64,128]{3,2,1,0:T(8,128)(2,1)S(1)}, bf16[4,2,64,128]{3,2,1,0:T(8,128)(2,1)S(1)}, u32[]{:S(2)}, u32[]{:S(2)}) collective-permute-start(bf16[4,2,64,128]{3,2,1,0:T(8,128)(2,1)S(1)} %get-tuple-element.27), channel_id=1, source_target_pairs={{0,8},{2,10},{4,12},{6,14},{8,0},{10,2},{12,4},{14,6},{16,24},{18,... | collective-permute-start | bytes 393224 | tf_op jit(solution)/shard_map/ppermute | solution.py:259
  7.3 8.3 %collective-permute-start.2 = (bf16[4,2,64,128]{3,2,1,0:T(8,128)(2,1)S(1)}, bf16[4,2,64,128]{3,2,1,0:T(8,128)(2,1)S(1)}, u32[]{:S(2)}, u32[]{:S(2)}) collective-permute-start(bf16[4,2,64,128]{3,2,1,0:T(8,128)(2,1)S(1)} %get-tuple-element.26), channel_id=1, source_target_pairs={{0,4},{2,6},{4,0},{6,2},{8,12},{10,14},{12,8},{14,10},{16,20},{18,... | collective-permute-start | bytes 393224 | tf_op jit(solution)/shard_map/ppermute | solution.py:259
  8.8 6.8 %collective-permute-start.3 = (bf16[4,2,64,128]{3,2,1,0:T(8,128)(2,1)S(1)}, bf16[4,2,64,128]{3,2,1,0:T(8,128)(2,1)S(1)}, u32[]{:S(2)}, u32[]{:S(2)}) collective-permute-start(bf16[4,2,64,128]{3,2,1,0:T(8,128)(2,1)S(1)} %get-tuple-element.25), channel_id=1, source_target_pairs={{0,12},{2,14},{4,8},{6,10},{8,4},{10,6},{12,0},{14,2},{16,28},{18,... | collective-permute-start | bytes 393224 | tf_op jit(solution)/shard_map/ppermute | solution.py:259
  8.8 17.7 %copy-start.1 = (bf16[8,64,128]{2,1,0:T(8,128)(2,1)S(1)}, bf16[8,64,128]{2,1,0:T(8,128)(2,1)}, u32[]{:S(2)}) copy-start(bf16[8,64,128]{2,1,0:T(8,128)(2,1)} %constant.24.refs_3_.refs_8_.refs_5_) | copy-start | bytes 393220
  15.6 6.9 %collective-permute-start.4 = (bf16[4,2,64,128]{3,2,1,0:T(8,128)(2,1)S(1)}, bf16[4,2,64,128]{3,2,1,0:T(8,128)(2,1)S(1)}, u32[]{:S(2)}, u32[]{:S(2)}) collective-permute-start(bf16[4,2,64,128]{3,2,1,0:T(8,128)(2,1)S(1)} %fusion.5), channel_id=1, source_target_pairs={{0,24},{2,26},{4,28},{6,30},{8,16},{10,18},{12,20},{14,22},{16,8},... | collective-permute-start | bytes 393224 | tf_op jit(solution)/shard_map/ppermute | solution.py:259
  22.6 3.9 %collective-permute-start.8 = (bf16[4,2,64,128]{3,2,1,0:T(8,128)(2,1)S(1)}, bf16[4,2,64,128]{3,2,1,0:T(8,128)(2,1)S(1)}, u32[]{:S(2)}, u32[]{:S(2)}) collective-permute-start(bf16[4,2,64,128]{3,2,1,0:T(8,128)(2,1)S(1)} %pad_maximum_fusion.refs_0_), channel_id=1, source_target_pairs={{0,2},{2,0},{4,6},{6,4},{8,10},{10,8},{12,14},{14,12},{16,18},{18,... | collective-permute-start | bytes 393224 | tf_op jit(solution)/shard_map/ppermute | solution.py:259
  22.7 6.4 %collective-permute-start.5 = (bf16[4,2,64,128]{3,2,1,0:T(8,128)(2,1)S(1)}, bf16[4,2,64,128]{3,2,1,0:T(8,128)(2,1)S(1)}, u32[]{:S(2)}, u32[]{:S(2)}) collective-permute-start(bf16[4,2,64,128]{3,2,1,0:T(8,128)(2,1)S(1)} %pad_maximum_fusion.refs_0_), channel_id=1, source_target_pairs={{0,8},{2,10},{4,12},{6,14},{8,0},{10,2},{12,4},{14,6},{16,24},{18,... | collective-permute-start | bytes 393224 | tf_op jit(solution)/shard_map/ppermute | solution.py:259
  25.0 8.4 %collective-permute-start.6 = (bf16[4,2,64,128]{3,2,1,0:T(8,128)(2,1)S(1)}, bf16[4,2,64,128]{3,2,1,0:T(8,128)(2,1)S(1)}, u32[]{:S(2)}, u32[]{:S(2)}) collective-permute-start(bf16[4,2,64,128]{3,2,1,0:T(8,128)(2,1)S(1)} %pad_maximum_fusion.refs_0_), channel_id=1, source_target_pairs={{0,4},{2,6},{4,0},{6,2},{8,12},{10,14},{12,8},{14,10},{16,20},{18,... | collective-permute-start | bytes 393224 | tf_op jit(solution)/shard_map/ppermute | solution.py:259
  26.3 7.0 %collective-permute-start.7 = (bf16[4,2,64,128]{3,2,1,0:T(8,128)(2,1)S(1)}, bf16[4,2,64,128]{3,2,1,0:T(8,128)(2,1)S(1)}, u32[]{:S(2)}, u32[]{:S(2)}) collective-permute-start(bf16[4,2,64,128]{3,2,1,0:T(8,128)(2,1)S(1)} %pad_maximum_fusion.refs_0_), channel_id=1, source_target_pairs={{0,12},{2,14},{4,8},{6,10},{8,4},{10,6},{12,0},{14,2},{16,28},{18,... | collective-permute-start | bytes 393224 | tf_op jit(solution)/shard_map/ppermute | solution.py:259
  33.3 2.1 %collective-permute-start.10 = (bf16[4,2,64,128]{3,2,1,0:T(8,128)(2,1)S(1)}, bf16[4,2,64,128]{3,2,1,0:T(8,128)(2,1)S(1)}, u32[]{:S(2)}, u32[]{:S(2)}) collective-permute-start(bf16[4,2,64,128]{3,2,1,0:T(8,128)(2,1)S(1)} %collective-permute-done.6.refs_1_), channel_id=1, source_target_pairs={{0,2},{2,0},{4,6},{6,4},{8,10},{10,8},{12,14},{14,12},{16,18},{18,... | collective-permute-start | bytes 393224 | tf_op jit(solution)/shard_map/ppermute | solution.py:259
  33.3 2.1 %collective-permute-start.11 = (bf16[4,2,64,128]{3,2,1,0:T(8,128)(2,1)S(1)}, bf16[4,2,64,128]{3,2,1,0:T(8,128)(2,1)S(1)}, u32[]{:S(2)}, u32[]{:S(2)}) collective-permute-start(bf16[4,2,64,128]{3,2,1,0:T(8,128)(2,1)S(1)} %collective-permute-done.7.refs_2_), channel_id=1, source_target_pairs={{0,2},{2,0},{4,6},{6,4},{8,10},{10,8},{12,14},{14,12},{16,18},{18,... | collective-permute-start | bytes 393224 | tf_op jit(solution)/shard_map/ppermute | solution.py:259
  33.9 1.6 %collective-permute-start.9 = (bf16[4,2,64,128]{3,2,1,0:T(8,128)(2,1)S(1)}, bf16[4,2,64,128]{3,2,1,0:T(8,128)(2,1)S(1)}, u32[]{:S(2)}, u32[]{:S(2)}) collective-permute-start(bf16[4,2,64,128]{3,2,1,0:T(8,128)(2,1)S(1)} %collective-permute-done.5.refs_0_), channel_id=1, source_target_pairs={{0,2},{2,0},{4,6},{6,4},{8,10},{10,8},{12,14},{14,12},{16,18},{18,... | collective-permute-start | bytes 393224 | tf_op jit(solution)/shard_map/ppermute | solution.py:259
  36.1 9.1 %collective-permute-start.15 = (bf16[64,1024]{1,0:T(8,128)(2,1)S(1)}, bf16[64,1024]{1,0:T(8,128)(2,1)S(1)}, u32[]{:S(2)}, u32[]{:S(2)}) collective-permute-start(bf16[64,1024]{1,0:T(8,128)(2,1)S(1)} %cross_coefficients.13), channel_id=1, source_target_pairs={{0,1},{1,0},{2,3},{3,2},{4,5},{5,4},{6,7},{7,6},{8,9},{9,8},{10,11... | collective-permute-start | bytes 393224 | tf_op jit(solution)/shard_map/ppermute | solution.py:308
  38.2 7.0 %collective-permute-start.14 = (bf16[64,1024]{1,0:T(8,128)(2,1)S(1)}, bf16[64,1024]{1,0:T(8,128)(2,1)S(1)}, u32[]{:S(2)}, u32[]{:S(2)}) collective-permute-start(bf16[64,1024]{1,0:T(8,128)(2,1)S(1)} %cross_coefficients.12), channel_id=1, source_target_pairs={{0,1},{1,0},{2,3},{3,2},{4,5},{5,4},{6,7},{7,6},{8,9},{9,8},{10,11... | collective-permute-start | bytes 393224 | tf_op jit(solution)/shard_map/ppermute | solution.py:308
  39.4 8.6 %collective-permute-start.13 = (bf16[64,1024]{1,0:T(8,128)(2,1)S(1)}, bf16[64,1024]{1,0:T(8,128)(2,1)S(1)}, u32[]{:S(2)}, u32[]{:S(2)}) collective-permute-start(bf16[64,1024]{1,0:T(8,128)(2,1)S(1)} %cross_coefficients.11), channel_id=1, source_target_pairs={{0,1},{1,0},{2,3},{3,2},{4,5},{5,4},{6,7},{7,6},{8,9},{9,8},{10,11... | collective-permute-start | bytes 393224 | tf_op jit(solution)/shard_map/ppermute | solution.py:308
  41.6 8.9 %copy-start.2 = (bf16[192,128]{1,0:T(8,128)(2,1)S(1)}, bf16[192,128]{1,0:T(8,128)(2,1)}, u32[]{:S(2)}) copy-start(bf16[192,128]{1,0:T(8,128)(2,1)} %constant.21.clone.refs_4_) | copy-start | bytes 147460
  41.6 8.9 %collective-permute-start.12 = (bf16[64,1024]{1,0:T(8,128)(2,1)S(1)}, bf16[64,1024]{1,0:T(8,128)(2,1)S(1)}, u32[]{:S(2)}, u32[]{:S(2)}) collective-permute-start(bf16[64,1024]{1,0:T(8,128)(2,1)S(1)} %cross_coefficients.10), channel_id=1, source_target_pairs={{0,1},{1,0},{2,3},{3,2},{4,5},{5,4},{6,7},{7,6},{8,9},{9,8},{10,11... | collective-permute-start | bytes 393224 | tf_op jit(solution)/shard_map/ppermute | solution.py:308
where the time goes:
time: 52.4 us; the launch traced here: 52.2 us
  waiting for transfers between devices  18.9 us (36%)
  starting transfers between devices  16.7 us (32%)
  Pallas kernels  16 us (31%)
    ppermute x12, waiting for transfers between devices, across(): return lax.ppermute(block, 'chan', [(i, i ^ mask) for i in range(size)])  13.6 us
    ppermute x12, starting transfers between devices, across(): return lax.ppermute(block, 'chan', [(i, i ^ mask) for i in range(size)])  12.4 us
    pallas_call x7, Pallas kernels, coefficients(): pl.pallas_call(functools.partial(cross_kernel, places, first, begun), in_...  8.93 us
    ppermute x4, waiting for transfers between devices, per_device(): lax.ppermute(part, ('tm', 'freq'), [(i, i ^ d) for i in range(shards)])  5.31 us
    ppermute x4, starting transfers between devices, per_device(): lax.ppermute(part, ('tm', 'freq'), [(i, i ^ d) for i in range(shards)])  4.31 us
    pallas_call x2, Pallas kernels, pick(): pl.pallas_call(functools.partial(pick_kernel, shards, side), in_specs=[pl...  3.8 us
    pallas_call x1, Pallas kernels, to_lags(): pl.pallas_call(lags_kernel, in_specs=[pl.BlockSpec(memory_space=pltpu.VME...  1.71 us
    pallas_call x1, Pallas kernels, whiten(): pl.pallas_call(whiten_kernel, grid_spec=pltpu.PrefetchScalarGridSpec(num_...  1.52 us
  transfers between devices with their start and end apart: 16, of which 8 were waited for; matrix products, arithmetic and copies ran while one was open for 0% of the time, Pallas kernels for 23%

commit v1 on v0

v1 whole, which is shorter than its diff:
```python
import functools
import math

import jax
import jax.numpy as jnp
import numpy as np
from jax import lax
from jax.experimental import pallas as pl
from jax.experimental.pallas import tpu as pltpu
from jax.sharding import PartitionSpec as P

WINDOW_LEN = 4096
FIRST_BIN = 64
LAGS = 128
RANK = 56
LOTS = 2
WATER = 0.5
VMEM_LIMIT = 48 * 1024 * 1024

CORE_MASK = 1
HOP_MASKS = (4, 2, 6)
CHUNKS = 8


def chunk_id(index):
    core = index & 1
    second = (index >> 1) & 1
    third = ((index >> 2) ^ (index >> 3)) & 1
    return core * 4 + second * 2 + third


def lag_basis(bins):
    k = FIRST_BIN + np.arange(bins)
    shifts = np.arange(LAGS) - LAGS // 2
    angle = 2.0 * np.pi * np.mod(k[:, None] * shifts[None, :], WINDOW_LEN) / WINDOW_LEN
    table = np.stack([np.cos(angle), -np.sin(angle)])
    _, _, rows = np.linalg.svd(table.reshape(2 * bins, LAGS), full_matrices=False)
    basis = rows[:RANK]
    return np.einsum("ofl,rl->ofr", table, basis), basis


def pick_kernel(shards, side, owners_in, rows_in, spectra, *refs):
    outs, (owners, rows, staged, sems) = refs[:LOTS], refs[LOTS:]
    steps, count = rows.shape
    keep = count // shards
    few = steps // LOTS
    total = few * count
    me = lax.axis_index("chan")
    mine = lax.axis_index("tm") * lax.axis_size("freq") + lax.axis_index("freq")
    place = chunk_id(me)
    scalars = [
        pltpu.make_async_copy(owners_in, owners, sems.at[4]),
        pltpu.make_async_copy(rows_in, rows, sems.at[5]),
    ]
    for copy in scalars:
        copy.start()
    fc = staged.shape[2]
    copies = []
    for j in range(4):
        at = pl.multiple_of((place ^ (side + j)) * fc, fc)
        copy = pltpu.make_async_copy(spectra.at[:, pl.ds(at, fc)], staged.at[j], sems.at[j])
        copy.start()
        copies.append(copy)
    for copy in scalars:
        copy.wait()
    sub = lax.broadcasted_iota(jnp.int32, (8, 128), 0)
    lane = lax.broadcasted_iota(jnp.int32, (8, 128), 1)
    hot = []
    for first in range(0, LOTS * total, 8):
        want = jnp.full((8, 128), -1, jnp.int32)
        for i in range(8):
            lot, rest = divmod(first + i, total)
            d, rest = divmod(rest, few * keep)
            t, k = divmod(rest, keep)
            t += lot * few
            row = jnp.where(owners[t] == me, rows[t, (mine ^ d) * keep + k], -1)
            want = jnp.where(sub == i, row, want)
        hot.append(jnp.where(want == lane, 1.0, 0.0))
    hot = jnp.concatenate(hot, axis=0).astype(jnp.bfloat16)
    for j in range(4):
        copies[j].wait()
        for k in range(2):
            block = staged[j, k].reshape(-1, staged.shape[4])
            got = lax.dot_general(
                hot, block, (((1,), (1,)), ((), ())), preferred_element_type=jnp.float32
            ).astype(jnp.bfloat16)
            for lot in range(LOTS):
                for g in range(outs[lot].shape[1]):
                    outs[lot][j, g, k] = got[lot * total : (lot + 1) * total, g * 128 : (g + 1) * 128]


def pick(owners, rows, spectra, shards, side):
    bins, win, chans = spectra.shape[1:]
    total = rows.size // LOTS
    gc = bins * win // 128 // CHUNKS
    return pl.pallas_call(
        functools.partial(pick_kernel, shards, side),
        in_specs=[pl.BlockSpec(memory_space=pl.ANY)] * 3,
        out_specs=[pl.BlockSpec(memory_space=pltpu.VMEM)] * LOTS,
        out_shape=[jax.ShapeDtypeStruct((4, gc, 2, total, 128), jnp.bfloat16)] * LOTS,
        scratch_shapes=[
            pltpu.SMEM(owners.shape, jnp.int32),
            pltpu.SMEM(rows.shape, jnp.int32),
            pltpu.VMEM((4, 2, bins // CHUNKS, win, chans), jnp.bfloat16),
            pltpu.SemaphoreType.DMA((6,)),
        ],
        compiler_params=pltpu.CompilerParams(vmem_limit_bytes=VMEM_LIMIT),
        cost_estimate=pl.CostEstimate(
            flops=2 * bins * win * chans * total, bytes_accessed=2 << 20, transcendentals=0
        ),
        name="pick_sources",
    )(owners, rows, spectra)


def whiten_pair(real, imag):
    real = real.astype(jnp.float32)
    imag = imag.astype(jnp.float32)
    size = jnp.sqrt(real * real + imag * imag) + WATER
    return (real / size).astype(jnp.bfloat16), (imag / size).astype(jnp.bfloat16)


def whiten_sum_kernel(left, right, out):
    for g in range(out.shape[0]):
        parts = [left[g, k].astype(jnp.float32) + right[g, k].astype(jnp.float32) for k in range(2)]
        out[g, 0], out[g, 1] = whiten_pair(*parts)


def whiten_sum(left, right):
    return pl.pallas_call(
        whiten_sum_kernel,
        in_specs=[pl.BlockSpec(memory_space=pltpu.VMEM)] * 2,
        out_specs=pl.BlockSpec(memory_space=pltpu.VMEM),
        out_shape=jax.ShapeDtypeStruct(left.shape, left.dtype),
        compiler_params=pltpu.CompilerParams(vmem_limit_bytes=VMEM_LIMIT),
        cost_estimate=pl.CostEstimate(flops=1 << 10, bytes_accessed=1 << 10, transcendentals=0),
        name="whiten_sources",
    )(left, right)


def whiten_kernel(meta, spectra, out):
    gc = out.shape[1]
    gf = spectra.shape[1] // gc
    for g in range(gc):
        real = spectra[0, g * gf : (g + 1) * gf].reshape(128, 128)
        imag = spectra[1, g * gf : (g + 1) * gf].reshape(128, 128)
        out[0, g, 0], out[0, g, 1] = whiten_pair(real, imag)


def whiten(meta, spectra):
    bins, win, chans = spectra.shape[1:]
    gc = bins * win // 128 // CHUNKS
    return pl.pallas_call(
        whiten_kernel,
        grid_spec=pltpu.PrefetchScalarGridSpec(
            num_scalar_prefetch=1,
            grid=(CHUNKS,),
            in_specs=[pl.BlockSpec((2, bins // CHUNKS, win, chans), lambda p, meta: (0, meta[0] ^ p, 0, 0))],
            out_specs=pl.BlockSpec((1, gc, 2, 128, 128), lambda p, meta: (p, 0, 0, 0, 0)),
        ),
        out_shape=jax.ShapeDtypeStruct((CHUNKS, gc, 2, 128, 128), jnp.bfloat16),
        compiler_params=pltpu.CompilerParams(vmem_limit_bytes=VMEM_LIMIT),
        cost_estimate=pl.CostEstimate(flops=1 << 24, bytes_accessed=4 << 20, transcendentals=1 << 20),
        name="whiten_block",
    )(meta, spectra)


def cross_kernel(places, first, begun, behind, meta, *refs):
    groups, refs = refs[: len(places)], refs[len(places) + behind :]
    if begun is not None:
        start, *refs = refs
    white, table, out, cross = refs
    count = out.shape[1] // 128
    gc = white.shape[1]
    gf = table.shape[2] // (2 * gc)
    win = 128 // gf
    row = lax.broadcasted_iota(jnp.int32, (gf, 128), 0)
    lane = lax.broadcasted_iota(jnp.int32, (gf, 128), 1)
    mask = jnp.where(lane // win == row, 1.0, 0.0).astype(jnp.bfloat16)
    low = first // 16 * 16
    high = min(-(-(first + count) // 16) * 16, groups[0].shape[3])
    step = math.gcd(8, count)
    order = [(p, group, n) for place, group in zip(places, groups) for n, p in enumerate(place)]
    for i, (p, group, n) in enumerate(order):
        for g in range(gc):
            wr = white[p, g, 0]
            wi = white[p, g, 1]
            right = jnp.concatenate(
                [jnp.concatenate([wr, wi], axis=1), jnp.concatenate([wi, -wr], axis=1)], axis=0
            )
            real = group[n, g, 0, low:high].astype(jnp.float32)[first - low : first - low + count]
            imag = group[n, g, 1, low:high].astype(jnp.float32)[first - low : first - low + count]
            for s0 in range(0, count, step):
                rows = []
                for s in range(s0, s0 + step):
                    lr = jnp.broadcast_to(real[s : s + 1], (gf, 128)).astype(jnp.bfloat16) * mask
                    li = jnp.broadcast_to(imag[s : s + 1], (gf, 128)).astype(jnp.bfloat16) * mask
                    rows.append(jnp.concatenate([lr, li], axis=1))
                left = jnp.concatenate(rows, axis=0)
                both = jnp.dot(left, right, preferred_element_type=jnp.float32).astype(jnp.bfloat16)
                for o in range(2):
                    at = (i * 2 + o) * gc * gf + g * gf
                    for s in range(step):
                        cross[at : at + gf, (s0 + s) * 128 : (s0 + s + 1) * 128] = both[
                            s * gf : (s + 1) * gf, o * 128 : (o + 1) * 128
                        ]
    left = jnp.concatenate([table[meta[0] ^ p] for p, _, _ in order], axis=1)
    wide = math.gcd(4, count) * 128
    for n in range(count * 128 // wide):
        got = jnp.dot(left, cross[:, n * wide : (n + 1) * wide], preferred_element_type=jnp.float32)
        if begun is not None:
            got = got + start[:, begun * 128 + n * wide : begun * 128 + (n + 1) * wide]
        out[:, n * wide : (n + 1) * wide] = got.astype(out.dtype)


def coefficients(meta, chunks, start, white, table, first, count, dtype, cost=1 << 10, behind=()):
    gc = white.shape[1]
    places = tuple(chunks)
    begun = None if start is None else start[1]
    operands = [*chunks.values(), *behind, *([] if start is None else [start[0]]), white, table]
    whole = pl.BlockSpec(memory_space=pltpu.VMEM)
    return pl.pallas_call(
        functools.partial(cross_kernel, places, first, begun, len(behind)),
        in_specs=[pl.BlockSpec(memory_space=pltpu.SMEM)]
        + [whole] * len(places)
        + [pl.BlockSpec(memory_space=pl.ANY)] * len(behind)
        + [whole] * (len(operands) - len(places) - len(behind)),
        out_specs=whole,
        out_shape=jax.ShapeDtypeStruct((RANK, count * 128), dtype),
        scratch_shapes=[pltpu.VMEM((sum(map(len, places)) * table.shape[2], count * 128), jnp.bfloat16)],
        compiler_params=pltpu.CompilerParams(vmem_limit_bytes=VMEM_LIMIT),
        cost_estimate=pl.CostEstimate(flops=cost, bytes_accessed=1 << 10, transcendentals=0),
        name="cross_coefficients",
    )(meta, *operands)


def lags_kernel(shards, first, *refs):
    own, *others, basis, out, staged, sems = refs[-shards - 4 :]
    count = staged.shape[0]
    step = count // sems.shape[0]
    copies = []
    for s in range(count):
        at = slice(s * 128, (s + 1) * 128)
        value = own[:, at]
        for other in others:
            value = value + other[:, at].astype(jnp.float32)
        high = value.astype(jnp.bfloat16)
        low = (value - high.astype(jnp.float32)).astype(jnp.bfloat16)
        left = jnp.concatenate([high, low, high], axis=0)
        staged[s] = lax.dot_general(
            left, basis[...], (((0,), (0,)), ((), ())), preferred_element_type=jnp.float32
        )
        if (s + 1) % step == 0:
            start = s + 1 - step
            copy = pltpu.make_async_copy(
                staged.at[start : s + 1], out.at[first + start : first + s + 1], sems.at[s // step]
            )
            copy.start()
            copies.append(copy)
    for copy in copies:
        copy.wait()


def to_lags(own, others, basis, lot, done, cost):
    count = own.shape[1] // 128
    operands = [own, *others, basis]
    specs = [pl.BlockSpec(memory_space=pltpu.VMEM)] * len(operands)
    aliases = {}
    if done is not None:
        aliases = {0: 0}
        specs.insert(0, pl.BlockSpec(memory_space=pl.ANY))
        operands.insert(0, done)
    return pl.pallas_call(
        functools.partial(lags_kernel, 1 + len(others), lot * count),
        in_specs=specs,
        out_specs=pl.BlockSpec(memory_space=pl.ANY),
        out_shape=jax.ShapeDtypeStruct((LOTS * count, 128, LAGS), jnp.float32),
        input_output_aliases=aliases,
        scratch_shapes=[
            pltpu.VMEM((count, 128, LAGS), jnp.float32),
            pltpu.SemaphoreType.DMA((count // math.gcd(4, count),)),
        ],
        compiler_params=pltpu.CompilerParams(vmem_limit_bytes=VMEM_LIMIT),
        cost_estimate=pl.CostEstimate(flops=cost, bytes_accessed=1 << 10, transcendentals=0),
        name="lags",
    )(*operands)


def per_device(size, spectra, owners, source_rows):
    bins = spectra.shape[1]
    steps, count = source_rows.shape
    shards = lax.axis_size("tm") * lax.axis_size("freq")
    keep = count // shards
    me = lax.axis_index("chan").astype(jnp.int32)
    meta = chunk_id(me).reshape(1)

    def across(block, mask):
        return lax.ppermute(block, "chan", [(i, i ^ mask) for i in range(size)])

    all_bins = bins * lax.axis_size("freq")
    table, basis = lag_basis(all_bins)
    windows = spectra.shape[2] * lax.axis_size("tm")
    table = jnp.asarray((table / windows).astype(jnp.bfloat16))
    if all_bins != bins:
        table = lax.dynamic_slice_in_dim(table, lax.axis_index("freq") * bins, bins, 1)
    table = jnp.transpose(table.reshape(2, CHUNKS, bins // CHUNKS, RANK), (1, 3, 0, 2)).reshape(CHUNKS, RANK, -1)
    high = basis.astype(jnp.bfloat16)
    low = (basis - high.astype(np.float64)).astype(jnp.bfloat16)
    basis = jnp.asarray(np.concatenate([high, high, low], axis=0))

    inputs = [pltpu.with_memory_space_constraint(x, pltpu.HBM) for x in (owners, source_rows, spectra)]
    away = pick(*inputs, shards, 4)
    home = pick(*inputs, shards, 0)
    lots = range(LOTS)
    halves = [home[i] + across(away[i], CORE_MASK) for i in lots]
    halves[0], spectra = lax.optimization_barrier((halves[0], spectra))
    arrived = [[across(half[j + 1], mask) for j, mask in enumerate(HOP_MASKS)] for half in halves]
    white = whiten(meta, spectra)
    arrived[0], white = lax.optimization_barrier((arrived[0], white))
    totals = []
    for half, parts in zip(halves, arrived):
        total = half[0]
        for part in parts:
            total = total + part
        totals.append(total)
    masks = [16 << i for i in range(10) if 16 << i < size] + [12] * (size >= 16)
    for mask in masks[:-1]:
        totals = [total + across(total, mask) for total in totals]
    others = [across(total, masks[-1]) if masks else jnp.zeros_like(total) for total in totals]
    own = [whiten_sum(total, other) for total, other in zip(totals, others)]
    chunks = [jnp.stack([chunk] + [across(chunk, mask) for mask in HOP_MASKS]) for chunk in own]

    every = steps * keep // LOTS
    near, far = (0, 1, 2, 3), (4, 5, 6, 7)
    out = None
    sent, kept = [], []
    got = []
    for i in lots:
        beside = across(chunks[i], CORE_MASK)
        begun = coefficients(
            meta, {near: chunks[i]}, None, white, table, every, every * (shards - 1), jnp.float32, behind=got
        )
        got = [
            coefficients(meta, {far: beside}, (begun, (d - 1) * every), white, table, d * every, every, jnp.bfloat16)
            for d in range(1, shards)
        ]
        sent.append(
            [
                lax.ppermute(part, ("tm", "freq"), [(m, m ^ (d + 1)) for m in range(shards)])
                for d, part in enumerate(got)
            ]
        )
        kept.append(
            coefficients(meta, {near: chunks[i], far: beside}, None, white, table, 0, every, jnp.float32)
        )
    for i in lots:
        out = to_lags(kept[i], sent[i], basis, i, out, 1 << (10 if i + 1 == LOTS else 30))
    return out.reshape(steps, keep, 128, LAGS)


def solution(mesh):
    placed = (P(None, "freq", "tm", ("parts", "chan")), P("parts"), P("parts", None))
    return jax.shard_map(
        functools.partial(per_device, mesh.shape["chan"]),
        mesh=mesh,
        in_specs=placed,
        out_specs=P(None, ("tm", "freq"), ("parts", "chan"), None),
        check_vma=False,
    )
```

time: 52.4 us -> 49 us (0.935)
  waiting for transfers between devices: 18.9 us -> 6.29 us
  starting transfers between devices: 16.7 us -> 25.5 us
    ppermute x12 -> x18, starting transfers between devices: 12.4 us -> 23.4 us  [across(): return lax.ppermute(block, 'chan', [(i, i ^ mask) for i in range(size)])]
    ppermute x12 -> x18, waiting for transfers between devices: 13.6 us -> 3.09 us  [across(): return lax.ppermute(block, 'chan', [(i, i ^ mask) for i in range(size)])]
    ppermute x4 -> x2, starting transfers between devices: 4.31 us -> 2.16 us  [per_device(): lax.ppermute(part, ('tm', 'freq'), [(m, m ^ d + 1) for m in range(shards)])]
    ppermute x4 -> x2, waiting for transfers between devices: 5.31 us -> 3.2 us  [per_device(): lax.ppermute(part, ('tm', 'freq'), [(m, m ^ d + 1) for m in range(shards)])]
    pallas_call x8 -> x10, Pallas kernels: 10.6 us -> 11.2 us  [the longest x6 8.47 us: coefficients(): pl.pallas_call(functools.partial(cross_kernel, places, first, begun, len(...]
  transfers between devices with their start and end apart: 16 -> 20, of which waited for: 8 -> 6; matrix products, arithmetic and copies ran while one was open for 0% -> 1% of each run, Pallas kernels for 23% -> 27%
where the time goes in v1:
time: 49 us; the launch traced here: 48.8 us
  starting transfers between devices  25.5 us (52%)
  Pallas kernels  16.5 us (34%)
  waiting for transfers between devices  6.29 us (13%)
    ppermute x18, starting transfers between devices, across(): return lax.ppermute(block, 'chan', [(i, i ^ mask) for i in range(size)])  23.4 us
    pallas_call x6, Pallas kernels, coefficients(): pl.pallas_call(functools.partial(cross_kernel, places, first, begun, len(...  8.47 us
    pallas_call x2, Pallas kernels, pick(): pl.pallas_call(functools.partial(pick_kernel, shards, side), in_specs=[pl...  3.84 us
    ppermute x2, waiting for transfers between devices, per_device(): lax.ppermute(part, ('tm', 'freq'), [(m, m ^ d + 1) for m in range(shards)])  3.2 us
    ppermute x18, waiting for transfers between devices, across(): return lax.ppermute(block, 'chan', [(i, i ^ mask) for i in range(size)])  3.09 us
    pallas_call x2, Pallas kernels, to_lags(): pl.pallas_call(functools.partial(lags_kernel, 1 + len(others), lot * coun...  2.57 us
    ppermute x2, starting transfers between devices, per_device(): lax.ppermute(part, ('tm', 'freq'), [(m, m ^ d + 1) for m in range(shards)])  2.16 us
    pallas_call x1, Pallas kernels, whiten(): pl.pallas_call(whiten_kernel, grid_spec=pltpu.PrefetchScalarGridSpec(num_...  1.52 us
  transfers between devices with their start and end apart: 20, of which 6 were waited for; matrix products, arithmetic and copies ran while one was open for 1% of the time, Pallas kernels for 27%

profile of v1, /device:TPU:0, one launch (start us, length us, event | category | flops | bytes accessed | tf_op | source)
XLA Modules:
  0.0 48.8 jit_solution(6298787370501916627)
XLA Ops:
  0.0 1.8 %pick_sources.3 = (bf16[4,4,2,32,128]{4,3,2,1,0:T(8,128)(2,1)S(1)}, bf16[4,4,2,32,128]{4,3,2,1,0:T(8,128)(2,1)S(1)}) custom-call(s32[4]{0:T(128)} %owners_in.3, s32[4,16]{1,0:T(4,128)} %rows_in.3, bf16[2,512,8,128]{3,2,1,0:T(8,128)(2,1)} %spectra.4), custom_call_target="tpu_custom_call" | custom-call | flops 33554432 | bytes 2097152 | tf_op jit(solution)/shard_map/pick_sources/pallas_call | solution.py:96
  1.9 0.5 %collective-permute-start = (bf16[4,4,2,32,128]{4,3,2,1,0:T(8,128)(2,1)S(1)}, bf16[4,4,2,32,128]{4,3,2,1,0:T(8,128)(2,1)S(1)}, u32[]{:S(2)}, u32[]{:S(2)}) collective-permute-start(bf16[4,4,2,32,128]{4,3,2,1,0:T(8,128)(2,1)S(1)} %get-tuple-element.16), channel_id=1, source_target_pairs={{0,2},{2,0},{4,6},{6,4},{8,10},{10,8},{12,14},{14,12},{16,18},{18,... | collective-permute-start | bytes 786440 | tf_op jit(solution)/shard_map/ppermute | solution.py:297
  2.4 0.1 collective-permute-start.10
  2.4 2.0 %pick_sources.2 = (bf16[4,4,2,32,128]{4,3,2,1,0:T(8,128)(2,1)S(1)}, bf16[4,4,2,32,128]{4,3,2,1,0:T(8,128)(2,1)S(1)}) custom-call(s32[4]{0:T(128)} %owners_in.3, s32[4,16]{1,0:T(4,128)} %rows_in.3, bf16[2,512,8,128]{3,2,1,0:T(8,128)(2,1)} %spectra.4), custom_call_target="tpu_custom_call" | custom-call | flops 33554432 | bytes 2097152 | tf_op jit(solution)/shard_map/pick_sources/pallas_call | solution.py:96
  4.6 4.0 %collective-permute-start.3 = (bf16[4,2,32,128]{3,2,1,0:T(8,128)(2,1)S(1)}, bf16[4,2,32,128]{3,2,1,0:T(8,128)(2,1)S(1)}, u32[]{:S(2)}, u32[]{:S(2)}) collective-permute-start(bf16[4,2,32,128]{3,2,1,0:T(8,128)(2,1)S(1)} %get-tuple-element.28), channel_id=1, source_target_pairs={{0,12},{2,14},{4,8},{6,10},{8,4},{10,6},{12,0},{14,2},{16,28},{18,... | collective-permute-start | bytes 196616 | tf_op jit(solution)/shard_map/ppermute | solution.py:297
  8.6 0.5 %collective-permute-start.2 = (bf16[4,2,32,128]{3,2,1,0:T(8,128)(2,1)S(1)}, bf16[4,2,32,128]{3,2,1,0:T(8,128)(2,1)S(1)}, u32[]{:S(2)}, u32[]{:S(2)}) collective-permute-start(bf16[4,2,32,128]{3,2,1,0:T(8,128)(2,1)S(1)} %get-tuple-element.29), channel_id=1, source_target_pairs={{0,4},{2,6},{4,0},{6,2},{8,12},{10,14},{12,8},{14,10},{16,20},{18,... | collective-permute-start | bytes 196616 | tf_op jit(solution)/shard_map/ppermute | solution.py:297
  9.1 0.1 collective-permute-start.1
  9.4 1.9 %collective-permute-start.11 = (bf16[4,2,32,128]{3,2,1,0:T(8,128)(2,1)S(1)}, bf16[4,2,32,128]{3,2,1,0:T(8,128)(2,1)S(1)}, u32[]{:S(2)}, u32[]{:S(2)}) collective-permute-start(bf16[4,2,32,128]{3,2,1,0:T(8,128)(2,1)S(1)} %get-tuple-element.25), channel_id=1, source_target_pairs={{0,8},{2,10},{4,12},{6,14},{8,0},{10,2},{12,4},{14,6},{16,24},{18,... | collective-permute-start | bytes 196616 | tf_op jit(solution)/shard_map/ppermute | solution.py:297
  11.3 1.4 %collective-permute-start.13 = (bf16[4,2,32,128]{3,2,1,0:T(8,128)(2,1)S(1)}, bf16[4,2,32,128]{3,2,1,0:T(8,128)(2,1)S(1)}, u32[]{:S(2)}, u32[]{:S(2)}) collective-permute-start(bf16[4,2,32,128]{3,2,1,0:T(8,128)(2,1)S(1)} %get-tuple-element.26), channel_id=1, source_target_pairs={{0,12},{2,14},{4,8},{6,10},{8,4},{10,6},{12,0},{14,2},{16,28},{18,... | collective-permute-start | bytes 196616 | tf_op jit(solution)/shard_map/ppermute | solution.py:297
  12.7 1.5 %whiten_block.1.refs_2_.refs_1_ = bf16[8,4,2,128,128]{4,3,2,1,0:T(8,128)(2,1)S(1)} custom-call(s32[1]{0:T(128)} %bitcast.meta, bf16[2,512,8,128]{3,2,1,0:T(8,128)(2,1)S(1)} %copy-done), custom_call_target="tpu_custom_call" | custom-call | flops 16777216 | bytes 4194304 | tf_op jit(solution)/shard_map/whiten_block/pallas_call | solution.py:152
  14.3 0.3 collective-permute-start.12
  14.6 4.0 %collective-permute-start.4 = (bf16[4,2,32,128]{3,2,1,0:T(8,128)(2,1)S(1)}, bf16[4,2,32,128]{3,2,1,0:T(8,128)(2,1)S(1)}, u32[]{:S(2)}, u32[]{:S(2)}) collective-permute-start(bf16[4,2,32,128]{3,2,1,0:T(8,128)(2,1)S(1)} %fusion.4.left), channel_id=1, source_target_pairs={{0,24},{2,26},{4,28},{6,30},{8,16},{10,18},{12,20},{14,22},{16,8},... | collective-permute-start | bytes 196616 | tf_op jit(solution)/shard_map/ppermute | solution.py:297
  18.6 3.7 %collective-permute-start.14 = (bf16[4,2,32,128]{3,2,1,0:T(8,128)(2,1)S(1)}, bf16[4,2,32,128]{3,2,1,0:T(8,128)(2,1)S(1)}, u32[]{:S(2)}, u32[]{:S(2)}) collective-permute-start(bf16[4,2,32,128]{3,2,1,0:T(8,128)(2,1)S(1)} %fusion.2.left), channel_id=1, source_target_pairs={{0,24},{2,26},{4,28},{6,30},{8,16},{10,18},{12,20},{14,22},{16,8},... | collective-permute-start | bytes 196616 | tf_op jit(solution)/shard_map/ppermute | solution.py:297
  22.3 1.6 %collective-permute-start.7 = (bf16[4,2,32,128]{3,2,1,0:T(8,128)(2,1)S(1)}, bf16[4,2,32,128]{3,2,1,0:T(8,128)(2,1)S(1)}, u32[]{:S(2)}, u32[]{:S(2)}) collective-permute-start(bf16[4,2,32,128]{3,2,1,0:T(8,128)(2,1)S(1)} %whiten_sources.2), channel_id=1, source_target_pairs={{0,12},{2,14},{4,8},{6,10},{8,4},{10,6},{12,0},{14,2},{16,28},{18,... | collective-permute-start | bytes 196616 | tf_op jit(solution)/shard_map/ppermute | solution.py:297
  24.0 1.9 %collective-permute-start.5 = (bf16[4,2,32,128]{3,2,1,0:T(8,128)(2,1)S(1)}, bf16[4,2,32,128]{3,2,1,0:T(8,128)(2,1)S(1)}, u32[]{:S(2)}, u32[]{:S(2)}) collective-permute-start(bf16[4,2,32,128]{3,2,1,0:T(8,128)(2,1)S(1)} %whiten_sources.2), channel_id=1, source_target_pairs={{0,8},{2,10},{4,12},{6,14},{8,0},{10,2},{12,4},{14,6},{16,24},{18,... | collective-permute-start | bytes 196616 | tf_op jit(solution)/shard_map/ppermute | solution.py:297
  26.0 1.6 %collective-permute-start.17 = (bf16[4,2,32,128]{3,2,1,0:T(8,128)(2,1)S(1)}, bf16[4,2,32,128]{3,2,1,0:T(8,128)(2,1)S(1)}, u32[]{:S(2)}, u32[]{:S(2)}) collective-permute-start(bf16[4,2,32,128]{3,2,1,0:T(8,128)(2,1)S(1)} %whiten_sources.3), channel_id=1, source_target_pairs={{0,12},{2,14},{4,8},{6,10},{8,4},{10,6},{12,0},{14,2},{16,28},{18,... | collective-permute-start | bytes 196616 | tf_op jit(solution)/shard_map/ppermute | solution.py:297
  27.6 0.4 collective-permute-done.7
  28.0 1.5 %collective-permute-start.15 = (bf16[4,2,32,128]{3,2,1,0:T(8,128)(2,1)S(1)}, bf16[4,2,32,128]{3,2,1,0:T(8,128)(2,1)S(1)}, u32[]{:S(2)}, u32[]{:S(2)}) collective-permute-start(bf16[4,2,32,128]{3,2,1,0:T(8,128)(2,1)S(1)} %whiten_sources.3), channel_id=1, source_target_pairs={{0,8},{2,10},{4,12},{6,14},{8,0},{10,2},{12,4},{14,6},{16,24},{18,... | collective-permute-start | bytes 196616 | tf_op jit(solution)/shard_map/ppermute | solution.py:297
  29.6 1.5 %collective-permute-done.17 = bf16[4,2,32,128]{3,2,1,0:T(8,128)(2,1)S(1)} collective-permute-done((bf16[4,2,32,128]{3,2,1,0:T(8,128)(2,1)S(1)}, bf16[4,2,32,128]{3,2,1,0:T(8,128)(2,1)S(1)}, u32[]{:S(2)}, u32[]{:S(2)}) %collective-permute-start.17) | collective-permute-done | bytes 65568 | tf_op jit(solution)/shard_map/ppermute | solution.py:297
  31.2 0.7 %collective-permute-done.16 = bf16[4,2,32,128]{3,2,1,0:T(8,128)(2,1)S(1)} collective-permute-done((bf16[4,2,32,128]{3,2,1,0:T(8,128)(2,1)S(1)}, bf16[4,2,32,128]{3,2,1,0:T(8,128)(2,1)S(1)}, u32[]{:S(2)}, u32[]{:S(2)}) %collective-permute-start.16) | collective-permute-done | bytes 65568 | tf_op jit(solution)/shard_map/ppermute | solution.py:297
  31.9 0.3 collective-permute-done.15
  32.4 1.1 %cross_coefficients.7.refs_1_ = f32[56,2048]{1,0:T(8,128)S(1)} custom-call(s32[1]{0:T(128)} %bitcast.meta, bf16[4,4,2,32,128]{4,3,2,1,0:T(8,128)(2,1)S(1)} %pad_maximum_fusion.refs_0_, bf16[8,4,2,128,128]{4,3,2,1,0:T(8,128)(2,1)S(1)} %whiten_block.1.refs_2_.refs_1_, bf16[8,56,128]{2,1,0:T(8,128)(2,1)S(1)} %copy-done.1), custom_call_target="tpu_custom_call" | custom-call | flops 1024 | bytes 1024 | tf_op jit(solution)/shard_map/cross_coefficients/pallas_call | solution.py:221
  33.5 1.1 %cross_coefficients.8.refs_1_ = bf16[56,2048]{1,0:T(8,128)(2,1)S(1)} custom-call(s32[1]{0:T(128)} %bitcast.meta, bf16[4,4,2,32,128]{4,3,2,1,0:T(8,128)(2,1)S(1)} %collective-permute-done.8.refs_1_.refs_0_, f32[56,2048]{1,0:T(8,128)S(1)} %cross_coefficients.7.refs_1_, bf16[8,4,2,128,128]{4,3,2,1,0:T(8,128)(2,1)S(1)} %whiten_block.1.refs_2_.refs_1_, ...), custom_call_target="tpu_custom_call" | custom-call | flops 1024 | bytes 1024 | tf_op jit(solution)/shard_map/cross_coefficients/pallas_call | solution.py:221
  34.6 1.5 %collective-permute-start.9 = (bf16[56,2048]{1,0:T(8,128)(2,1)S(1)}, bf16[56,2048]{1,0:T(8,128)(2,1)S(1)}, u32[]{:S(2)}, u32[]{:S(2)}) collective-permute-start(bf16[56,2048]{1,0:T(8,128)(2,1)S(1)} %cross_coefficients.8.refs_1_), channel_id=1, source_target_pairs={{0,1},{1,0},{2,3},{3,2},{4,5},{5,4},{6,7},{7,6},{8,9},{9,8},{10,11... | collective-permute-start | bytes 688136 | tf_op jit(solution)/shard_map/ppermute | solution.py:348
  36.1 1.1 %cross_coefficients.10.refs_1_ = f32[56,2048]{1,0:T(8,128)S(1)} custom-call(s32[1]{0:T(128)} %bitcast.meta, bf16[4,4,2,32,128]{4,3,2,1,0:T(8,128)(2,1)S(1)} %pad_maximum_fusion.1.refs_0_, bf16[56,2048]{1,0:T(8,128)(2,1)S(1)} %cross_coefficients.8.refs_1_, bf16[8,4,2,128,128]{4,3,2,1,0:T(8,128)(2,1)S(1)} %whiten_block.1.refs_2_.refs_1_, ...), custom_call_target="tpu_custom_call" | custom-call | flops 1024 | bytes 1024 | tf_op jit(solution)/shard_map/cross_coefficients/pallas_call | solution.py:221
  37.3 1.1 %cross_coefficients.11 = bf16[56,2048]{1,0:T(8,128)(2,1)S(1)} custom-call(s32[1]{0:T(128)} %bitcast.meta, bf16[4,4,2,32,128]{4,3,2,1,0:T(8,128)(2,1)S(1)} %collective-permute-done.18.refs_1_.refs_0_, f32[56,2048]{1,0:T(8,128)S(1)} %cross_coefficients.10.refs_1_, bf16[8,4,2,128,128]{4,3,2,1,0:T(8,128)(2,1)S(1)} %whiten_block.1.refs_2_.refs_1_, ...), custom_call_target="tpu_custom_call" | custom-call | flops 1024 | bytes 1024 | tf_op jit(solution)/shard_map/cross_coefficients/pallas_call | solution.py:221
  38.4 0.6 %collective-permute-start.19 = (bf16[56,2048]{1,0:T(8,128)(2,1)S(1)}, bf16[56,2048]{1,0:T(8,128)(2,1)S(1)}, u32[]{:S(2)}, u32[]{:S(2)}) collective-permute-start(bf16[56,2048]{1,0:T(8,128)(2,1)S(1)} %cross_coefficients.11), channel_id=1, source_target_pairs={{0,1},{1,0},{2,3},{3,2},{4,5},{5,4},{6,7},{7,6},{8,9},{9,8},{10,11... | collective-permute-start | bytes 688136 | tf_op jit(solution)/shard_map/ppermute | solution.py:348
  39.0 2.0 %cross_coefficients.6.refs_0_ = f32[56,2048]{1,0:T(8,128)S(1)} custom-call(s32[1]{0:T(128)} %bitcast.meta, bf16[4,4,2,32,128]{4,3,2,1,0:T(8,128)(2,1)S(1)} %pad_maximum_fusion.refs_0_, bf16[4,4,2,32,128]{4,3,2,1,0:T(8,128)(2,1)S(1)} %collective-permute-done.8.refs_1_.refs_0_, bf16[8,4,2,128,128]{4,3,2,1,0:T(8,128)(2,1)S(1)} %whiten_block.1.refs_2_.refs_1_, ...), custom_call_target="tpu_custom_call" | custom-call | flops 1024 | bytes 1024 | tf_op jit(solution)/shard_map/cross_coefficients/pallas_call | solution.py:221
  41.0 2.0 %cross_coefficients.9.refs_1_ = f32[56,2048]{1,0:T(8,128)S(1)} custom-call(s32[1]{0:T(128)} %bitcast.meta, bf16[4,4,2,32,128]{4,3,2,1,0:T(8,128)(2,1)S(1)} %pad_maximum_fusion.1.refs_0_, bf16[4,4,2,32,128]{4,3,2,1,0:T(8,128)(2,1)S(1)} %collective-permute-done.18.refs_1_.refs_0_, bf16[8,4,2,128,128]{4,3,2,1,0:T(8,128)(2,1)S(1)} %whiten_block.1.refs_2_.refs_1_, ...), custom_call_target="tpu_custom_call" | custom-call | flops 1024 | bytes 1024 | tf_op jit(solution)/shard_map/cross_coefficients/pallas_call | solution.py:221
  43.1 1.3 %lags.2.refs_0_ = f32[32,128,128]{2,1,0:T(8,128)} custom-call(f32[56,2048]{1,0:T(8,128)S(1)} %cross_coefficients.6.refs_0_, bf16[56,2048]{1,0:T(8,128)(2,1)S(1)} %collective-permute-done.9.refs_1_, bf16[168,128]{1,0:T(8,128)(2,1)S(1)} %copy-done.2), custom_call_target="tpu_custom_call" | custom-call | flops 1073741824 | bytes 1024 | tf_op jit(solution)/shard_map/lags/pallas_call | solution.py:272
  44.4 3.2 %collective-permute-done.19.refs_2_ = bf16[56,2048]{1,0:T(8,128)(2,1)S(1)} collective-permute-done((bf16[56,2048]{1,0:T(8,128)(2,1)S(1)}, bf16[56,2048]{1,0:T(8,128)(2,1)S(1)}, u32[]{:S(2)}, u32[]{:S(2)}) %collective-permute-start.19) | collective-permute-done | bytes 229408 | tf_op jit(solution)/shard_map/ppermute | solution.py:348
  47.6 1.3 %lags.3 = f32[32,128,128]{2,1,0:T(8,128)} custom-call(f32[32,128,128]{2,1,0:T(8,128)} %lags.2.refs_0_, f32[56,2048]{1,0:T(8,128)S(1)} %cross_coefficients.9.refs_1_, bf16[56,2048]{1,0:T(8,128)(2,1)S(1)} %collective-permute-done.19.refs_2_, bf16[168,128]{1,0:T(8,128)(2,1)S(1)} %copy-done.2), custom_call_target="tpu_custom_call", output_to_operand_aliasing={{}: (0, {})} | custom-call | flops 1024 | bytes 1024 | tf_op jit(solution)/shard_map/lags/pallas_call | solution.py:272
  (35 shorter events, 0.7 us)
Async XLA Ops:
  1.9 2.6 %collective-permute-start = (bf16[4,4,2,32,128]{4,3,2,1,0:T(8,128)(2,1)S(1)}, bf16[4,4,2,32,128]{4,3,2,1,0:T(8,128)(2,1)S(1)}, u32[]{:S(2)}, u32[]{:S(2)}) collective-permute-start(bf16[4,4,2,32,128]{4,3,2,1,0:T(8,128)(2,1)S(1)} %get-tuple-element.16), channel_id=1, source_target_pairs={{0,2},{2,0},{4,6},{6,4},{8,10},{10,8},{12,14},{14,12},{16,18},{18,... | collective-permute-start | bytes 786440 | tf_op jit(solution)/shard_map/ppermute | solution.py:297
  2.4 6.9 %collective-permute-start.10 = (bf16[4,4,2,32,128]{4,3,2,1,0:T(8,128)(2,1)S(1)}, bf16[4,4,2,32,128]{4,3,2,1,0:T(8,128)(2,1)S(1)}, u32[]{:S(2)}, u32[]{:S(2)}) collective-permute-start(bf16[4,4,2,32,128]{4,3,2,1,0:T(8,128)(2,1)S(1)} %get-tuple-element.24), channel_id=1, source_target_pairs={{0,2},{2,0},{4,6},{6,4},{8,10},{10,8},{12,14},{14,12},{16,18},{18,... | collective-permute-start | bytes 786440 | tf_op jit(solution)/shard_map/ppermute | solution.py:297
  2.4 10.3 %copy-start = (bf16[2,512,8,128]{3,2,1,0:T(8,128)(2,1)S(1)}, bf16[2,512,8,128]{3,2,1,0:T(8,128)(2,1)}, u32[]{:S(2)}) copy-start(bf16[2,512,8,128]{3,2,1,0:T(8,128)(2,1)} %spectra.4) | copy-start | bytes 6291460
  4.6 9.7 %collective-permute-start.3 = (bf16[4,2,32,128]{3,2,1,0:T(8,128)(2,1)S(1)}, bf16[4,2,32,128]{3,2,1,0:T(8,128)(2,1)S(1)}, u32[]{:S(2)}, u32[]{:S(2)}) collective-permute-start(bf16[4,2,32,128]{3,2,1,0:T(8,128)(2,1)S(1)} %get-tuple-element.28), channel_id=1, source_target_pairs={{0,12},{2,14},{4,8},{6,10},{8,4},{10,6},{12,0},{14,2},{16,28},{18,... | collective-permute-start | bytes 196616 | tf_op jit(solution)/shard_map/ppermute | solution.py:297
  8.6 5.9 %collective-permute-start.2 = (bf16[4,2,32,128]{3,2,1,0:T(8,128)(2,1)S(1)}, bf16[4,2,32,128]{3,2,1,0:T(8,128)(2,1)S(1)}, u32[]{:S(2)}, u32[]{:S(2)}) collective-permute-start(bf16[4,2,32,128]{3,2,1,0:T(8,128)(2,1)S(1)} %get-tuple-element.29), channel_id=1, source_target_pairs={{0,4},{2,6},{4,0},{6,2},{8,12},{10,14},{12,8},{14,10},{16,20},{18,... | collective-permute-start | bytes 196616 | tf_op jit(solution)/shard_map/ppermute | solution.py:297
  9.1 5.4 %collective-permute-start.1 = (bf16[4,2,32,128]{3,2,1,0:T(8,128)(2,1)S(1)}, bf16[4,2,32,128]{3,2,1,0:T(8,128)(2,1)S(1)}, u32[]{:S(2)}, u32[]{:S(2)}) collective-permute-start(bf16[4,2,32,128]{3,2,1,0:T(8,128)(2,1)S(1)} %get-tuple-element.30), channel_id=1, source_target_pairs={{0,8},{2,10},{4,12},{6,14},{8,0},{10,2},{12,4},{14,6},{16,24},{18,... | collective-permute-start | bytes 196616 | tf_op jit(solution)/shard_map/ppermute | solution.py:297
  9.4 9.2 %collective-permute-start.11 = (bf16[4,2,32,128]{3,2,1,0:T(8,128)(2,1)S(1)}, bf16[4,2,32,128]{3,2,1,0:T(8,128)(2,1)S(1)}, u32[]{:S(2)}, u32[]{:S(2)}) collective-permute-start(bf16[4,2,32,128]{3,2,1,0:T(8,128)(2,1)S(1)} %get-tuple-element.25), channel_id=1, source_target_pairs={{0,8},{2,10},{4,12},{6,14},{8,0},{10,2},{12,4},{14,6},{16,24},{18,... | collective-permute-start | bytes 196616 | tf_op jit(solution)/shard_map/ppermute | solution.py:297
  11.3 7.2 %collective-permute-start.13 = (bf16[4,2,32,128]{3,2,1,0:T(8,128)(2,1)S(1)}, bf16[4,2,32,128]{3,2,1,0:T(8,128)(2,1)S(1)}, u32[]{:S(2)}, u32[]{:S(2)}) collective-permute-start(bf16[4,2,32,128]{3,2,1,0:T(8,128)(2,1)S(1)} %get-tuple-element.26), channel_id=1, source_target_pairs={{0,12},{2,14},{4,8},{6,10},{8,4},{10,6},{12,0},{14,2},{16,28},{18,... | collective-permute-start | bytes 196616 | tf_op jit(solution)/shard_map/ppermute | solution.py:297
  14.2 18.1 %copy-start.1 = (bf16[8,56,128]{2,1,0:T(8,128)(2,1)S(1)}, bf16[8,56,128]{2,1,0:T(8,128)(2,1)}, u32[]{:S(2)}) copy-start(bf16[8,56,128]{2,1,0:T(8,128)(2,1)} %constant.22.refs_3_.refs_2_) | copy-start | bytes 344068
  14.3 4.3 %collective-permute-start.12 = (bf16[4,2,32,128]{3,2,1,0:T(8,128)(2,1)S(1)}, bf16[4,2,32,128]{3,2,1,0:T(8,128)(2,1)S(1)}, u32[]{:S(2)}, u32[]{:S(2)}) collective-permute-start(bf16[4,2,32,128]{3,2,1,0:T(8,128)(2,1)S(1)} %get-tuple-element.27), channel_id=1, source_target_pairs={{0,4},{2,6},{4,0},{6,2},{8,12},{10,14},{12,8},{14,10},{16,20},{18,... | collective-permute-start | bytes 196616 | tf_op jit(solution)/shard_map/ppermute | solution.py:297
  14.6 7.7 %collective-permute-start.4 = (bf16[4,2,32,128]{3,2,1,0:T(8,128)(2,1)S(1)}, bf16[4,2,32,128]{3,2,1,0:T(8,128)(2,1)S(1)}, u32[]{:S(2)}, u32[]{:S(2)}) collective-permute-start(bf16[4,2,32,128]{3,2,1,0:T(8,128)(2,1)S(1)} %fusion.4.left), channel_id=1, source_target_pairs={{0,24},{2,26},{4,28},{6,30},{8,16},{10,18},{12,20},{14,22},{16,8},... | collective-permute-start | bytes 196616 | tf_op jit(solution)/shard_map/ppermute | solution.py:297
  18.6 7.3 %collective-permute-start.14 = (bf16[4,2,32,128]{3,2,1,0:T(8,128)(2,1)S(1)}, bf16[4,2,32,128]{3,2,1,0:T(8,128)(2,1)S(1)}, u32[]{:S(2)}, u32[]{:S(2)}) collective-permute-start(bf16[4,2,32,128]{3,2,1,0:T(8,128)(2,1)S(1)} %fusion.2.left), channel_id=1, source_target_pairs={{0,24},{2,26},{4,28},{6,30},{8,16},{10,18},{12,20},{14,22},{16,8},... | collective-permute-start | bytes 196616 | tf_op jit(solution)/shard_map/ppermute | solution.py:297
  22.3 5.6 %collective-permute-start.7 = (bf16[4,2,32,128]{3,2,1,0:T(8,128)(2,1)S(1)}, bf16[4,2,32,128]{3,2,1,0:T(8,128)(2,1)S(1)}, u32[]{:S(2)}, u32[]{:S(2)}) collective-permute-start(bf16[4,2,32,128]{3,2,1,0:T(8,128)(2,1)S(1)} %whiten_sources.2), channel_id=1, source_target_pairs={{0,12},{2,14},{4,8},{6,10},{8,4},{10,6},{12,0},{14,2},{16,28},{18,... | collective-permute-start | bytes 196616 | tf_op jit(solution)/shard_map/ppermute | solution.py:297
  24.0 5.6 %collective-permute-start.6 = (bf16[4,2,32,128]{3,2,1,0:T(8,128)(2,1)S(1)}, bf16[4,2,32,128]{3,2,1,0:T(8,128)(2,1)S(1)}, u32[]{:S(2)}, u32[]{:S(2)}) collective-permute-start(bf16[4,2,32,128]{3,2,1,0:T(8,128)(2,1)S(1)} %whiten_sources.2), channel_id=1, source_target_pairs={{0,4},{2,6},{4,0},{6,2},{8,12},{10,14},{12,8},{14,10},{16,20},{18,... | collective-permute-start | bytes 196616 | tf_op jit(solution)/shard_map/ppermute | solution.py:297
  24.0 5.6 %collective-permute-start.5 = (bf16[4,2,32,128]{3,2,1,0:T(8,128)(2,1)S(1)}, bf16[4,2,32,128]{3,2,1,0:T(8,128)(2,1)S(1)}, u32[]{:S(2)}, u32[]{:S(2)}) collective-permute-start(bf16[4,2,32,128]{3,2,1,0:T(8,128)(2,1)S(1)} %whiten_sources.2), channel_id=1, source_target_pairs={{0,8},{2,10},{4,12},{6,14},{8,0},{10,2},{12,4},{14,6},{16,24},{18,... | collective-permute-start | bytes 196616 | tf_op jit(solution)/shard_map/ppermute | solution.py:297
  26.0 5.2 %collective-permute-start.17 = (bf16[4,2,32,128]{3,2,1,0:T(8,128)(2,1)S(1)}, bf16[4,2,32,128]{3,2,1,0:T(8,128)(2,1)S(1)}, u32[]{:S(2)}, u32[]{:S(2)}) collective-permute-start(bf16[4,2,32,128]{3,2,1,0:T(8,128)(2,1)S(1)} %whiten_sources.3), channel_id=1, source_target_pairs={{0,12},{2,14},{4,8},{6,10},{8,4},{10,6},{12,0},{14,2},{16,28},{18,... | collective-permute-start | bytes 196616 | tf_op jit(solution)/shard_map/ppermute | solution.py:297
  27.6 4.3 %collective-permute-start.16 = (bf16[4,2,32,128]{3,2,1,0:T(8,128)(2,1)S(1)}, bf16[4,2,32,128]{3,2,1,0:T(8,128)(2,1)S(1)}, u32[]{:S(2)}, u32[]{:S(2)}) collective-permute-start(bf16[4,2,32,128]{3,2,1,0:T(8,128)(2,1)S(1)} %whiten_sources.3), channel_id=1, source_target_pairs={{0,4},{2,6},{4,0},{6,2},{8,12},{10,14},{12,8},{14,10},{16,20},{18,... | collective-permute-start | bytes 196616 | tf_op jit(solution)/shard_map/ppermute | solution.py:297
  28.0 4.3 %collective-permute-start.15 = (bf16[4,2,32,128]{3,2,1,0:T(8,128)(2,1)S(1)}, bf16[4,2,32,128]{3,2,1,0:T(8,128)(2,1)S(1)}, u32[]{:S(2)}, u32[]{:S(2)}) collective-permute-start(bf16[4,2,32,128]{3,2,1,0:T(8,128)(2,1)S(1)} %whiten_sources.3), channel_id=1, source_target_pairs={{0,8},{2,10},{4,12},{6,14},{8,0},{10,2},{12,4},{14,6},{16,24},{18,... | collective-permute-start | bytes 196616 | tf_op jit(solution)/shard_map/ppermute | solution.py:297
  29.6 3.9 %collective-permute-start.8 = (bf16[4,4,2,32,128]{4,3,2,1,0:T(8,128)(2,1)S(1)}, bf16[4,4,2,32,128]{4,3,2,1,0:T(8,128)(2,1)S(1)}, u32[]{:S(2)}, u32[]{:S(2)}) collective-permute-start(bf16[4,4,2,32,128]{4,3,2,1,0:T(8,128)(2,1)S(1)} %pad_maximum_fusion.refs_0_), channel_id=1, source_target_pairs={{0,2},{2,0},{4,6},{6,4},{8,10},{10,8},{12,14},{14,12},{16,18},{18,... | collective-permute-start | bytes 786440 | tf_op jit(solution)/shard_map/ppermute | solution.py:297
  32.3 5.0 %collective-permute-start.18 = (bf16[4,4,2,32,128]{4,3,2,1,0:T(8,128)(2,1)S(1)}, bf16[4,4,2,32,128]{4,3,2,1,0:T(8,128)(2,1)S(1)}, u32[]{:S(2)}, u32[]{:S(2)}) collective-permute-start(bf16[4,4,2,32,128]{4,3,2,1,0:T(8,128)(2,1)S(1)} %pad_maximum_fusion.1.refs_0_), channel_id=1, source_target_pairs={{0,2},{2,0},{4,6},{6,4},{8,10},{10,8},{12,14},{14,12},{16,18},{18,... | collective-permute-start | bytes 786440 | tf_op jit(solution)/shard_map/ppermute | solution.py:297
  34.6 8.5 %collective-permute-start.9 = (bf16[56,2048]{1,0:T(8,128)(2,1)S(1)}, bf16[56,2048]{1,0:T(8,128)(2,1)S(1)}, u32[]{:S(2)}, u32[]{:S(2)}) collective-permute-start(bf16[56,2048]{1,0:T(8,128)(2,1)S(1)} %cross_coefficients.8.refs_1_), channel_id=1, source_target_pairs={{0,1},{1,0},{2,3},{3,2},{4,5},{5,4},{6,7},{7,6},{8,9},{9,8},{10,11... | collective-permute-start | bytes 688136 | tf_op jit(solution)/shard_map/ppermute | solution.py:348
  38.4 9.2 %collective-permute-start.19 = (bf16[56,2048]{1,0:T(8,128)(2,1)S(1)}, bf16[56,2048]{1,0:T(8,128)(2,1)S(1)}, u32[]{:S(2)}, u32[]{:S(2)}) collective-permute-start(bf16[56,2048]{1,0:T(8,128)(2,1)S(1)} %cross_coefficients.11), channel_id=1, source_target_pairs={{0,1},{1,0},{2,3},{3,2},{4,5},{5,4},{6,7},{7,6},{8,9},{9,8},{10,11... | collective-permute-start | bytes 688136 | tf_op jit(solution)/shard_map/ppermute | solution.py:348
  41.0 2.1 %copy-start.2 = (bf16[168,128]{1,0:T(8,128)(2,1)S(1)}, bf16[168,128]{1,0:T(8,128)(2,1)}, u32[]{:S(2)}) copy-start(bf16[168,128]{1,0:T(8,128)(2,1)} %constant.19.clone.refs_2_.refs_3_) | copy-start | bytes 129028

commit v2 on v1

--- a/solution.py
+++ b/solution.py
@@ -285,6 +285,24 @@
     )(*operands)
 
 
+def stack_kernel(count, *refs):
+    for i in range(count):
+        refs[-1][i] = refs[i][...]
+
+
+def stack(blocks, behind):
+    whole = pl.BlockSpec(memory_space=pltpu.VMEM)
+    return pl.pallas_call(
+        functools.partial(stack_kernel, len(blocks)),
+        in_specs=[whole] * len(blocks) + [pl.BlockSpec(memory_space=pl.ANY)] * len(behind),
+        out_specs=whole,
+        out_shape=jax.ShapeDtypeStruct((len(blocks), *blocks[0].shape), blocks[0].dtype),
+        compiler_params=pltpu.CompilerParams(vmem_limit_bytes=VMEM_LIMIT),
+        cost_estimate=pl.CostEstimate(flops=1 << 10, bytes_accessed=1 << 10, transcendentals=0),
+        name="stack",
+    )(*blocks, *behind)
+
+
 def per_device(size, spectra, owners, source_rows):
     bins = spectra.shape[1]
     steps, count = source_rows.shape
@@ -327,7 +345,7 @@
         totals = [total + across(total, mask) for total in totals]
     others = [across(total, masks[-1]) if masks else jnp.zeros_like(total) for total in totals]
     own = [whiten_sum(total, other) for total, other in zip(totals, others)]
-    chunks = [jnp.stack([chunk] + [across(chunk, mask) for mask in HOP_MASKS]) for chunk in own]
+    arrived = [[chunk] + [across(chunk, mask) for mask in HOP_MASKS] for chunk in own]
 
     every = steps * keep // LOTS
     near, far = (0, 1, 2, 3), (4, 5, 6, 7)
@@ -335,9 +353,10 @@
     sent, kept = [], []
     got = []
     for i in lots:
-        beside = across(chunks[i], CORE_MASK)
+        chunks = stack(arrived[i], [begun] if i else [])
+        beside = across(chunks, CORE_MASK)
         begun = coefficients(
-            meta, {near: chunks[i]}, None, white, table, every, every * (shards - 1), jnp.float32, behind=got
+            meta, {near: chunks}, None, white, table, every, every * (shards - 1), jnp.float32
         )
         got = [
             coefficients(meta, {far: beside}, (begun, (d - 1) * every), white, table, d * every, every, jnp.bfloat16)
@@ -350,10 +369,10 @@
             ]
         )
         kept.append(
-            coefficients(meta, {near: chunks[i], far: beside}, None, white, table, 0, every, jnp.float32)
+            coefficients(meta, {near: chunks, far: beside}, None, white, table, 0, every, jnp.float32)
         )
     for i in lots:
-        out = to_lags(kept[i], sent[i], basis, i, out, 1 << (10 if i + 1 == LOTS else 30))
+        out = to_lags(kept[i], sent[i], basis, i, out, 1 << (10 if i + 1 == LOTS else 28))
     return out.reshape(steps, keep, 128, LAGS)
 
 

time: 49 us -> 47.8 us (0.976)
  waiting for transfers between devices: 6.29 us -> 5.19 us
    ppermute x18, waiting for transfers between devices: 3.09 us -> 1.98 us  [across(): return lax.ppermute(block, 'chan', [(i, i ^ mask) for i in range(size)])]
  transfers between devices with their start and end apart: 20 -> 20, of which waited for: 6 -> 6; matrix products, arithmetic and copies ran while one was open for 1% -> 0% of each run, Pallas kernels for 27% -> 28%
where the time goes in v2:
time: 47.8 us; the launch traced here: 47.7 us
  starting transfers between devices  25.5 us (53%)
  Pallas kernels  16.5 us (35%)
  waiting for transfers between devices  5.19 us (11%)
    ppermute x18, starting transfers between devices, across(): return lax.ppermute(block, 'chan', [(i, i ^ mask) for i in range(size)])  23.4 us
    pallas_call x6, Pallas kernels, coefficients(): pl.pallas_call(functools.partial(cross_kernel, places, first, begun, len(...  8.45 us
    pallas_call x2, Pallas kernels, pick(): pl.pallas_call(functools.partial(pick_kernel, shards, side), in_specs=[pl...  3.84 us
    ppermute x2, waiting for transfers between devices, per_device(): lax.ppermute(part, ('tm', 'freq'), [(m, m ^ d + 1) for m in range(shards)])  3.21 us
    pallas_call x2, Pallas kernels, to_lags(): pl.pallas_call(functools.partial(lags_kernel, 1 + len(others), lot * coun...  2.57 us
    ppermute x2, starting transfers between devices, per_device(): lax.ppermute(part, ('tm', 'freq'), [(m, m ^ d + 1) for m in range(shards)])  2.16 us
    ppermute x18, waiting for transfers between devices, across(): return lax.ppermute(block, 'chan', [(i, i ^ mask) for i in range(size)])  1.98 us
    pallas_call x1, Pallas kernels, whiten(): pl.pallas_call(whiten_kernel, grid_spec=pltpu.PrefetchScalarGridSpec(num_...  1.52 us
  transfers between devices with their start and end apart: 20, of which 6 were waited for; matrix products, arithmetic and copies ran while one was open for 0% of the time, Pallas kernels for 28%

profile of v2, /device:TPU:0, one launch (start us, length us, event | category | flops | bytes accessed | tf_op | source)
XLA Modules:
  0.0 47.7 jit_solution(13724672928630480461)
XLA Ops:
  0.0 1.8 %pick_sources.3 = (bf16[4,4,2,32,128]{4,3,2,1,0:T(8,128)(2,1)S(1)}, bf16[4,4,2,32,128]{4,3,2,1,0:T(8,128)(2,1)S(1)}) custom-call(s32[4]{0:T(128)} %owners_in.3, s32[4,16]{1,0:T(4,128)} %rows_in.3, bf16[2,512,8,128]{3,2,1,0:T(8,128)(2,1)} %spectra.4), custom_call_target="tpu_custom_call" | custom-call | flops 33554432 | bytes 2097152 | tf_op jit(solution)/shard_map/pick_sources/pallas_call | solution.py:96
  1.9 0.5 %collective-permute-start = (bf16[4,4,2,32,128]{4,3,2,1,0:T(8,128)(2,1)S(1)}, bf16[4,4,2,32,128]{4,3,2,1,0:T(8,128)(2,1)S(1)}, u32[]{:S(2)}, u32[]{:S(2)}) collective-permute-start(bf16[4,4,2,32,128]{4,3,2,1,0:T(8,128)(2,1)S(1)} %get-tuple-element.16), channel_id=1, source_target_pairs={{0,2},{2,0},{4,6},{6,4},{8,10},{10,8},{12,14},{14,12},{16,18},{18,... | collective-permute-start | bytes 786440 | tf_op jit(solution)/shard_map/ppermute | solution.py:315
  2.4 0.1 collective-permute-start.10
  2.4 2.0 %pick_sources.2 = (bf16[4,4,2,32,128]{4,3,2,1,0:T(8,128)(2,1)S(1)}, bf16[4,4,2,32,128]{4,3,2,1,0:T(8,128)(2,1)S(1)}) custom-call(s32[4]{0:T(128)} %owners_in.3, s32[4,16]{1,0:T(4,128)} %rows_in.3, bf16[2,512,8,128]{3,2,1,0:T(8,128)(2,1)} %spectra.4), custom_call_target="tpu_custom_call" | custom-call | flops 33554432 | bytes 2097152 | tf_op jit(solution)/shard_map/pick_sources/pallas_call | solution.py:96
  4.6 4.0 %collective-permute-start.3 = (bf16[4,2,32,128]{3,2,1,0:T(8,128)(2,1)S(1)}, bf16[4,2,32,128]{3,2,1,0:T(8,128)(2,1)S(1)}, u32[]{:S(2)}, u32[]{:S(2)}) collective-permute-start(bf16[4,2,32,128]{3,2,1,0:T(8,128)(2,1)S(1)} %get-tuple-element.28), channel_id=1, source_target_pairs={{0,12},{2,14},{4,8},{6,10},{8,4},{10,6},{12,0},{14,2},{16,28},{18,... | collective-permute-start | bytes 196616 | tf_op jit(solution)/shard_map/ppermute | solution.py:315
  8.6 0.5 %collective-permute-start.2 = (bf16[4,2,32,128]{3,2,1,0:T(8,128)(2,1)S(1)}, bf16[4,2,32,128]{3,2,1,0:T(8,128)(2,1)S(1)}, u32[]{:S(2)}, u32[]{:S(2)}) collective-permute-start(bf16[4,2,32,128]{3,2,1,0:T(8,128)(2,1)S(1)} %get-tuple-element.29), channel_id=1, source_target_pairs={{0,4},{2,6},{4,0},{6,2},{8,12},{10,14},{12,8},{14,10},{16,20},{18,... | collective-permute-start | bytes 196616 | tf_op jit(solution)/shard_map/ppermute | solution.py:315
  9.1 0.1 collective-permute-start.1
  9.4 1.9 %collective-permute-start.11 = (bf16[4,2,32,128]{3,2,1,0:T(8,128)(2,1)S(1)}, bf16[4,2,32,128]{3,2,1,0:T(8,128)(2,1)S(1)}, u32[]{:S(2)}, u32[]{:S(2)}) collective-permute-start(bf16[4,2,32,128]{3,2,1,0:T(8,128)(2,1)S(1)} %get-tuple-element.25), channel_id=1, source_target_pairs={{0,8},{2,10},{4,12},{6,14},{8,0},{10,2},{12,4},{14,6},{16,24},{18,... | collective-permute-start | bytes 196616 | tf_op jit(solution)/shard_map/ppermute | solution.py:315
  11.3 1.4 %collective-permute-start.13 = (bf16[4,2,32,128]{3,2,1,0:T(8,128)(2,1)S(1)}, bf16[4,2,32,128]{3,2,1,0:T(8,128)(2,1)S(1)}, u32[]{:S(2)}, u32[]{:S(2)}) collective-permute-start(bf16[4,2,32,128]{3,2,1,0:T(8,128)(2,1)S(1)} %get-tuple-element.26), channel_id=1, source_target_pairs={{0,12},{2,14},{4,8},{6,10},{8,4},{10,6},{12,0},{14,2},{16,28},{18,... | collective-permute-start | bytes 196616 | tf_op jit(solution)/shard_map/ppermute | solution.py:315
  12.7 1.5 %whiten_block.1.refs_2_.refs_1_ = bf16[8,4,2,128,128]{4,3,2,1,0:T(8,128)(2,1)S(1)} custom-call(s32[1]{0:T(128)} %bitcast.meta, bf16[2,512,8,128]{3,2,1,0:T(8,128)(2,1)S(1)} %copy-done), custom_call_target="tpu_custom_call" | custom-call | flops 16777216 | bytes 4194304 | tf_op jit(solution)/shard_map/whiten_block/pallas_call | solution.py:152
  14.3 0.3 collective-permute-start.12
  14.5 4.0 %collective-permute-start.4 = (bf16[4,2,32,128]{3,2,1,0:T(8,128)(2,1)S(1)}, bf16[4,2,32,128]{3,2,1,0:T(8,128)(2,1)S(1)}, u32[]{:S(2)}, u32[]{:S(2)}) collective-permute-start(bf16[4,2,32,128]{3,2,1,0:T(8,128)(2,1)S(1)} %fusion.4.left), channel_id=1, source_target_pairs={{0,24},{2,26},{4,28},{6,30},{8,16},{10,18},{12,20},{14,22},{16,8},... | collective-permute-start | bytes 196616 | tf_op jit(solution)/shard_map/ppermute | solution.py:315
  18.6 3.7 %collective-permute-start.14 = (bf16[4,2,32,128]{3,2,1,0:T(8,128)(2,1)S(1)}, bf16[4,2,32,128]{3,2,1,0:T(8,128)(2,1)S(1)}, u32[]{:S(2)}, u32[]{:S(2)}) collective-permute-start(bf16[4,2,32,128]{3,2,1,0:T(8,128)(2,1)S(1)} %fusion.2.left), channel_id=1, source_target_pairs={{0,24},{2,26},{4,28},{6,30},{8,16},{10,18},{12,20},{14,22},{16,8},... | collective-permute-start | bytes 196616 | tf_op jit(solution)/shard_map/ppermute | solution.py:315
  22.3 1.6 %collective-permute-start.7 = (bf16[4,2,32,128]{3,2,1,0:T(8,128)(2,1)S(1)}, bf16[4,2,32,128]{3,2,1,0:T(8,128)(2,1)S(1)}, u32[]{:S(2)}, u32[]{:S(2)}) collective-permute-start(bf16[4,2,32,128]{3,2,1,0:T(8,128)(2,1)S(1)} %whiten_sources.2.refs_0_), channel_id=1, source_target_pairs={{0,12},{2,14},{4,8},{6,10},{8,4},{10,6},{12,0},{14,2},{16,28},{18,... | collective-permute-start | bytes 196616 | tf_op jit(solution)/shard_map/ppermute | solution.py:315
  23.9 1.9 %collective-permute-start.5 = (bf16[4,2,32,128]{3,2,1,0:T(8,128)(2,1)S(1)}, bf16[4,2,32,128]{3,2,1,0:T(8,128)(2,1)S(1)}, u32[]{:S(2)}, u32[]{:S(2)}) collective-permute-start(bf16[4,2,32,128]{3,2,1,0:T(8,128)(2,1)S(1)} %whiten_sources.2.refs_0_), channel_id=1, source_target_pairs={{0,8},{2,10},{4,12},{6,14},{8,0},{10,2},{12,4},{14,6},{16,24},{18,... | collective-permute-start | bytes 196616 | tf_op jit(solution)/shard_map/ppermute | solution.py:315
  25.9 1.6 %collective-permute-start.17 = (bf16[4,2,32,128]{3,2,1,0:T(8,128)(2,1)S(1)}, bf16[4,2,32,128]{3,2,1,0:T(8,128)(2,1)S(1)}, u32[]{:S(2)}, u32[]{:S(2)}) collective-permute-start(bf16[4,2,32,128]{3,2,1,0:T(8,128)(2,1)S(1)} %whiten_sources.3.refs_0_), channel_id=1, source_target_pairs={{0,12},{2,14},{4,8},{6,10},{8,4},{10,6},{12,0},{14,2},{16,28},{18,... | collective-permute-start | bytes 196616 | tf_op jit(solution)/shard_map/ppermute | solution.py:315
  27.6 0.4 collective-permute-done.7.refs_3_
  28.0 1.6 %collective-permute-start.15 = (bf16[4,2,32,128]{3,2,1,0:T(8,128)(2,1)S(1)}, bf16[4,2,32,128]{3,2,1,0:T(8,128)(2,1)S(1)}, u32[]{:S(2)}, u32[]{:S(2)}) collective-permute-start(bf16[4,2,32,128]{3,2,1,0:T(8,128)(2,1)S(1)} %whiten_sources.3.refs_0_), channel_id=1, source_target_pairs={{0,8},{2,10},{4,12},{6,14},{8,0},{10,2},{12,4},{14,6},{16,24},{18,... | collective-permute-start | bytes 196616 | tf_op jit(solution)/shard_map/ppermute | solution.py:315
  29.6 1.1 %cross_coefficients.7.refs_1_.refs_4_ = f32[56,2048]{1,0:T(8,128)S(1)} custom-call(s32[1]{0:T(128)} %bitcast.meta, bf16[4,4,2,32,128]{4,3,2,1,0:T(8,128)(2,1)S(1)} %stack.2.refs_0_, bf16[8,4,2,128,128]{4,3,2,1,0:T(8,128)(2,1)S(1)} %whiten_block.1.refs_2_.refs_1_, bf16[8,56,128]{2,1,0:T(8,128)(2,1)S(1)} %copy-done.1), custom_call_target="tpu_custom_call" | custom-call | flops 1024 | bytes 1024 | tf_op jit(solution)/shard_map/cross_coefficients/pallas_call | solution.py:221
  30.7 0.5 collective-permute-done.17.refs_3_
  31.2 0.7 %collective-permute-done.16.refs_2_ = bf16[4,2,32,128]{3,2,1,0:T(8,128)(2,1)S(1)} collective-permute-done((bf16[4,2,32,128]{3,2,1,0:T(8,128)(2,1)S(1)}, bf16[4,2,32,128]{3,2,1,0:T(8,128)(2,1)S(1)}, u32[]{:S(2)}, u32[]{:S(2)}) %collective-permute-start.16) | collective-permute-done | bytes 65568 | tf_op jit(solution)/shard_map/ppermute | solution.py:315
  31.9 0.3 collective-permute-done.15.refs_1_
  32.3 1.1 %cross_coefficients.8 = bf16[56,2048]{1,0:T(8,128)(2,1)S(1)} custom-call(s32[1]{0:T(128)} %bitcast.meta, bf16[4,4,2,32,128]{4,3,2,1,0:T(8,128)(2,1)S(1)} %collective-permute-done.8.refs_1_.refs_0_, f32[56,2048]{1,0:T(8,128)S(1)} %cross_coefficients.7.refs_1_.refs_4_, bf16[8,4,2,128,128]{4,3,2,1,0:T(8,128)(2,1)S(1)} %whiten_block.1.refs_2_.refs_1_, ...), custom_call_target="tpu_custom_call" | custom-call | flops 1024 | bytes 1024 | tf_op jit(solution)/shard_map/cross_coefficients/pallas_call | solution.py:221
  33.4 1.6 %collective-permute-start.9 = (bf16[56,2048]{1,0:T(8,128)(2,1)S(1)}, bf16[56,2048]{1,0:T(8,128)(2,1)S(1)}, u32[]{:S(2)}, u32[]{:S(2)}) collective-permute-start(bf16[56,2048]{1,0:T(8,128)(2,1)S(1)} %cross_coefficients.8), channel_id=1, source_target_pairs={{0,1},{1,0},{2,3},{3,2},{4,5},{5,4},{6,7},{7,6},{8,9},{9,8},{10,11... | collective-permute-start | bytes 688136 | tf_op jit(solution)/shard_map/ppermute | solution.py:367
  35.0 1.1 %cross_coefficients.10.refs_1_ = f32[56,2048]{1,0:T(8,128)S(1)} custom-call(s32[1]{0:T(128)} %bitcast.meta, bf16[4,4,2,32,128]{4,3,2,1,0:T(8,128)(2,1)S(1)} %stack.3.refs_0_, bf16[8,4,2,128,128]{4,3,2,1,0:T(8,128)(2,1)S(1)} %whiten_block.1.refs_2_.refs_1_, bf16[8,56,128]{2,1,0:T(8,128)(2,1)S(1)} %copy-done.1), custom_call_target="tpu_custom_call" | custom-call | flops 1024 | bytes 1024 | tf_op jit(solution)/shard_map/cross_coefficients/pallas_call | solution.py:221
  36.1 1.1 %cross_coefficients.11 = bf16[56,2048]{1,0:T(8,128)(2,1)S(1)} custom-call(s32[1]{0:T(128)} %bitcast.meta, bf16[4,4,2,32,128]{4,3,2,1,0:T(8,128)(2,1)S(1)} %collective-permute-done.18.refs_1_.refs_0_, f32[56,2048]{1,0:T(8,128)S(1)} %cross_coefficients.10.refs_1_, bf16[8,4,2,128,128]{4,3,2,1,0:T(8,128)(2,1)S(1)} %whiten_block.1.refs_2_.refs_1_, ...), custom_call_target="tpu_custom_call" | custom-call | flops 1024 | bytes 1024 | tf_op jit(solution)/shard_map/cross_coefficients/pallas_call | solution.py:221
  37.2 0.6 %collective-permute-start.19 = (bf16[56,2048]{1,0:T(8,128)(2,1)S(1)}, bf16[56,2048]{1,0:T(8,128)(2,1)S(1)}, u32[]{:S(2)}, u32[]{:S(2)}) collective-permute-start(bf16[56,2048]{1,0:T(8,128)(2,1)S(1)} %cross_coefficients.11), channel_id=1, source_target_pairs={{0,1},{1,0},{2,3},{3,2},{4,5},{5,4},{6,7},{7,6},{8,9},{9,8},{10,11... | collective-permute-start | bytes 688136 | tf_op jit(solution)/shard_map/ppermute | solution.py:367
  37.8 2.0 %cross_coefficients.6.refs_0_ = f32[56,2048]{1,0:T(8,128)S(1)} custom-call(s32[1]{0:T(128)} %bitcast.meta, bf16[4,4,2,32,128]{4,3,2,1,0:T(8,128)(2,1)S(1)} %stack.2.refs_0_, bf16[4,4,2,32,128]{4,3,2,1,0:T(8,128)(2,1)S(1)} %collective-permute-done.8.refs_1_.refs_0_, bf16[8,4,2,128,128]{4,3,2,1,0:T(8,128)(2,1)S(1)} %whiten_block.1.refs_2_.refs_1_, ...), custom_call_target="tpu_custom_call" | custom-call | flops 1024 | bytes 1024 | tf_op jit(solution)/shard_map/cross_coefficients/pallas_call | solution.py:221
  39.9 2.0 %cross_coefficients.9.refs_1_ = f32[56,2048]{1,0:T(8,128)S(1)} custom-call(s32[1]{0:T(128)} %bitcast.meta, bf16[4,4,2,32,128]{4,3,2,1,0:T(8,128)(2,1)S(1)} %stack.3.refs_0_, bf16[4,4,2,32,128]{4,3,2,1,0:T(8,128)(2,1)S(1)} %collective-permute-done.18.refs_1_.refs_0_, bf16[8,4,2,128,128]{4,3,2,1,0:T(8,128)(2,1)S(1)} %whiten_block.1.refs_2_.refs_1_, ...), custom_call_target="tpu_custom_call" | custom-call | flops 1024 | bytes 1024 | tf_op jit(solution)/shard_map/cross_coefficients/pallas_call | solution.py:221
  41.9 1.3 %lags.2.refs_0_ = f32[32,128,128]{2,1,0:T(8,128)} custom-call(f32[56,2048]{1,0:T(8,128)S(1)} %cross_coefficients.6.refs_0_, bf16[56,2048]{1,0:T(8,128)(2,1)S(1)} %collective-permute-done.9.refs_1_, bf16[168,128]{1,0:T(8,128)(2,1)S(1)} %copy-done.2), custom_call_target="tpu_custom_call" | custom-call | flops 268435456 | bytes 1024 | tf_op jit(solution)/shard_map/lags/pallas_call | solution.py:272
  43.2 3.2 %collective-permute-done.19.refs_2_ = bf16[56,2048]{1,0:T(8,128)(2,1)S(1)} collective-permute-done((bf16[56,2048]{1,0:T(8,128)(2,1)S(1)}, bf16[56,2048]{1,0:T(8,128)(2,1)S(1)}, u32[]{:S(2)}, u32[]{:S(2)}) %collective-permute-start.19) | collective-permute-done | bytes 229408 | tf_op jit(solution)/shard_map/ppermute | solution.py:367
  46.4 1.3 %lags.3 = f32[32,128,128]{2,1,0:T(8,128)} custom-call(f32[32,128,128]{2,1,0:T(8,128)} %lags.2.refs_0_, f32[56,2048]{1,0:T(8,128)S(1)} %cross_coefficients.9.refs_1_, bf16[56,2048]{1,0:T(8,128)(2,1)S(1)} %collective-permute-done.19.refs_2_, bf16[168,128]{1,0:T(8,128)(2,1)S(1)} %copy-done.2), custom_call_target="tpu_custom_call", output_to_operand_aliasing={{}: (0, {})} | custom-call | flops 1024 | bytes 1024 | tf_op jit(solution)/shard_map/lags/pallas_call | solution.py:272
  (35 shorter events, 0.6 us)
Async XLA Ops:
  1.9 2.6 %collective-permute-start = (bf16[4,4,2,32,128]{4,3,2,1,0:T(8,128)(2,1)S(1)}, bf16[4,4,2,32,128]{4,3,2,1,0:T(8,128)(2,1)S(1)}, u32[]{:S(2)}, u32[]{:S(2)}) collective-permute-start(bf16[4,4,2,32,128]{4,3,2,1,0:T(8,128)(2,1)S(1)} %get-tuple-element.16), channel_id=1, source_target_pairs={{0,2},{2,0},{4,6},{6,4},{8,10},{10,8},{12,14},{14,12},{16,18},{18,... | collective-permute-start | bytes 786440 | tf_op jit(solution)/shard_map/ppermute | solution.py:315
  2.4 6.9 %collective-permute-start.10 = (bf16[4,4,2,32,128]{4,3,2,1,0:T(8,128)(2,1)S(1)}, bf16[4,4,2,32,128]{4,3,2,1,0:T(8,128)(2,1)S(1)}, u32[]{:S(2)}, u32[]{:S(2)}) collective-permute-start(bf16[4,4,2,32,128]{4,3,2,1,0:T(8,128)(2,1)S(1)} %get-tuple-element.24), channel_id=1, source_target_pairs={{0,2},{2,0},{4,6},{6,4},{8,10},{10,8},{12,14},{14,12},{16,18},{18,... | collective-permute-start | bytes 786440 | tf_op jit(solution)/shard_map/ppermute | solution.py:315
  2.4 10.3 %copy-start = (bf16[2,512,8,128]{3,2,1,0:T(8,128)(2,1)S(1)}, bf16[2,512,8,128]{3,2,1,0:T(8,128)(2,1)}, u32[]{:S(2)}) copy-start(bf16[2,512,8,128]{3,2,1,0:T(8,128)(2,1)} %spectra.4) | copy-start | bytes 6291460
  4.6 9.7 %collective-permute-start.3 = (bf16[4,2,32,128]{3,2,1,0:T(8,128)(2,1)S(1)}, bf16[4,2,32,128]{3,2,1,0:T(8,128)(2,1)S(1)}, u32[]{:S(2)}, u32[]{:S(2)}) collective-permute-start(bf16[4,2,32,128]{3,2,1,0:T(8,128)(2,1)S(1)} %get-tuple-element.28), channel_id=1, source_target_pairs={{0,12},{2,14},{4,8},{6,10},{8,4},{10,6},{12,0},{14,2},{16,28},{18,... | collective-permute-start | bytes 196616 | tf_op jit(solution)/shard_map/ppermute | solution.py:315
  8.6 5.9 %collective-permute-start.2 = (bf16[4,2,32,128]{3,2,1,0:T(8,128)(2,1)S(1)}, bf16[4,2,32,128]{3,2,1,0:T(8,128)(2,1)S(1)}, u32[]{:S(2)}, u32[]{:S(2)}) collective-permute-start(bf16[4,2,32,128]{3,2,1,0:T(8,128)(2,1)S(1)} %get-tuple-element.29), channel_id=1, source_target_pairs={{0,4},{2,6},{4,0},{6,2},{8,12},{10,14},{12,8},{14,10},{16,20},{18,... | collective-permute-start | bytes 196616 | tf_op jit(solution)/shard_map/ppermute | solution.py:315
  9.1 5.4 %collective-permute-start.1 = (bf16[4,2,32,128]{3,2,1,0:T(8,128)(2,1)S(1)}, bf16[4,2,32,128]{3,2,1,0:T(8,128)(2,1)S(1)}, u32[]{:S(2)}, u32[]{:S(2)}) collective-permute-start(bf16[4,2,32,128]{3,2,1,0:T(8,128)(2,1)S(1)} %get-tuple-element.30), channel_id=1, source_target_pairs={{0,8},{2,10},{4,12},{6,14},{8,0},{10,2},{12,4},{14,6},{16,24},{18,... | collective-permute-start | bytes 196616 | tf_op jit(solution)/shard_map/ppermute | solution.py:315
  9.4 9.2 %collective-permute-start.11 = (bf16[4,2,32,128]{3,2,1,0:T(8,128)(2,1)S(1)}, bf16[4,2,32,128]{3,2,1,0:T(8,128)(2,1)S(1)}, u32[]{:S(2)}, u32[]{:S(2)}) collective-permute-start(bf16[4,2,32,128]{3,2,1,0:T(8,128)(2,1)S(1)} %get-tuple-element.25), channel_id=1, source_target_pairs={{0,8},{2,10},{4,12},{6,14},{8,0},{10,2},{12,4},{14,6},{16,24},{18,... | collective-permute-start | bytes 196616 | tf_op jit(solution)/shard_map/ppermute | solution.py:315
  11.3 7.2 %collective-permute-start.13 = (bf16[4,2,32,128]{3,2,1,0:T(8,128)(2,1)S(1)}, bf16[4,2,32,128]{3,2,1,0:T(8,128)(2,1)S(1)}, u32[]{:S(2)}, u32[]{:S(2)}) collective-permute-start(bf16[4,2,32,128]{3,2,1,0:T(8,128)(2,1)S(1)} %get-tuple-element.26), channel_id=1, source_target_pairs={{0,12},{2,14},{4,8},{6,10},{8,4},{10,6},{12,0},{14,2},{16,28},{18,... | collective-permute-start | bytes 196616 | tf_op jit(solution)/shard_map/ppermute | solution.py:315
  12.7 16.9 %copy-start.1 = (bf16[8,56,128]{2,1,0:T(8,128)(2,1)S(1)}, bf16[8,56,128]{2,1,0:T(8,128)(2,1)}, u32[]{:S(2)}) copy-start(bf16[8,56,128]{2,1,0:T(8,128)(2,1)} %constant.22.refs_3_.refs_2_) | copy-start | bytes 344068
  14.3 4.3 %collective-permute-start.12 = (bf16[4,2,32,128]{3,2,1,0:T(8,128)(2,1)S(1)}, bf16[4,2,32,128]{3,2,1,0:T(8,128)(2,1)S(1)}, u32[]{:S(2)}, u32[]{:S(2)}) collective-permute-start(bf16[4,2,32,128]{3,2,1,0:T(8,128)(2,1)S(1)} %get-tuple-element.27), channel_id=1, source_target_pairs={{0,4},{2,6},{4,0},{6,2},{8,12},{10,14},{12,8},{14,10},{16,20},{18,... | collective-permute-start | bytes 196616 | tf_op jit(solution)/shard_map/ppermute | solution.py:315
  14.5 7.7 %collective-permute-start.4 = (bf16[4,2,32,128]{3,2,1,0:T(8,128)(2,1)S(1)}, bf16[4,2,32,128]{3,2,1,0:T(8,128)(2,1)S(1)}, u32[]{:S(2)}, u32[]{:S(2)}) collective-permute-start(bf16[4,2,32,128]{3,2,1,0:T(8,128)(2,1)S(1)} %fusion.4.left), channel_id=1, source_target_pairs={{0,24},{2,26},{4,28},{6,30},{8,16},{10,18},{12,20},{14,22},{16,8},... | collective-permute-start | bytes 196616 | tf_op jit(solution)/shard_map/ppermute | solution.py:315
  18.6 7.3 %collective-permute-start.14 = (bf16[4,2,32,128]{3,2,1,0:T(8,128)(2,1)S(1)}, bf16[4,2,32,128]{3,2,1,0:T(8,128)(2,1)S(1)}, u32[]{:S(2)}, u32[]{:S(2)}) collective-permute-start(bf16[4,2,32,128]{3,2,1,0:T(8,128)(2,1)S(1)} %fusion.2.left), channel_id=1, source_target_pairs={{0,24},{2,26},{4,28},{6,30},{8,16},{10,18},{12,20},{14,22},{16,8},... | collective-permute-start | bytes 196616 | tf_op jit(solution)/shard_map/ppermute | solution.py:315
  22.3 5.6 %collective-permute-start.7 = (bf16[4,2,32,128]{3,2,1,0:T(8,128)(2,1)S(1)}, bf16[4,2,32,128]{3,2,1,0:T(8,128)(2,1)S(1)}, u32[]{:S(2)}, u32[]{:S(2)}) collective-permute-start(bf16[4,2,32,128]{3,2,1,0:T(8,128)(2,1)S(1)} %whiten_sources.2.refs_0_), channel_id=1, source_target_pairs={{0,12},{2,14},{4,8},{6,10},{8,4},{10,6},{12,0},{14,2},{16,28},{18,... | collective-permute-start | bytes 196616 | tf_op jit(solution)/shard_map/ppermute | solution.py:315
  23.9 5.6 %collective-permute-start.6 = (bf16[4,2,32,128]{3,2,1,0:T(8,128)(2,1)S(1)}, bf16[4,2,32,128]{3,2,1,0:T(8,128)(2,1)S(1)}, u32[]{:S(2)}, u32[]{:S(2)}) collective-permute-start(bf16[4,2,32,128]{3,2,1,0:T(8,128)(2,1)S(1)} %whiten_sources.2.refs_0_), channel_id=1, source_target_pairs={{0,4},{2,6},{4,0},{6,2},{8,12},{10,14},{12,8},{14,10},{16,20},{18,... | collective-permute-start | bytes 196616 | tf_op jit(solution)/shard_map/ppermute | solution.py:315
  23.9 5.6 %collective-permute-start.5 = (bf16[4,2,32,128]{3,2,1,0:T(8,128)(2,1)S(1)}, bf16[4,2,32,128]{3,2,1,0:T(8,128)(2,1)S(1)}, u32[]{:S(2)}, u32[]{:S(2)}) collective-permute-start(bf16[4,2,32,128]{3,2,1,0:T(8,128)(2,1)S(1)} %whiten_sources.2.refs_0_), channel_id=1, source_target_pairs={{0,8},{2,10},{4,12},{6,14},{8,0},{10,2},{12,4},{14,6},{16,24},{18,... | collective-permute-start | bytes 196616 | tf_op jit(solution)/shard_map/ppermute | solution.py:315
  25.9 5.2 %collective-permute-start.17 = (bf16[4,2,32,128]{3,2,1,0:T(8,128)(2,1)S(1)}, bf16[4,2,32,128]{3,2,1,0:T(8,128)(2,1)S(1)}, u32[]{:S(2)}, u32[]{:S(2)}) collective-permute-start(bf16[4,2,32,128]{3,2,1,0:T(8,128)(2,1)S(1)} %whiten_sources.3.refs_0_), channel_id=1, source_target_pairs={{0,12},{2,14},{4,8},{6,10},{8,4},{10,6},{12,0},{14,2},{16,28},{18,... | collective-permute-start | bytes 196616 | tf_op jit(solution)/shard_map/ppermute | solution.py:315
  27.6 4.3 %collective-permute-start.16 = (bf16[4,2,32,128]{3,2,1,0:T(8,128)(2,1)S(1)}, bf16[4,2,32,128]{3,2,1,0:T(8,128)(2,1)S(1)}, u32[]{:S(2)}, u32[]{:S(2)}) collective-permute-start(bf16[4,2,32,128]{3,2,1,0:T(8,128)(2,1)S(1)} %whiten_sources.3.refs_0_), channel_id=1, source_target_pairs={{0,4},{2,6},{4,0},{6,2},{8,12},{10,14},{12,8},{14,10},{16,20},{18,... | collective-permute-start | bytes 196616 | tf_op jit(solution)/shard_map/ppermute | solution.py:315
  28.0 4.3 %collective-permute-start.15 = (bf16[4,2,32,128]{3,2,1,0:T(8,128)(2,1)S(1)}, bf16[4,2,32,128]{3,2,1,0:T(8,128)(2,1)S(1)}, u32[]{:S(2)}, u32[]{:S(2)}) collective-permute-start(bf16[4,2,32,128]{3,2,1,0:T(8,128)(2,1)S(1)} %whiten_sources.3.refs_0_), channel_id=1, source_target_pairs={{0,8},{2,10},{4,12},{6,14},{8,0},{10,2},{12,4},{14,6},{16,24},{18,... | collective-permute-start | bytes 196616 | tf_op jit(solution)/shard_map/ppermute | solution.py:315
  29.5 2.8 %collective-permute-start.8 = (bf16[4,4,2,32,128]{4,3,2,1,0:T(8,128)(2,1)S(1)}, bf16[4,4,2,32,128]{4,3,2,1,0:T(8,128)(2,1)S(1)}, u32[]{:S(2)}, u32[]{:S(2)}) collective-permute-start(bf16[4,4,2,32,128]{4,3,2,1,0:T(8,128)(2,1)S(1)} %stack.2.refs_0_), channel_id=1, source_target_pairs={{0,2},{2,0},{4,6},{6,4},{8,10},{10,8},{12,14},{14,12},{16,18},{18,... | collective-permute-start | bytes 786440 | tf_op jit(solution)/shard_map/ppermute | solution.py:315
  32.2 3.9 %collective-permute-start.18 = (bf16[4,4,2,32,128]{4,3,2,1,0:T(8,128)(2,1)S(1)}, bf16[4,4,2,32,128]{4,3,2,1,0:T(8,128)(2,1)S(1)}, u32[]{:S(2)}, u32[]{:S(2)}) collective-permute-start(bf16[4,4,2,32,128]{4,3,2,1,0:T(8,128)(2,1)S(1)} %stack.3.refs_0_), channel_id=1, source_target_pairs={{0,2},{2,0},{4,6},{6,4},{8,10},{10,8},{12,14},{14,12},{16,18},{18,... | collective-permute-start | bytes 786440 | tf_op jit(solution)/shard_map/ppermute | solution.py:315
  33.4 8.5 %collective-permute-start.9 = (bf16[56,2048]{1,0:T(8,128)(2,1)S(1)}, bf16[56,2048]{1,0:T(8,128)(2,1)S(1)}, u32[]{:S(2)}, u32[]{:S(2)}) collective-permute-start(bf16[56,2048]{1,0:T(8,128)(2,1)S(1)} %cross_coefficients.8), channel_id=1, source_target_pairs={{0,1},{1,0},{2,3},{3,2},{4,5},{5,4},{6,7},{7,6},{8,9},{9,8},{10,11... | collective-permute-start | bytes 688136 | tf_op jit(solution)/shard_map/ppermute | solution.py:367
  37.2 9.2 %collective-permute-start.19 = (bf16[56,2048]{1,0:T(8,128)(2,1)S(1)}, bf16[56,2048]{1,0:T(8,128)(2,1)S(1)}, u32[]{:S(2)}, u32[]{:S(2)}) collective-permute-start(bf16[56,2048]{1,0:T(8,128)(2,1)S(1)} %cross_coefficients.11), channel_id=1, source_target_pairs={{0,1},{1,0},{2,3},{3,2},{4,5},{5,4},{6,7},{7,6},{8,9},{9,8},{10,11... | collective-permute-start | bytes 688136 | tf_op jit(solution)/shard_map/ppermute | solution.py:367
  39.8 2.1 %copy-start.2 = (bf16[168,128]{1,0:T(8,128)(2,1)S(1)}, bf16[168,128]{1,0:T(8,128)(2,1)}, u32[]{:S(2)}) copy-start(bf16[168,128]{1,0:T(8,128)(2,1)} %constant.19.clone.refs_2_.refs_3_) | copy-start | bytes 129028

commit v3 on v2

--- a/solution.py
+++ b/solution.py
@@ -14,6 +14,7 @@
 LAGS = 128
 RANK = 56
 LOTS = 2
+BLOCK = 8
 WATER = 0.5
 VMEM_LIMIT = 48 * 1024 * 1024
 
@@ -233,15 +234,17 @@
     )(meta, *operands)
 
 
-def lags_kernel(shards, first, *refs):
-    own, *others, basis, out, staged, sems = refs[-shards - 4 :]
+def lags_kernel(blocks, first, skip, *refs):
+    *inputs, out, staged, sems = refs
+    own, *others, basis = inputs[len(inputs) - 2 - blocks[0] * blocks[1] :]
     count = staged.shape[0]
+    size = count // blocks[0]
     step = count // sems.shape[0]
     copies = []
     for s in range(count):
-        at = slice(s * 128, (s + 1) * 128)
-        value = own[:, at]
-        for other in others:
+        at = slice(s % size * 128, (s % size + 1) * 128)
+        value = own[:, (skip + s) * 128 : (skip + s + 1) * 128]
+        for other in others[s // size * blocks[1] : (s // size + 1) * blocks[1]]:
             value = value + other[:, at].astype(jnp.float32)
         high = value.astype(jnp.bfloat16)
         low = (value - high.astype(jnp.float32)).astype(jnp.bfloat16)
@@ -260,9 +263,9 @@
         copy.wait()
 
 
-def to_lags(own, others, basis, lot, done, cost):
-    count = own.shape[1] // 128
-    operands = [own, *others, basis]
+def to_lags(own, blocks, basis, first, skip, total, done, cost):
+    count = len(blocks) * blocks[0][0].shape[1] // 128
+    operands = [own, *[part for block in blocks for part in block], basis]
     specs = [pl.BlockSpec(memory_space=pltpu.VMEM)] * len(operands)
     aliases = {}
     if done is not None:
@@ -270,10 +273,10 @@
         specs.insert(0, pl.BlockSpec(memory_space=pl.ANY))
         operands.insert(0, done)
     return pl.pallas_call(
-        functools.partial(lags_kernel, 1 + len(others), lot * count),
+        functools.partial(lags_kernel, (len(blocks), len(blocks[0])), first, skip),
         in_specs=specs,
         out_specs=pl.BlockSpec(memory_space=pl.ANY),
-        out_shape=jax.ShapeDtypeStruct((LOTS * count, 128, LAGS), jnp.float32),
+        out_shape=jax.ShapeDtypeStruct((total, 128, LAGS), jnp.float32),
         input_output_aliases=aliases,
         scratch_shapes=[
             pltpu.VMEM((count, 128, LAGS), jnp.float32),
@@ -348,31 +351,41 @@
     arrived = [[chunk] + [across(chunk, mask) for mask in HOP_MASKS] for chunk in own]
 
     every = steps * keep // LOTS
+    block = math.gcd(BLOCK, every)
     near, far = (0, 1, 2, 3), (4, 5, 6, 7)
     out = None
     sent, kept = [], []
-    got = []
     for i in lots:
         chunks = stack(arrived[i], [begun] if i else [])
         beside = across(chunks, CORE_MASK)
-        begun = coefficients(
-            meta, {near: chunks}, None, white, table, every, every * (shards - 1), jnp.float32
-        )
-        got = [
-            coefficients(meta, {far: beside}, (begun, (d - 1) * every), white, table, d * every, every, jnp.bfloat16)
-            for d in range(1, shards)
-        ]
-        sent.append(
-            [
-                lax.ppermute(part, ("tm", "freq"), [(m, m ^ (d + 1)) for m in range(shards)])
-                for d, part in enumerate(got)
+        low = 0 if i + 1 < LOTS else every
+        begun = coefficients(meta, {near: chunks}, None, white, table, low, every * shards - low, jnp.float32)
+        blocks = []
+        for first in range(0, every, block):
+            got = [
+                coefficients(
+                    meta, {far: beside}, (begun, d * every + first - low), white, table, d * every + first, block,
+                    jnp.bfloat16,
+                )
+                for d in range(1, shards)
             ]
-        )
-        kept.append(
-            coefficients(meta, {near: chunks, far: beside}, None, white, table, 0, every, jnp.float32)
-        )
+            blocks.append(
+                [
+                    lax.ppermute(part, ("tm", "freq"), [(m, m ^ (d + 1)) for m in range(shards)])
+                    for d, part in enumerate(got)
+                ]
+            )
+        sent.append(blocks)
+        if low:
+            own = coefficients(meta, {near: chunks, far: beside}, None, white, table, 0, every, jnp.float32)
+        else:
+            own = coefficients(meta, {far: beside}, (begun, 0), white, table, 0, every, jnp.float32)
+        kept.append(own)
     for i in lots:
-        out = to_lags(kept[i], sent[i], basis, i, out, 1 << (10 if i + 1 == LOTS else 28))
+        size = every if i + 1 < LOTS else block
+        for first in range(0, every, size):
+            some = sent[i][first // block : (first + size) // block]
+            out = to_lags(kept[i], some, basis, i * every + first, first, every * LOTS, out, 1 << 28)
     return out.reshape(steps, keep, 128, LAGS)
 
 

time: 47.8 us -> 47.2 us (0.987)
  waiting for transfers between devices: 5.19 us -> 1.13 us
  starting transfers between devices: 25.5 us -> 27.7 us
  Pallas kernels: 16.5 us -> 17.8 us
    ppermute x2 -> x4, waiting for transfers between devices: 3.21 us -> 0.01 us  [per_device(): lax.ppermute(part, ('tm', 'freq'), [(m, m ^ d + 1) for m in range(shards)])]
    ppermute x2 -> x4, starting transfers between devices: 2.16 us -> 4.31 us  [per_device(): lax.ppermute(part, ('tm', 'freq'), [(m, m ^ d + 1) for m in range(shards)])]
    pallas_call x2 -> x3, Pallas kernels: 2.57 us -> 3.47 us  [to_lags(): pl.pallas_call(functools.partial(lags_kernel, (len(blocks), len(blocks[0]...]
    ppermute x18, waiting for transfers between devices: 1.98 us -> 1.11 us  [across(): return lax.ppermute(block, 'chan', [(i, i ^ mask) for i in range(size)])]
    pallas_call x6 -> x8, Pallas kernels: 8.45 us -> 8.8 us  [coefficients(): pl.pallas_call(functools.partial(cross_kernel, places, first, begun, len(...]
  transfers between devices with their start and end apart: 20 -> 22, of which waited for: 6 -> 4; matrix products, arithmetic and copies ran while one was open for 0% -> 0% of each run, Pallas kernels for 28% -> 31%
where the time goes in v3:
time: 47.2 us; the launch traced here: 47.1 us
  starting transfers between devices  27.7 us (59%)
  Pallas kernels  17.8 us (38%)
  waiting for transfers between devices  1.13 us (2%)
    ppermute x18, starting transfers between devices, across(): return lax.ppermute(block, 'chan', [(i, i ^ mask) for i in range(size)])  23.4 us
    pallas_call x8, Pallas kernels, coefficients(): pl.pallas_call(functools.partial(cross_kernel, places, first, begun, len(...  8.8 us
    ppermute x4, starting transfers between devices, per_device(): lax.ppermute(part, ('tm', 'freq'), [(m, m ^ d + 1) for m in range(shards)])  4.31 us
    pallas_call x2, Pallas kernels, pick(): pl.pallas_call(functools.partial(pick_kernel, shards, side), in_specs=[pl...  3.84 us
    pallas_call x3, Pallas kernels, to_lags(): pl.pallas_call(functools.partial(lags_kernel, (len(blocks), len(blocks[0]...  3.47 us
    pallas_call x1, Pallas kernels, whiten(): pl.pallas_call(whiten_kernel, grid_spec=pltpu.PrefetchScalarGridSpec(num_...  1.52 us
    ppermute x18, waiting for transfers between devices, across(): return lax.ppermute(block, 'chan', [(i, i ^ mask) for i in range(size)])  1.11 us
  transfers between devices with their start and end apart: 22, of which 4 were waited for; matrix products, arithmetic and copies ran while one was open for 0% of the time, Pallas kernels for 31%

profile of v3, /device:TPU:0, one launch (start us, length us, event | category | flops | bytes accessed | tf_op | source)
XLA Modules:
  0.0 47.1 jit_solution(5127195948400893638)
XLA Ops:
  0.0 1.8 %pick_sources.3 = (bf16[4,4,2,32,128]{4,3,2,1,0:T(8,128)(2,1)S(1)}, bf16[4,4,2,32,128]{4,3,2,1,0:T(8,128)(2,1)S(1)}) custom-call(s32[4]{0:T(128)} %owners_in.3, s32[4,16]{1,0:T(4,128)} %rows_in.3, bf16[2,512,8,128]{3,2,1,0:T(8,128)(2,1)} %spectra.4), custom_call_target="tpu_custom_call" | custom-call | flops 33554432 | bytes 2097152 | tf_op jit(solution)/shard_map/pick_sources/pallas_call | solution.py:97
  1.9 0.5 %collective-permute-start = (bf16[4,4,2,32,128]{4,3,2,1,0:T(8,128)(2,1)S(1)}, bf16[4,4,2,32,128]{4,3,2,1,0:T(8,128)(2,1)S(1)}, u32[]{:S(2)}, u32[]{:S(2)}) collective-permute-start(bf16[4,4,2,32,128]{4,3,2,1,0:T(8,128)(2,1)S(1)} %get-tuple-element.16), channel_id=1, source_target_pairs={{0,2},{2,0},{4,6},{6,4},{8,10},{10,8},{12,14},{14,12},{16,18},{18,... | collective-permute-start | bytes 786440 | tf_op jit(solution)/shard_map/ppermute | solution.py:318
  2.4 2.0 %pick_sources.2 = (bf16[4,4,2,32,128]{4,3,2,1,0:T(8,128)(2,1)S(1)}, bf16[4,4,2,32,128]{4,3,2,1,0:T(8,128)(2,1)S(1)}) custom-call(s32[4]{0:T(128)} %owners_in.3, s32[4,16]{1,0:T(4,128)} %rows_in.3, bf16[2,512,8,128]{3,2,1,0:T(8,128)(2,1)} %spectra.4), custom_call_target="tpu_custom_call" | custom-call | flops 33554432 | bytes 2097152 | tf_op jit(solution)/shard_map/pick_sources/pallas_call | solution.py:97
  4.6 4.0 %collective-permute-start.3 = (bf16[4,2,32,128]{3,2,1,0:T(8,128)(2,1)S(1)}, bf16[4,2,32,128]{3,2,1,0:T(8,128)(2,1)S(1)}, u32[]{:S(2)}, u32[]{:S(2)}) collective-permute-start(bf16[4,2,32,128]{3,2,1,0:T(8,128)(2,1)S(1)} %get-tuple-element.28), channel_id=1, source_target_pairs={{0,12},{2,14},{4,8},{6,10},{8,4},{10,6},{12,0},{14,2},{16,28},{18,... | collective-permute-start | bytes 196616 | tf_op jit(solution)/shard_map/ppermute | solution.py:318
  8.6 0.5 %collective-permute-start.2 = (bf16[4,2,32,128]{3,2,1,0:T(8,128)(2,1)S(1)}, bf16[4,2,32,128]{3,2,1,0:T(8,128)(2,1)S(1)}, u32[]{:S(2)}, u32[]{:S(2)}) collective-permute-start(bf16[4,2,32,128]{3,2,1,0:T(8,128)(2,1)S(1)} %get-tuple-element.29), channel_id=1, source_target_pairs={{0,4},{2,6},{4,0},{6,2},{8,12},{10,14},{12,8},{14,10},{16,20},{18,... | collective-permute-start | bytes 196616 | tf_op jit(solution)/shard_map/ppermute | solution.py:318
  9.4 1.9 %collective-permute-start.12 = (bf16[4,2,32,128]{3,2,1,0:T(8,128)(2,1)S(1)}, bf16[4,2,32,128]{3,2,1,0:T(8,128)(2,1)S(1)}, u32[]{:S(2)}, u32[]{:S(2)}) collective-permute-start(bf16[4,2,32,128]{3,2,1,0:T(8,128)(2,1)S(1)} %get-tuple-element.25), channel_id=1, source_target_pairs={{0,8},{2,10},{4,12},{6,14},{8,0},{10,2},{12,4},{14,6},{16,24},{18,... | collective-permute-start | bytes 196616 | tf_op jit(solution)/shard_map/ppermute | solution.py:318
  11.3 1.4 %collective-permute-start.14 = (bf16[4,2,32,128]{3,2,1,0:T(8,128)(2,1)S(1)}, bf16[4,2,32,128]{3,2,1,0:T(8,128)(2,1)S(1)}, u32[]{:S(2)}, u32[]{:S(2)}) collective-permute-start(bf16[4,2,32,128]{3,2,1,0:T(8,128)(2,1)S(1)} %get-tuple-element.26), channel_id=1, source_target_pairs={{0,12},{2,14},{4,8},{6,10},{8,4},{10,6},{12,0},{14,2},{16,28},{18,... | collective-permute-start | bytes 196616 | tf_op jit(solution)/shard_map/ppermute | solution.py:318
  12.7 1.5 %whiten_block.1.refs_1_.refs_2_ = bf16[8,4,2,128,128]{4,3,2,1,0:T(8,128)(2,1)S(1)} custom-call(s32[1]{0:T(128)} %bitcast.meta, bf16[2,512,8,128]{3,2,1,0:T(8,128)(2,1)S(1)} %copy-done), custom_call_target="tpu_custom_call" | custom-call | flops 16777216 | bytes 4194304 | tf_op jit(solution)/shard_map/whiten_block/pallas_call | solution.py:153
  14.5 4.0 %collective-permute-start.4 = (bf16[4,2,32,128]{3,2,1,0:T(8,128)(2,1)S(1)}, bf16[4,2,32,128]{3,2,1,0:T(8,128)(2,1)S(1)}, u32[]{:S(2)}, u32[]{:S(2)}) collective-permute-start(bf16[4,2,32,128]{3,2,1,0:T(8,128)(2,1)S(1)} %fusion.4.left), channel_id=1, source_target_pairs={{0,24},{2,26},{4,28},{6,30},{8,16},{10,18},{12,20},{14,22},{16,8},... | collective-permute-start | bytes 196616 | tf_op jit(solution)/shard_map/ppermute | solution.py:318
  18.6 3.7 %collective-permute-start.15 = (bf16[4,2,32,128]{3,2,1,0:T(8,128)(2,1)S(1)}, bf16[4,2,32,128]{3,2,1,0:T(8,128)(2,1)S(1)}, u32[]{:S(2)}, u32[]{:S(2)}) collective-permute-start(bf16[4,2,32,128]{3,2,1,0:T(8,128)(2,1)S(1)} %fusion.2.left), channel_id=1, source_target_pairs={{0,24},{2,26},{4,28},{6,30},{8,16},{10,18},{12,20},{14,22},{16,8},... | collective-permute-start | bytes 196616 | tf_op jit(solution)/shard_map/ppermute | solution.py:318
  22.3 1.6 %collective-permute-start.7 = (bf16[4,2,32,128]{3,2,1,0:T(8,128)(2,1)S(1)}, bf16[4,2,32,128]{3,2,1,0:T(8,128)(2,1)S(1)}, u32[]{:S(2)}, u32[]{:S(2)}) collective-permute-start(bf16[4,2,32,128]{3,2,1,0:T(8,128)(2,1)S(1)} %whiten_sources.2.refs_0_), channel_id=1, source_target_pairs={{0,12},{2,14},{4,8},{6,10},{8,4},{10,6},{12,0},{14,2},{16,28},{18,... | collective-permute-start | bytes 196616 | tf_op jit(solution)/shard_map/ppermute | solution.py:318
  23.9 1.9 %collective-permute-start.5 = (bf16[4,2,32,128]{3,2,1,0:T(8,128)(2,1)S(1)}, bf16[4,2,32,128]{3,2,1,0:T(8,128)(2,1)S(1)}, u32[]{:S(2)}, u32[]{:S(2)}) collective-permute-start(bf16[4,2,32,128]{3,2,1,0:T(8,128)(2,1)S(1)} %whiten_sources.2.refs_0_), channel_id=1, source_target_pairs={{0,8},{2,10},{4,12},{6,14},{8,0},{10,2},{12,4},{14,6},{16,24},{18,... | collective-permute-start | bytes 196616 | tf_op jit(solution)/shard_map/ppermute | solution.py:318
  25.9 1.6 %collective-permute-start.18 = (bf16[4,2,32,128]{3,2,1,0:T(8,128)(2,1)S(1)}, bf16[4,2,32,128]{3,2,1,0:T(8,128)(2,1)S(1)}, u32[]{:S(2)}, u32[]{:S(2)}) collective-permute-start(bf16[4,2,32,128]{3,2,1,0:T(8,128)(2,1)S(1)} %whiten_sources.3.refs_0_), channel_id=1, source_target_pairs={{0,12},{2,14},{4,8},{6,10},{8,4},{10,6},{12,0},{14,2},{16,28},{18,... | collective-permute-start | bytes 196616 | tf_op jit(solution)/shard_map/ppermute | solution.py:318
  27.6 0.4 collective-permute-done.7.refs_3_
  28.0 1.6 %collective-permute-start.16 = (bf16[4,2,32,128]{3,2,1,0:T(8,128)(2,1)S(1)}, bf16[4,2,32,128]{3,2,1,0:T(8,128)(2,1)S(1)}, u32[]{:S(2)}, u32[]{:S(2)}) collective-permute-start(bf16[4,2,32,128]{3,2,1,0:T(8,128)(2,1)S(1)} %whiten_sources.3.refs_0_), channel_id=1, source_target_pairs={{0,8},{2,10},{4,12},{6,14},{8,0},{10,2},{12,4},{14,6},{16,24},{18,... | collective-permute-start | bytes 196616 | tf_op jit(solution)/shard_map/ppermute | solution.py:318
  29.6 1.9 %cross_coefficients.8.refs_1_.refs_4_ = f32[56,4096]{1,0:T(8,128)S(1)} custom-call(s32[1]{0:T(128)} %bitcast.meta, bf16[4,4,2,32,128]{4,3,2,1,0:T(8,128)(2,1)S(1)} %stack.2.refs_0_, bf16[8,4,2,128,128]{4,3,2,1,0:T(8,128)(2,1)S(1)} %whiten_block.1.refs_1_.refs_2_, bf16[8,56,128]{2,1,0:T(8,128)(2,1)S(1)} %copy-done.1), custom_call_target="tpu_custom_call" | custom-call | flops 1024 | bytes 1024 | tf_op jit(solution)/shard_map/cross_coefficients/pallas_call | solution.py:222
  31.6 0.3 collective-permute-done.17.refs_2_
  31.9 0.3 collective-permute-done.16.refs_1_
  32.3 0.7 %cross_coefficients.10 = bf16[56,1024]{1,0:T(8,128)(2,1)S(1)} custom-call(s32[1]{0:T(128)} %bitcast.meta, bf16[4,4,2,32,128]{4,3,2,1,0:T(8,128)(2,1)S(1)} %collective-permute-done.8.refs_0_, f32[56,4096]{1,0:T(8,128)S(1)} %cross_coefficients.8.refs_1_.refs_4_, bf16[8,4,2,128,128]{4,3,2,1,0:T(8,128)(2,1)S(1)} %whiten_block.1.refs_1_.refs_2_, ...), custom_call_target="tpu_custom_call" | custom-call | flops 1024 | bytes 1024 | tf_op jit(solution)/shard_map/cross_coefficients/pallas_call | solution.py:222
  33.0 1.6 %collective-permute-start.9 = (bf16[56,1024]{1,0:T(8,128)(2,1)S(1)}, bf16[56,1024]{1,0:T(8,128)(2,1)S(1)}, u32[]{:S(2)}, u32[]{:S(2)}) collective-permute-start(bf16[56,1024]{1,0:T(8,128)(2,1)S(1)} %cross_coefficients.10), channel_id=1, source_target_pairs={{0,1},{1,0},{2,3},{3,2},{4,5},{5,4},{6,7},{7,6},{8,9},{9,8},{10,11... | collective-permute-start | bytes 344072 | tf_op jit(solution)/shard_map/ppermute | solution.py:374
  34.5 0.7 %cross_coefficients.11 = bf16[56,1024]{1,0:T(8,128)(2,1)S(1)} custom-call(s32[1]{0:T(128)} %bitcast.meta, bf16[4,4,2,32,128]{4,3,2,1,0:T(8,128)(2,1)S(1)} %collective-permute-done.8.refs_0_, f32[56,4096]{1,0:T(8,128)S(1)} %cross_coefficients.8.refs_1_.refs_4_, bf16[8,4,2,128,128]{4,3,2,1,0:T(8,128)(2,1)S(1)} %whiten_block.1.refs_1_.refs_2_, ...), custom_call_target="tpu_custom_call" | custom-call | flops 1024 | bytes 1024 | tf_op jit(solution)/shard_map/cross_coefficients/pallas_call | solution.py:222
  35.2 0.6 %collective-permute-start.10 = (bf16[56,1024]{1,0:T(8,128)(2,1)S(1)}, bf16[56,1024]{1,0:T(8,128)(2,1)S(1)}, u32[]{:S(2)}, u32[]{:S(2)}) collective-permute-start(bf16[56,1024]{1,0:T(8,128)(2,1)S(1)} %cross_coefficients.11), channel_id=1, source_target_pairs={{0,1},{1,0},{2,3},{3,2},{4,5},{5,4},{6,7},{7,6},{8,9},{9,8},{10,11... | collective-permute-start | bytes 344072 | tf_op jit(solution)/shard_map/ppermute | solution.py:374
  35.8 1.1 %cross_coefficients.13.refs_1_ = f32[56,2048]{1,0:T(8,128)S(1)} custom-call(s32[1]{0:T(128)} %bitcast.meta, bf16[4,4,2,32,128]{4,3,2,1,0:T(8,128)(2,1)S(1)} %stack.3.refs_0_, bf16[8,4,2,128,128]{4,3,2,1,0:T(8,128)(2,1)S(1)} %whiten_block.1.refs_1_.refs_2_, bf16[8,56,128]{2,1,0:T(8,128)(2,1)S(1)} %copy-done.1), custom_call_target="tpu_custom_call" | custom-call | flops 1024 | bytes 1024 | tf_op jit(solution)/shard_map/cross_coefficients/pallas_call | solution.py:222
  36.9 0.7 %cross_coefficients.14 = bf16[56,1024]{1,0:T(8,128)(2,1)S(1)} custom-call(s32[1]{0:T(128)} %bitcast.meta, bf16[4,4,2,32,128]{4,3,2,1,0:T(8,128)(2,1)S(1)} %collective-permute-done.19.refs_1_.refs_0_, f32[56,2048]{1,0:T(8,128)S(1)} %cross_coefficients.13.refs_1_, bf16[8,4,2,128,128]{4,3,2,1,0:T(8,128)(2,1)S(1)} %whiten_block.1.refs_1_.refs_2_, ...), custom_call_target="tpu_custom_call" | custom-call | flops 1024 | bytes 1024 | tf_op jit(solution)/shard_map/cross_coefficients/pallas_call | solution.py:222
  37.6 1.5 %collective-permute-start.20 = (bf16[56,1024]{1,0:T(8,128)(2,1)S(1)}, bf16[56,1024]{1,0:T(8,128)(2,1)S(1)}, u32[]{:S(2)}, u32[]{:S(2)}) collective-permute-start(bf16[56,1024]{1,0:T(8,128)(2,1)S(1)} %cross_coefficients.14), channel_id=1, source_target_pairs={{0,1},{1,0},{2,3},{3,2},{4,5},{5,4},{6,7},{7,6},{8,9},{9,8},{10,11... | collective-permute-start | bytes 344072 | tf_op jit(solution)/shard_map/ppermute | solution.py:374
  39.1 0.7 %cross_coefficients.15 = bf16[56,1024]{1,0:T(8,128)(2,1)S(1)} custom-call(s32[1]{0:T(128)} %bitcast.meta, bf16[4,4,2,32,128]{4,3,2,1,0:T(8,128)(2,1)S(1)} %collective-permute-done.19.refs_1_.refs_0_, f32[56,2048]{1,0:T(8,128)S(1)} %cross_coefficients.13.refs_1_, bf16[8,4,2,128,128]{4,3,2,1,0:T(8,128)(2,1)S(1)} %whiten_block.1.refs_1_.refs_2_, ...), custom_call_target="tpu_custom_call" | custom-call | flops 1024 | bytes 1024 | tf_op jit(solution)/shard_map/cross_coefficients/pallas_call | solution.py:222
  39.8 0.6 %collective-permute-start.21 = (bf16[56,1024]{1,0:T(8,128)(2,1)S(1)}, bf16[56,1024]{1,0:T(8,128)(2,1)S(1)}, u32[]{:S(2)}, u32[]{:S(2)}) collective-permute-start(bf16[56,1024]{1,0:T(8,128)(2,1)S(1)} %cross_coefficients.15), channel_id=1, source_target_pairs={{0,1},{1,0},{2,3},{3,2},{4,5},{5,4},{6,7},{7,6},{8,9},{9,8},{10,11... | collective-permute-start | bytes 344072 | tf_op jit(solution)/shard_map/ppermute | solution.py:374
  40.4 1.1 %cross_coefficients.9.refs_0_ = f32[56,2048]{1,0:T(8,128)S(1)} custom-call(s32[1]{0:T(128)} %bitcast.meta, bf16[4,4,2,32,128]{4,3,2,1,0:T(8,128)(2,1)S(1)} %collective-permute-done.8.refs_0_, f32[56,4096]{1,0:T(8,128)S(1)} %cross_coefficients.8.refs_1_.refs_4_, bf16[8,4,2,128,128]{4,3,2,1,0:T(8,128)(2,1)S(1)} %whiten_block.1.refs_1_.refs_2_, ...), custom_call_target="tpu_custom_call" | custom-call | flops 1024 | bytes 1024 | tf_op jit(solution)/shard_map/cross_coefficients/pallas_call | solution.py:222
  41.5 2.0 %cross_coefficients.12.refs_1_ = f32[56,2048]{1,0:T(8,128)S(1)} custom-call(s32[1]{0:T(128)} %bitcast.meta, bf16[4,4,2,32,128]{4,3,2,1,0:T(8,128)(2,1)S(1)} %stack.3.refs_0_, bf16[4,4,2,32,128]{4,3,2,1,0:T(8,128)(2,1)S(1)} %collective-permute-done.19.refs_1_.refs_0_, bf16[8,4,2,128,128]{4,3,2,1,0:T(8,128)(2,1)S(1)} %whiten_block.1.refs_1_.refs_2_, ...), custom_call_target="tpu_custom_call" | custom-call | flops 1024 | bytes 1024 | tf_op jit(solution)/shard_map/cross_coefficients/pallas_call | solution.py:222
  43.6 1.3 %lags.3.refs_0_ = f32[32,128,128]{2,1,0:T(8,128)} custom-call(f32[56,2048]{1,0:T(8,128)S(1)} %cross_coefficients.9.refs_0_, bf16[56,1024]{1,0:T(8,128)(2,1)S(1)} %collective-permute-done.9.refs_1_, bf16[56,1024]{1,0:T(8,128)(2,1)S(1)} %collective-permute-done.10.refs_2_, bf16[168,128]{1,0:T(8,128)(2,1)S(1)} %copy-done.2), custom_call_target="tpu_custom_call" | custom-call | flops 268435456 | bytes 1024 | tf_op jit(solution)/shard_map/lags/pallas_call | solution.py:275
  44.9 1.1 %lags.4.refs_0_ = f32[32,128,128]{2,1,0:T(8,128)} custom-call(f32[32,128,128]{2,1,0:T(8,128)} %lags.3.refs_0_, f32[56,2048]{1,0:T(8,128)S(1)} %cross_coefficients.12.refs_1_, bf16[56,1024]{1,0:T(8,128)(2,1)S(1)} %collective-permute-done.20.refs_2_, bf16[168,128]{1,0:T(8,128)(2,1)S(1)} %copy-done.2), custom_call_target="tpu_custom_call", output_to_operand_aliasing={{}: (0, {})} | custom-call | flops 268435456 | bytes 1024 | tf_op jit(solution)/shard_map/lags/pallas_call | solution.py:275
  46.0 1.1 %lags.5 = f32[32,128,128]{2,1,0:T(8,128)} custom-call(f32[32,128,128]{2,1,0:T(8,128)} %lags.4.refs_0_, f32[56,2048]{1,0:T(8,128)S(1)} %cross_coefficients.12.refs_1_, bf16[56,1024]{1,0:T(8,128)(2,1)S(1)} %collective-permute-done.21.refs_2_, bf16[168,128]{1,0:T(8,128)(2,1)S(1)} %copy-done.2), custom_call_target="tpu_custom_call", output_to_operand_aliasing={{}: (0, {})} | custom-call | flops 268435456 | bytes 1024 | tf_op jit(solution)/shard_map/lags/pallas_call | solution.py:275
  (42 shorter events, 1.1 us)
Async XLA Ops:
  1.9 2.6 %collective-permute-start = (bf16[4,4,2,32,128]{4,3,2,1,0:T(8,128)(2,1)S(1)}, bf16[4,4,2,32,128]{4,3,2,1,0:T(8,128)(2,1)S(1)}, u32[]{:S(2)}, u32[]{:S(2)}) collective-permute-start(bf16[4,4,2,32,128]{4,3,2,1,0:T(8,128)(2,1)S(1)} %get-tuple-element.16), channel_id=1, source_target_pairs={{0,2},{2,0},{4,6},{6,4},{8,10},{10,8},{12,14},{14,12},{16,18},{18,... | collective-permute-start | bytes 786440 | tf_op jit(solution)/shard_map/ppermute | solution.py:318
  2.4 6.9 %collective-permute-start.11 = (bf16[4,4,2,32,128]{4,3,2,1,0:T(8,128)(2,1)S(1)}, bf16[4,4,2,32,128]{4,3,2,1,0:T(8,128)(2,1)S(1)}, u32[]{:S(2)}, u32[]{:S(2)}) collective-permute-start(bf16[4,4,2,32,128]{4,3,2,1,0:T(8,128)(2,1)S(1)} %get-tuple-element.24), channel_id=1, source_target_pairs={{0,2},{2,0},{4,6},{6,4},{8,10},{10,8},{12,14},{14,12},{16,18},{18,... | collective-permute-start | bytes 786440 | tf_op jit(solution)/shard_map/ppermute | solution.py:318
  2.4 10.3 %copy-start = (bf16[2,512,8,128]{3,2,1,0:T(8,128)(2,1)S(1)}, bf16[2,512,8,128]{3,2,1,0:T(8,128)(2,1)}, u32[]{:S(2)}) copy-start(bf16[2,512,8,128]{3,2,1,0:T(8,128)(2,1)} %spectra.4) | copy-start | bytes 6291460
  4.6 9.7 %collective-permute-start.3 = (bf16[4,2,32,128]{3,2,1,0:T(8,128)(2,1)S(1)}, bf16[4,2,32,128]{3,2,1,0:T(8,128)(2,1)S(1)}, u32[]{:S(2)}, u32[]{:S(2)}) collective-permute-start(bf16[4,2,32,128]{3,2,1,0:T(8,128)(2,1)S(1)} %get-tuple-element.28), channel_id=1, source_target_pairs={{0,12},{2,14},{4,8},{6,10},{8,4},{10,6},{12,0},{14,2},{16,28},{18,... | collective-permute-start | bytes 196616 | tf_op jit(solution)/shard_map/ppermute | solution.py:318
  8.6 5.9 %collective-permute-start.2 = (bf16[4,2,32,128]{3,2,1,0:T(8,128)(2,1)S(1)}, bf16[4,2,32,128]{3,2,1,0:T(8,128)(2,1)S(1)}, u32[]{:S(2)}, u32[]{:S(2)}) collective-permute-start(bf16[4,2,32,128]{3,2,1,0:T(8,128)(2,1)S(1)} %get-tuple-element.29), channel_id=1, source_target_pairs={{0,4},{2,6},{4,0},{6,2},{8,12},{10,14},{12,8},{14,10},{16,20},{18,... | collective-permute-start | bytes 196616 | tf_op jit(solution)/shard_map/ppermute | solution.py:318
  9.1 5.4 %collective-permute-start.1 = (bf16[4,2,32,128]{3,2,1,0:T(8,128)(2,1)S(1)}, bf16[4,2,32,128]{3,2,1,0:T(8,128)(2,1)S(1)}, u32[]{:S(2)}, u32[]{:S(2)}) collective-permute-start(bf16[4,2,32,128]{3,2,1,0:T(8,128)(2,1)S(1)} %get-tuple-element.30), channel_id=1, source_target_pairs={{0,8},{2,10},{4,12},{6,14},{8,0},{10,2},{12,4},{14,6},{16,24},{18,... | collective-permute-start | bytes 196616 | tf_op jit(solution)/shard_map/ppermute | solution.py:318
  9.4 9.2 %collective-permute-start.12 = (bf16[4,2,32,128]{3,2,1,0:T(8,128)(2,1)S(1)}, bf16[4,2,32,128]{3,2,1,0:T(8,128)(2,1)S(1)}, u32[]{:S(2)}, u32[]{:S(2)}) collective-permute-start(bf16[4,2,32,128]{3,2,1,0:T(8,128)(2,1)S(1)} %get-tuple-element.25), channel_id=1, source_target_pairs={{0,8},{2,10},{4,12},{6,14},{8,0},{10,2},{12,4},{14,6},{16,24},{18,... | collective-permute-start | bytes 196616 | tf_op jit(solution)/shard_map/ppermute | solution.py:318
  11.3 7.2 %collective-permute-start.14 = (bf16[4,2,32,128]{3,2,1,0:T(8,128)(2,1)S(1)}, bf16[4,2,32,128]{3,2,1,0:T(8,128)(2,1)S(1)}, u32[]{:S(2)}, u32[]{:S(2)}) collective-permute-start(bf16[4,2,32,128]{3,2,1,0:T(8,128)(2,1)S(1)} %get-tuple-element.26), channel_id=1, source_target_pairs={{0,12},{2,14},{4,8},{6,10},{8,4},{10,6},{12,0},{14,2},{16,28},{18,... | collective-permute-start | bytes 196616 | tf_op jit(solution)/shard_map/ppermute | solution.py:318
  12.7 16.9 %copy-start.1 = (bf16[8,56,128]{2,1,0:T(8,128)(2,1)S(1)}, bf16[8,56,128]{2,1,0:T(8,128)(2,1)}, u32[]{:S(2)}) copy-start(bf16[8,56,128]{2,1,0:T(8,128)(2,1)} %constant.22.refs_2_.refs_3_) | copy-start | bytes 344068
  14.3 4.3 %collective-permute-start.13 = (bf16[4,2,32,128]{3,2,1,0:T(8,128)(2,1)S(1)}, bf16[4,2,32,128]{3,2,1,0:T(8,128)(2,1)S(1)}, u32[]{:S(2)}, u32[]{:S(2)}) collective-permute-start(bf16[4,2,32,128]{3,2,1,0:T(8,128)(2,1)S(1)} %get-tuple-element.27), channel_id=1, source_target_pairs={{0,4},{2,6},{4,0},{6,2},{8,12},{10,14},{12,8},{14,10},{16,20},{18,... | collective-permute-start | bytes 196616 | tf_op jit(solution)/shard_map/ppermute | solution.py:318
  14.5 7.7 %collective-permute-start.4 = (bf16[4,2,32,128]{3,2,1,0:T(8,128)(2,1)S(1)}, bf16[4,2,32,128]{3,2,1,0:T(8,128)(2,1)S(1)}, u32[]{:S(2)}, u32[]{:S(2)}) collective-permute-start(bf16[4,2,32,128]{3,2,1,0:T(8,128)(2,1)S(1)} %fusion.4.left), channel_id=1, source_target_pairs={{0,24},{2,26},{4,28},{6,30},{8,16},{10,18},{12,20},{14,22},{16,8},... | collective-permute-start | bytes 196616 | tf_op jit(solution)/shard_map/ppermute | solution.py:318
  18.6 7.3 %collective-permute-start.15 = (bf16[4,2,32,128]{3,2,1,0:T(8,128)(2,1)S(1)}, bf16[4,2,32,128]{3,2,1,0:T(8,128)(2,1)S(1)}, u32[]{:S(2)}, u32[]{:S(2)}) collective-permute-start(bf16[4,2,32,128]{3,2,1,0:T(8,128)(2,1)S(1)} %fusion.2.left), channel_id=1, source_target_pairs={{0,24},{2,26},{4,28},{6,30},{8,16},{10,18},{12,20},{14,22},{16,8},... | collective-permute-start | bytes 196616 | tf_op jit(solution)/shard_map/ppermute | solution.py:318
  22.3 5.6 %collective-permute-start.7 = (bf16[4,2,32,128]{3,2,1,0:T(8,128)(2,1)S(1)}, bf16[4,2,32,128]{3,2,1,0:T(8,128)(2,1)S(1)}, u32[]{:S(2)}, u32[]{:S(2)}) collective-permute-start(bf16[4,2,32,128]{3,2,1,0:T(8,128)(2,1)S(1)} %whiten_sources.2.refs_0_), channel_id=1, source_target_pairs={{0,12},{2,14},{4,8},{6,10},{8,4},{10,6},{12,0},{14,2},{16,28},{18,... | collective-permute-start | bytes 196616 | tf_op jit(solution)/shard_map/ppermute | solution.py:318
  23.9 5.6 %collective-permute-start.6 = (bf16[4,2,32,128]{3,2,1,0:T(8,128)(2,1)S(1)}, bf16[4,2,32,128]{3,2,1,0:T(8,128)(2,1)S(1)}, u32[]{:S(2)}, u32[]{:S(2)}) collective-permute-start(bf16[4,2,32,128]{3,2,1,0:T(8,128)(2,1)S(1)} %whiten_sources.2.refs_0_), channel_id=1, source_target_pairs={{0,4},{2,6},{4,0},{6,2},{8,12},{10,14},{12,8},{14,10},{16,20},{18,... | collective-permute-start | bytes 196616 | tf_op jit(solution)/shard_map/ppermute | solution.py:318
  23.9 5.6 %collective-permute-start.5 = (bf16[4,2,32,128]{3,2,1,0:T(8,128)(2,1)S(1)}, bf16[4,2,32,128]{3,2,1,0:T(8,128)(2,1)S(1)}, u32[]{:S(2)}, u32[]{:S(2)}) collective-permute-start(bf16[4,2,32,128]{3,2,1,0:T(8,128)(2,1)S(1)} %whiten_sources.2.refs_0_), channel_id=1, source_target_pairs={{0,8},{2,10},{4,12},{6,14},{8,0},{10,2},{12,4},{14,6},{16,24},{18,... | collective-permute-start | bytes 196616 | tf_op jit(solution)/shard_map/ppermute | solution.py:318
  25.9 5.6 %collective-permute-start.18 = (bf16[4,2,32,128]{3,2,1,0:T(8,128)(2,1)S(1)}, bf16[4,2,32,128]{3,2,1,0:T(8,128)(2,1)S(1)}, u32[]{:S(2)}, u32[]{:S(2)}) collective-permute-start(bf16[4,2,32,128]{3,2,1,0:T(8,128)(2,1)S(1)} %whiten_sources.3.refs_0_), channel_id=1, source_target_pairs={{0,12},{2,14},{4,8},{6,10},{8,4},{10,6},{12,0},{14,2},{16,28},{18,... | collective-permute-start | bytes 196616 | tf_op jit(solution)/shard_map/ppermute | solution.py:318
  27.6 4.3 %collective-permute-start.17 = (bf16[4,2,32,128]{3,2,1,0:T(8,128)(2,1)S(1)}, bf16[4,2,32,128]{3,2,1,0:T(8,128)(2,1)S(1)}, u32[]{:S(2)}, u32[]{:S(2)}) collective-permute-start(bf16[4,2,32,128]{3,2,1,0:T(8,128)(2,1)S(1)} %whiten_sources.3.refs_0_), channel_id=1, source_target_pairs={{0,4},{2,6},{4,0},{6,2},{8,12},{10,14},{12,8},{14,10},{16,20},{18,... | collective-permute-start | bytes 196616 | tf_op jit(solution)/shard_map/ppermute | solution.py:318
  28.0 4.3 %collective-permute-start.16 = (bf16[4,2,32,128]{3,2,1,0:T(8,128)(2,1)S(1)}, bf16[4,2,32,128]{3,2,1,0:T(8,128)(2,1)S(1)}, u32[]{:S(2)}, u32[]{:S(2)}) collective-permute-start(bf16[4,2,32,128]{3,2,1,0:T(8,128)(2,1)S(1)} %whiten_sources.3.refs_0_), channel_id=1, source_target_pairs={{0,8},{2,10},{4,12},{6,14},{8,0},{10,2},{12,4},{14,6},{16,24},{18,... | collective-permute-start | bytes 196616 | tf_op jit(solution)/shard_map/ppermute | solution.py:318
  29.5 2.8 %collective-permute-start.8 = (bf16[4,4,2,32,128]{4,3,2,1,0:T(8,128)(2,1)S(1)}, bf16[4,4,2,32,128]{4,3,2,1,0:T(8,128)(2,1)S(1)}, u32[]{:S(2)}, u32[]{:S(2)}) collective-permute-start(bf16[4,4,2,32,128]{4,3,2,1,0:T(8,128)(2,1)S(1)} %stack.2.refs_0_), channel_id=1, source_target_pairs={{0,2},{2,0},{4,6},{6,4},{8,10},{10,8},{12,14},{14,12},{16,18},{18,... | collective-permute-start | bytes 786440 | tf_op jit(solution)/shard_map/ppermute | solution.py:318
  32.2 4.7 %collective-permute-start.19 = (bf16[4,4,2,32,128]{4,3,2,1,0:T(8,128)(2,1)S(1)}, bf16[4,4,2,32,128]{4,3,2,1,0:T(8,128)(2,1)S(1)}, u32[]{:S(2)}, u32[]{:S(2)}) collective-permute-start(bf16[4,4,2,32,128]{4,3,2,1,0:T(8,128)(2,1)S(1)} %stack.3.refs_0_), channel_id=1, source_target_pairs={{0,2},{2,0},{4,6},{6,4},{8,10},{10,8},{12,14},{14,12},{16,18},{18,... | collective-permute-start | bytes 786440 | tf_op jit(solution)/shard_map/ppermute | solution.py:318
  33.0 10.6 %collective-permute-start.9 = (bf16[56,1024]{1,0:T(8,128)(2,1)S(1)}, bf16[56,1024]{1,0:T(8,128)(2,1)S(1)}, u32[]{:S(2)}, u32[]{:S(2)}) collective-permute-start(bf16[56,1024]{1,0:T(8,128)(2,1)S(1)} %cross_coefficients.10), channel_id=1, source_target_pairs={{0,1},{1,0},{2,3},{3,2},{4,5},{5,4},{6,7},{7,6},{8,9},{9,8},{10,11... | collective-permute-start | bytes 344072 | tf_op jit(solution)/shard_map/ppermute | solution.py:374
  35.2 8.4 %collective-permute-start.10 = (bf16[56,1024]{1,0:T(8,128)(2,1)S(1)}, bf16[56,1024]{1,0:T(8,128)(2,1)S(1)}, u32[]{:S(2)}, u32[]{:S(2)}) collective-permute-start(bf16[56,1024]{1,0:T(8,128)(2,1)S(1)} %cross_coefficients.11), channel_id=1, source_target_pairs={{0,1},{1,0},{2,3},{3,2},{4,5},{5,4},{6,7},{7,6},{8,9},{9,8},{10,11... | collective-permute-start | bytes 344072 | tf_op jit(solution)/shard_map/ppermute | solution.py:374
  37.6 7.3 %collective-permute-start.20 = (bf16[56,1024]{1,0:T(8,128)(2,1)S(1)}, bf16[56,1024]{1,0:T(8,128)(2,1)S(1)}, u32[]{:S(2)}, u32[]{:S(2)}) collective-permute-start(bf16[56,1024]{1,0:T(8,128)(2,1)S(1)} %cross_coefficients.14), channel_id=1, source_target_pairs={{0,1},{1,0},{2,3},{3,2},{4,5},{5,4},{6,7},{7,6},{8,9},{9,8},{10,11... | collective-permute-start | bytes 344072 | tf_op jit(solution)/shard_map/ppermute | solution.py:374
  39.8 6.2 %collective-permute-start.21 = (bf16[56,1024]{1,0:T(8,128)(2,1)S(1)}, bf16[56,1024]{1,0:T(8,128)(2,1)S(1)}, u32[]{:S(2)}, u32[]{:S(2)}) collective-permute-start(bf16[56,1024]{1,0:T(8,128)(2,1)S(1)} %cross_coefficients.15), channel_id=1, source_target_pairs={{0,1},{1,0},{2,3},{3,2},{4,5},{5,4},{6,7},{7,6},{8,9},{9,8},{10,11... | collective-permute-start | bytes 344072 | tf_op jit(solution)/shard_map/ppermute | solution.py:374
  41.5 2.1 %copy-start.2 = (bf16[168,128]{1,0:T(8,128)(2,1)S(1)}, bf16[168,128]{1,0:T(8,128)(2,1)}, u32[]{:S(2)}) copy-start(bf16[168,128]{1,0:T(8,128)(2,1)} %constant.19.clone.refs_3_) | copy-start | bytes 129028

commit v4 on v3

--- a/solution.py
+++ b/solution.py
@@ -280,7 +280,7 @@
         input_output_aliases=aliases,
         scratch_shapes=[
             pltpu.VMEM((count, 128, LAGS), jnp.float32),
-            pltpu.SemaphoreType.DMA((count // math.gcd(4, count),)),
+            pltpu.SemaphoreType.DMA((count // math.gcd(2, count),)),
         ],
         compiler_params=pltpu.CompilerParams(vmem_limit_bytes=VMEM_LIMIT),
         cost_estimate=pl.CostEstimate(flops=cost, bytes_accessed=1 << 10, transcendentals=0),

time: 47.2 us -> 47.2 us (level)
  transfers between devices with their start and end apart: 22 -> 22, of which waited for: 4 -> 4; matrix products, arithmetic and copies ran while one was open for 0% -> 0% of each run, Pallas kernels for 31% -> 32%
where the time goes in v4:
time: 47.2 us; the launch traced here: 47 us
  starting transfers between devices  27.7 us (59%)
  Pallas kernels  17.7 us (38%)
  waiting for transfers between devices  1.13 us (2%)
    ppermute x18, starting transfers between devices, across(): return lax.ppermute(block, 'chan', [(i, i ^ mask) for i in range(size)])  23.4 us
    pallas_call x8, Pallas kernels, coefficients(): pl.pallas_call(functools.partial(cross_kernel, places, first, begun, len(...  8.8 us
    ppermute x4, starting transfers between devices, per_device(): lax.ppermute(part, ('tm', 'freq'), [(m, m ^ d + 1) for m in range(shards)])  4.31 us
    pallas_call x2, Pallas kernels, pick(): pl.pallas_call(functools.partial(pick_kernel, shards, side), in_specs=[pl...  3.84 us
    pallas_call x3, Pallas kernels, to_lags(): pl.pallas_call(functools.partial(lags_kernel, (len(blocks), len(blocks[0]...  3.42 us
    pallas_call x1, Pallas kernels, whiten(): pl.pallas_call(whiten_kernel, grid_spec=pltpu.PrefetchScalarGridSpec(num_...  1.52 us
    ppermute x18, waiting for transfers between devices, across(): return lax.ppermute(block, 'chan', [(i, i ^ mask) for i in range(size)])  1.11 us
  transfers between devices with their start and end apart: 22, of which 4 were waited for; matrix products, arithmetic and copies ran while one was open for 0% of the time, Pallas kernels for 32%

profile of v4, /device:TPU:0, one launch (start us, length us, event | category | flops | bytes accessed | tf_op | source)
XLA Modules:
  0.0 47.0 jit_solution(9670139843197180544)
XLA Ops:
  0.0 1.8 %pick_sources.3 = (bf16[4,4,2,32,128]{4,3,2,1,0:T(8,128)(2,1)S(1)}, bf16[4,4,2,32,128]{4,3,2,1,0:T(8,128)(2,1)S(1)}) custom-call(s32[4]{0:T(128)} %owners_in.3, s32[4,16]{1,0:T(4,128)} %rows_in.3, bf16[2,512,8,128]{3,2,1,0:T(8,128)(2,1)} %spectra.4), custom_call_target="tpu_custom_call" | custom-call | flops 33554432 | bytes 2097152 | tf_op jit(solution)/shard_map/pick_sources/pallas_call | solution.py:97
  1.9 0.5 %collective-permute-start = (bf16[4,4,2,32,128]{4,3,2,1,0:T(8,128)(2,1)S(1)}, bf16[4,4,2,32,128]{4,3,2,1,0:T(8,128)(2,1)S(1)}, u32[]{:S(2)}, u32[]{:S(2)}) collective-permute-start(bf16[4,4,2,32,128]{4,3,2,1,0:T(8,128)(2,1)S(1)} %get-tuple-element.16), channel_id=1, source_target_pairs={{0,2},{2,0},{4,6},{6,4},{8,10},{10,8},{12,14},{14,12},{16,18},{18,... | collective-permute-start | bytes 786440 | tf_op jit(solution)/shard_map/ppermute | solution.py:318
  2.4 2.0 %pick_sources.2 = (bf16[4,4,2,32,128]{4,3,2,1,0:T(8,128)(2,1)S(1)}, bf16[4,4,2,32,128]{4,3,2,1,0:T(8,128)(2,1)S(1)}) custom-call(s32[4]{0:T(128)} %owners_in.3, s32[4,16]{1,0:T(4,128)} %rows_in.3, bf16[2,512,8,128]{3,2,1,0:T(8,128)(2,1)} %spectra.4), custom_call_target="tpu_custom_call" | custom-call | flops 33554432 | bytes 2097152 | tf_op jit(solution)/shard_map/pick_sources/pallas_call | solution.py:97
  4.6 4.0 %collective-permute-start.3 = (bf16[4,2,32,128]{3,2,1,0:T(8,128)(2,1)S(1)}, bf16[4,2,32,128]{3,2,1,0:T(8,128)(2,1)S(1)}, u32[]{:S(2)}, u32[]{:S(2)}) collective-permute-start(bf16[4,2,32,128]{3,2,1,0:T(8,128)(2,1)S(1)} %get-tuple-element.28), channel_id=1, source_target_pairs={{0,12},{2,14},{4,8},{6,10},{8,4},{10,6},{12,0},{14,2},{16,28},{18,... | collective-permute-start | bytes 196616 | tf_op jit(solution)/shard_map/ppermute | solution.py:318
  8.6 0.5 %collective-permute-start.2 = (bf16[4,2,32,128]{3,2,1,0:T(8,128)(2,1)S(1)}, bf16[4,2,32,128]{3,2,1,0:T(8,128)(2,1)S(1)}, u32[]{:S(2)}, u32[]{:S(2)}) collective-permute-start(bf16[4,2,32,128]{3,2,1,0:T(8,128)(2,1)S(1)} %get-tuple-element.29), channel_id=1, source_target_pairs={{0,4},{2,6},{4,0},{6,2},{8,12},{10,14},{12,8},{14,10},{16,20},{18,... | collective-permute-start | bytes 196616 | tf_op jit(solution)/shard_map/ppermute | solution.py:318
  9.4 1.9 %collective-permute-start.12 = (bf16[4,2,32,128]{3,2,1,0:T(8,128)(2,1)S(1)}, bf16[4,2,32,128]{3,2,1,0:T(8,128)(2,1)S(1)}, u32[]{:S(2)}, u32[]{:S(2)}) collective-permute-start(bf16[4,2,32,128]{3,2,1,0:T(8,128)(2,1)S(1)} %get-tuple-element.25), channel_id=1, source_target_pairs={{0,8},{2,10},{4,12},{6,14},{8,0},{10,2},{12,4},{14,6},{16,24},{18,... | collective-permute-start | bytes 196616 | tf_op jit(solution)/shard_map/ppermute | solution.py:318
  11.3 1.4 %collective-permute-start.14 = (bf16[4,2,32,128]{3,2,1,0:T(8,128)(2,1)S(1)}, bf16[4,2,32,128]{3,2,1,0:T(8,128)(2,1)S(1)}, u32[]{:S(2)}, u32[]{:S(2)}) collective-permute-start(bf16[4,2,32,128]{3,2,1,0:T(8,128)(2,1)S(1)} %get-tuple-element.26), channel_id=1, source_target_pairs={{0,12},{2,14},{4,8},{6,10},{8,4},{10,6},{12,0},{14,2},{16,28},{18,... | collective-permute-start | bytes 196616 | tf_op jit(solution)/shard_map/ppermute | solution.py:318
  12.7 1.5 %whiten_block.1.refs_1_.refs_2_ = bf16[8,4,2,128,128]{4,3,2,1,0:T(8,128)(2,1)S(1)} custom-call(s32[1]{0:T(128)} %bitcast.meta, bf16[2,512,8,128]{3,2,1,0:T(8,128)(2,1)S(1)} %copy-done), custom_call_target="tpu_custom_call" | custom-call | flops 16777216 | bytes 4194304 | tf_op jit(solution)/shard_map/whiten_block/pallas_call | solution.py:153
  14.5 4.0 %collective-permute-start.4 = (bf16[4,2,32,128]{3,2,1,0:T(8,128)(2,1)S(1)}, bf16[4,2,32,128]{3,2,1,0:T(8,128)(2,1)S(1)}, u32[]{:S(2)}, u32[]{:S(2)}) collective-permute-start(bf16[4,2,32,128]{3,2,1,0:T(8,128)(2,1)S(1)} %fusion.4.left), channel_id=1, source_target_pairs={{0,24},{2,26},{4,28},{6,30},{8,16},{10,18},{12,20},{14,22},{16,8},... | collective-permute-start | bytes 196616 | tf_op jit(solution)/shard_map/ppermute | solution.py:318
  18.6 3.7 %collective-permute-start.15 = (bf16[4,2,32,128]{3,2,1,0:T(8,128)(2,1)S(1)}, bf16[4,2,32,128]{3,2,1,0:T(8,128)(2,1)S(1)}, u32[]{:S(2)}, u32[]{:S(2)}) collective-permute-start(bf16[4,2,32,128]{3,2,1,0:T(8,128)(2,1)S(1)} %fusion.2.left), channel_id=1, source_target_pairs={{0,24},{2,26},{4,28},{6,30},{8,16},{10,18},{12,20},{14,22},{16,8},... | collective-permute-start | bytes 196616 | tf_op jit(solution)/shard_map/ppermute | solution.py:318
  22.3 1.6 %collective-permute-start.7 = (bf16[4,2,32,128]{3,2,1,0:T(8,128)(2,1)S(1)}, bf16[4,2,32,128]{3,2,1,0:T(8,128)(2,1)S(1)}, u32[]{:S(2)}, u32[]{:S(2)}) collective-permute-start(bf16[4,2,32,128]{3,2,1,0:T(8,128)(2,1)S(1)} %whiten_sources.2.refs_0_), channel_id=1, source_target_pairs={{0,12},{2,14},{4,8},{6,10},{8,4},{10,6},{12,0},{14,2},{16,28},{18,... | collective-permute-start | bytes 196616 | tf_op jit(solution)/shard_map/ppermute | solution.py:318
  23.9 1.9 %collective-permute-start.5 = (bf16[4,2,32,128]{3,2,1,0:T(8,128)(2,1)S(1)}, bf16[4,2,32,128]{3,2,1,0:T(8,128)(2,1)S(1)}, u32[]{:S(2)}, u32[]{:S(2)}) collective-permute-start(bf16[4,2,32,128]{3,2,1,0:T(8,128)(2,1)S(1)} %whiten_sources.2.refs_0_), channel_id=1, source_target_pairs={{0,8},{2,10},{4,12},{6,14},{8,0},{10,2},{12,4},{14,6},{16,24},{18,... | collective-permute-start | bytes 196616 | tf_op jit(solution)/shard_map/ppermute | solution.py:318
  25.9 1.6 %collective-permute-start.18 = (bf16[4,2,32,128]{3,2,1,0:T(8,128)(2,1)S(1)}, bf16[4,2,32,128]{3,2,1,0:T(8,128)(2,1)S(1)}, u32[]{:S(2)}, u32[]{:S(2)}) collective-permute-start(bf16[4,2,32,128]{3,2,1,0:T(8,128)(2,1)S(1)} %whiten_sources.3.refs_0_), channel_id=1, source_target_pairs={{0,12},{2,14},{4,8},{6,10},{8,4},{10,6},{12,0},{14,2},{16,28},{18,... | collective-permute-start | bytes 196616 | tf_op jit(solution)/shard_map/ppermute | solution.py:318
  27.6 0.4 collective-permute-done.7.refs_3_
  28.0 1.6 %collective-permute-start.16 = (bf16[4,2,32,128]{3,2,1,0:T(8,128)(2,1)S(1)}, bf16[4,2,32,128]{3,2,1,0:T(8,128)(2,1)S(1)}, u32[]{:S(2)}, u32[]{:S(2)}) collective-permute-start(bf16[4,2,32,128]{3,2,1,0:T(8,128)(2,1)S(1)} %whiten_sources.3.refs_0_), channel_id=1, source_target_pairs={{0,8},{2,10},{4,12},{6,14},{8,0},{10,2},{12,4},{14,6},{16,24},{18,... | collective-permute-start | bytes 196616 | tf_op jit(solution)/shard_map/ppermute | solution.py:318
  29.6 1.9 %cross_coefficients.8.refs_1_.refs_4_ = f32[56,4096]{1,0:T(8,128)S(1)} custom-call(s32[1]{0:T(128)} %bitcast.meta, bf16[4,4,2,32,128]{4,3,2,1,0:T(8,128)(2,1)S(1)} %stack.2.refs_0_, bf16[8,4,2,128,128]{4,3,2,1,0:T(8,128)(2,1)S(1)} %whiten_block.1.refs_1_.refs_2_, bf16[8,56,128]{2,1,0:T(8,128)(2,1)S(1)} %copy-done.1), custom_call_target="tpu_custom_call" | custom-call | flops 1024 | bytes 1024 | tf_op jit(solution)/shard_map/cross_coefficients/pallas_call | solution.py:222
  31.6 0.3 collective-permute-done.17.refs_2_
  31.9 0.3 collective-permute-done.16.refs_1_
  32.3 0.7 %cross_coefficients.10 = bf16[56,1024]{1,0:T(8,128)(2,1)S(1)} custom-call(s32[1]{0:T(128)} %bitcast.meta, bf16[4,4,2,32,128]{4,3,2,1,0:T(8,128)(2,1)S(1)} %collective-permute-done.8.refs_0_, f32[56,4096]{1,0:T(8,128)S(1)} %cross_coefficients.8.refs_1_.refs_4_, bf16[8,4,2,128,128]{4,3,2,1,0:T(8,128)(2,1)S(1)} %whiten_block.1.refs_1_.refs_2_, ...), custom_call_target="tpu_custom_call" | custom-call | flops 1024 | bytes 1024 | tf_op jit(solution)/shard_map/cross_coefficients/pallas_call | solution.py:222
  33.0 1.6 %collective-permute-start.9 = (bf16[56,1024]{1,0:T(8,128)(2,1)S(1)}, bf16[56,1024]{1,0:T(8,128)(2,1)S(1)}, u32[]{:S(2)}, u32[]{:S(2)}) collective-permute-start(bf16[56,1024]{1,0:T(8,128)(2,1)S(1)} %cross_coefficients.10), channel_id=1, source_target_pairs={{0,1},{1,0},{2,3},{3,2},{4,5},{5,4},{6,7},{7,6},{8,9},{9,8},{10,11... | collective-permute-start | bytes 344072 | tf_op jit(solution)/shard_map/ppermute | solution.py:374
  34.5 0.7 %cross_coefficients.11 = bf16[56,1024]{1,0:T(8,128)(2,1)S(1)} custom-call(s32[1]{0:T(128)} %bitcast.meta, bf16[4,4,2,32,128]{4,3,2,1,0:T(8,128)(2,1)S(1)} %collective-permute-done.8.refs_0_, f32[56,4096]{1,0:T(8,128)S(1)} %cross_coefficients.8.refs_1_.refs_4_, bf16[8,4,2,128,128]{4,3,2,1,0:T(8,128)(2,1)S(1)} %whiten_block.1.refs_1_.refs_2_, ...), custom_call_target="tpu_custom_call" | custom-call | flops 1024 | bytes 1024 | tf_op jit(solution)/shard_map/cross_coefficients/pallas_call | solution.py:222
  35.2 0.6 %collective-permute-start.10 = (bf16[56,1024]{1,0:T(8,128)(2,1)S(1)}, bf16[56,1024]{1,0:T(8,128)(2,1)S(1)}, u32[]{:S(2)}, u32[]{:S(2)}) collective-permute-start(bf16[56,1024]{1,0:T(8,128)(2,1)S(1)} %cross_coefficients.11), channel_id=1, source_target_pairs={{0,1},{1,0},{2,3},{3,2},{4,5},{5,4},{6,7},{7,6},{8,9},{9,8},{10,11... | collective-permute-start | bytes 344072 | tf_op jit(solution)/shard_map/ppermute | solution.py:374
  35.8 1.1 %cross_coefficients.13.refs_1_ = f32[56,2048]{1,0:T(8,128)S(1)} custom-call(s32[1]{0:T(128)} %bitcast.meta, bf16[4,4,2,32,128]{4,3,2,1,0:T(8,128)(2,1)S(1)} %stack.3.refs_0_, bf16[8,4,2,128,128]{4,3,2,1,0:T(8,128)(2,1)S(1)} %whiten_block.1.refs_1_.refs_2_, bf16[8,56,128]{2,1,0:T(8,128)(2,1)S(1)} %copy-done.1), custom_call_target="tpu_custom_call" | custom-call | flops 1024 | bytes 1024 | tf_op jit(solution)/shard_map/cross_coefficients/pallas_call | solution.py:222
  36.9 0.7 %cross_coefficients.14 = bf16[56,1024]{1,0:T(8,128)(2,1)S(1)} custom-call(s32[1]{0:T(128)} %bitcast.meta, bf16[4,4,2,32,128]{4,3,2,1,0:T(8,128)(2,1)S(1)} %collective-permute-done.19.refs_1_.refs_0_, f32[56,2048]{1,0:T(8,128)S(1)} %cross_coefficients.13.refs_1_, bf16[8,4,2,128,128]{4,3,2,1,0:T(8,128)(2,1)S(1)} %whiten_block.1.refs_1_.refs_2_, ...), custom_call_target="tpu_custom_call" | custom-call | flops 1024 | bytes 1024 | tf_op jit(solution)/shard_map/cross_coefficients/pallas_call | solution.py:222
  37.6 1.5 %collective-permute-start.20 = (bf16[56,1024]{1,0:T(8,128)(2,1)S(1)}, bf16[56,1024]{1,0:T(8,128)(2,1)S(1)}, u32[]{:S(2)}, u32[]{:S(2)}) collective-permute-start(bf16[56,1024]{1,0:T(8,128)(2,1)S(1)} %cross_coefficients.14), channel_id=1, source_target_pairs={{0,1},{1,0},{2,3},{3,2},{4,5},{5,4},{6,7},{7,6},{8,9},{9,8},{10,11... | collective-permute-start | bytes 344072 | tf_op jit(solution)/shard_map/ppermute | solution.py:374
  39.1 0.7 %cross_coefficients.15 = bf16[56,1024]{1,0:T(8,128)(2,1)S(1)} custom-call(s32[1]{0:T(128)} %bitcast.meta, bf16[4,4,2,32,128]{4,3,2,1,0:T(8,128)(2,1)S(1)} %collective-permute-done.19.refs_1_.refs_0_, f32[56,2048]{1,0:T(8,128)S(1)} %cross_coefficients.13.refs_1_, bf16[8,4,2,128,128]{4,3,2,1,0:T(8,128)(2,1)S(1)} %whiten_block.1.refs_1_.refs_2_, ...), custom_call_target="tpu_custom_call" | custom-call | flops 1024 | bytes 1024 | tf_op jit(solution)/shard_map/cross_coefficients/pallas_call | solution.py:222
  39.8 0.6 %collective-permute-start.21 = (bf16[56,1024]{1,0:T(8,128)(2,1)S(1)}, bf16[56,1024]{1,0:T(8,128)(2,1)S(1)}, u32[]{:S(2)}, u32[]{:S(2)}) collective-permute-start(bf16[56,1024]{1,0:T(8,128)(2,1)S(1)} %cross_coefficients.15), channel_id=1, source_target_pairs={{0,1},{1,0},{2,3},{3,2},{4,5},{5,4},{6,7},{7,6},{8,9},{9,8},{10,11... | collective-permute-start | bytes 344072 | tf_op jit(solution)/shard_map/ppermute | solution.py:374
  40.4 1.1 %cross_coefficients.9.refs_0_ = f32[56,2048]{1,0:T(8,128)S(1)} custom-call(s32[1]{0:T(128)} %bitcast.meta, bf16[4,4,2,32,128]{4,3,2,1,0:T(8,128)(2,1)S(1)} %collective-permute-done.8.refs_0_, f32[56,4096]{1,0:T(8,128)S(1)} %cross_coefficients.8.refs_1_.refs_4_, bf16[8,4,2,128,128]{4,3,2,1,0:T(8,128)(2,1)S(1)} %whiten_block.1.refs_1_.refs_2_, ...), custom_call_target="tpu_custom_call" | custom-call | flops 1024 | bytes 1024 | tf_op jit(solution)/shard_map/cross_coefficients/pallas_call | solution.py:222
  41.5 2.0 %cross_coefficients.12.refs_1_ = f32[56,2048]{1,0:T(8,128)S(1)} custom-call(s32[1]{0:T(128)} %bitcast.meta, bf16[4,4,2,32,128]{4,3,2,1,0:T(8,128)(2,1)S(1)} %stack.3.refs_0_, bf16[4,4,2,32,128]{4,3,2,1,0:T(8,128)(2,1)S(1)} %collective-permute-done.19.refs_1_.refs_0_, bf16[8,4,2,128,128]{4,3,2,1,0:T(8,128)(2,1)S(1)} %whiten_block.1.refs_1_.refs_2_, ...), custom_call_target="tpu_custom_call" | custom-call | flops 1024 | bytes 1024 | tf_op jit(solution)/shard_map/cross_coefficients/pallas_call | solution.py:222
  43.6 1.3 %lags.3.refs_0_ = f32[32,128,128]{2,1,0:T(8,128)} custom-call(f32[56,2048]{1,0:T(8,128)S(1)} %cross_coefficients.9.refs_0_, bf16[56,1024]{1,0:T(8,128)(2,1)S(1)} %collective-permute-done.9.refs_1_, bf16[56,1024]{1,0:T(8,128)(2,1)S(1)} %collective-permute-done.10.refs_2_, bf16[168,128]{1,0:T(8,128)(2,1)S(1)} %copy-done.2), custom_call_target="tpu_custom_call" | custom-call | flops 268435456 | bytes 1024 | tf_op jit(solution)/shard_map/lags/pallas_call | solution.py:275
  44.9 1.1 %lags.4.refs_0_ = f32[32,128,128]{2,1,0:T(8,128)} custom-call(f32[32,128,128]{2,1,0:T(8,128)} %lags.3.refs_0_, f32[56,2048]{1,0:T(8,128)S(1)} %cross_coefficients.12.refs_1_, bf16[56,1024]{1,0:T(8,128)(2,1)S(1)} %collective-permute-done.20.refs_2_, bf16[168,128]{1,0:T(8,128)(2,1)S(1)} %copy-done.2), custom_call_target="tpu_custom_call", output_to_operand_aliasing={{}: (0, {})} | custom-call | flops 268435456 | bytes 1024 | tf_op jit(solution)/shard_map/lags/pallas_call | solution.py:275
  46.0 1.1 %lags.5 = f32[32,128,128]{2,1,0:T(8,128)} custom-call(f32[32,128,128]{2,1,0:T(8,128)} %lags.4.refs_0_, f32[56,2048]{1,0:T(8,128)S(1)} %cross_coefficients.12.refs_1_, bf16[56,1024]{1,0:T(8,128)(2,1)S(1)} %collective-permute-done.21.refs_2_, bf16[168,128]{1,0:T(8,128)(2,1)S(1)} %copy-done.2), custom_call_target="tpu_custom_call", output_to_operand_aliasing={{}: (0, {})} | custom-call | flops 268435456 | bytes 1024 | tf_op jit(solution)/shard_map/lags/pallas_call | solution.py:275
  (42 shorter events, 1.1 us)
Async XLA Ops:
  1.9 2.6 %collective-permute-start = (bf16[4,4,2,32,128]{4,3,2,1,0:T(8,128)(2,1)S(1)}, bf16[4,4,2,32,128]{4,3,2,1,0:T(8,128)(2,1)S(1)}, u32[]{:S(2)}, u32[]{:S(2)}) collective-permute-start(bf16[4,4,2,32,128]{4,3,2,1,0:T(8,128)(2,1)S(1)} %get-tuple-element.16), channel_id=1, source_target_pairs={{0,2},{2,0},{4,6},{6,4},{8,10},{10,8},{12,14},{14,12},{16,18},{18,... | collective-permute-start | bytes 786440 | tf_op jit(solution)/shard_map/ppermute | solution.py:318
  2.4 6.9 %collective-permute-start.11 = (bf16[4,4,2,32,128]{4,3,2,1,0:T(8,128)(2,1)S(1)}, bf16[4,4,2,32,128]{4,3,2,1,0:T(8,128)(2,1)S(1)}, u32[]{:S(2)}, u32[]{:S(2)}) collective-permute-start(bf16[4,4,2,32,128]{4,3,2,1,0:T(8,128)(2,1)S(1)} %get-tuple-element.24), channel_id=1, source_target_pairs={{0,2},{2,0},{4,6},{6,4},{8,10},{10,8},{12,14},{14,12},{16,18},{18,... | collective-permute-start | bytes 786440 | tf_op jit(solution)/shard_map/ppermute | solution.py:318
  2.4 10.3 %copy-start = (bf16[2,512,8,128]{3,2,1,0:T(8,128)(2,1)S(1)}, bf16[2,512,8,128]{3,2,1,0:T(8,128)(2,1)}, u32[]{:S(2)}) copy-start(bf16[2,512,8,128]{3,2,1,0:T(8,128)(2,1)} %spectra.4) | copy-start | bytes 6291460
  4.6 9.7 %collective-permute-start.3 = (bf16[4,2,32,128]{3,2,1,0:T(8,128)(2,1)S(1)}, bf16[4,2,32,128]{3,2,1,0:T(8,128)(2,1)S(1)}, u32[]{:S(2)}, u32[]{:S(2)}) collective-permute-start(bf16[4,2,32,128]{3,2,1,0:T(8,128)(2,1)S(1)} %get-tuple-element.28), channel_id=1, source_target_pairs={{0,12},{2,14},{4,8},{6,10},{8,4},{10,6},{12,0},{14,2},{16,28},{18,... | collective-permute-start | bytes 196616 | tf_op jit(solution)/shard_map/ppermute | solution.py:318
  8.6 5.9 %collective-permute-start.2 = (bf16[4,2,32,128]{3,2,1,0:T(8,128)(2,1)S(1)}, bf16[4,2,32,128]{3,2,1,0:T(8,128)(2,1)S(1)}, u32[]{:S(2)}, u32[]{:S(2)}) collective-permute-start(bf16[4,2,32,128]{3,2,1,0:T(8,128)(2,1)S(1)} %get-tuple-element.29), channel_id=1, source_target_pairs={{0,4},{2,6},{4,0},{6,2},{8,12},{10,14},{12,8},{14,10},{16,20},{18,... | collective-permute-start | bytes 196616 | tf_op jit(solution)/shard_map/ppermute | solution.py:318
  9.1 5.4 %collective-permute-start.1 = (bf16[4,2,32,128]{3,2,1,0:T(8,128)(2,1)S(1)}, bf16[4,2,32,128]{3,2,1,0:T(8,128)(2,1)S(1)}, u32[]{:S(2)}, u32[]{:S(2)}) collective-permute-start(bf16[4,2,32,128]{3,2,1,0:T(8,128)(2,1)S(1)} %get-tuple-element.30), channel_id=1, source_target_pairs={{0,8},{2,10},{4,12},{6,14},{8,0},{10,2},{12,4},{14,6},{16,24},{18,... | collective-permute-start | bytes 196616 | tf_op jit(solution)/shard_map/ppermute | solution.py:318
  9.4 9.2 %collective-permute-start.12 = (bf16[4,2,32,128]{3,2,1,0:T(8,128)(2,1)S(1)}, bf16[4,2,32,128]{3,2,1,0:T(8,128)(2,1)S(1)}, u32[]{:S(2)}, u32[]{:S(2)}) collective-permute-start(bf16[4,2,32,128]{3,2,1,0:T(8,128)(2,1)S(1)} %get-tuple-element.25), channel_id=1, source_target_pairs={{0,8},{2,10},{4,12},{6,14},{8,0},{10,2},{12,4},{14,6},{16,24},{18,... | collective-permute-start | bytes 196616 | tf_op jit(solution)/shard_map/ppermute | solution.py:318
  11.3 7.2 %collective-permute-start.14 = (bf16[4,2,32,128]{3,2,1,0:T(8,128)(2,1)S(1)}, bf16[4,2,32,128]{3,2,1,0:T(8,128)(2,1)S(1)}, u32[]{:S(2)}, u32[]{:S(2)}) collective-permute-start(bf16[4,2,32,128]{3,2,1,0:T(8,128)(2,1)S(1)} %get-tuple-element.26), channel_id=1, source_target_pairs={{0,12},{2,14},{4,8},{6,10},{8,4},{10,6},{12,0},{14,2},{16,28},{18,... | collective-permute-start | bytes 196616 | tf_op jit(solution)/shard_map/ppermute | solution.py:318
  12.7 16.9 %copy-start.1 = (bf16[8,56,128]{2,1,0:T(8,128)(2,1)S(1)}, bf16[8,56,128]{2,1,0:T(8,128)(2,1)}, u32[]{:S(2)}) copy-start(bf16[8,56,128]{2,1,0:T(8,128)(2,1)} %constant.22.refs_2_.refs_3_) | copy-start | bytes 344068
  14.3 4.3 %collective-permute-start.13 = (bf16[4,2,32,128]{3,2,1,0:T(8,128)(2,1)S(1)}, bf16[4,2,32,128]{3,2,1,0:T(8,128)(2,1)S(1)}, u32[]{:S(2)}, u32[]{:S(2)}) collective-permute-start(bf16[4,2,32,128]{3,2,1,0:T(8,128)(2,1)S(1)} %get-tuple-element.27), channel_id=1, source_target_pairs={{0,4},{2,6},{4,0},{6,2},{8,12},{10,14},{12,8},{14,10},{16,20},{18,... | collective-permute-start | bytes 196616 | tf_op jit(solution)/shard_map/ppermute | solution.py:318
  14.5 7.7 %collective-permute-start.4 = (bf16[4,2,32,128]{3,2,1,0:T(8,128)(2,1)S(1)}, bf16[4,2,32,128]{3,2,1,0:T(8,128)(2,1)S(1)}, u32[]{:S(2)}, u32[]{:S(2)}) collective-permute-start(bf16[4,2,32,128]{3,2,1,0:T(8,128)(2,1)S(1)} %fusion.4.left), channel_id=1, source_target_pairs={{0,24},{2,26},{4,28},{6,30},{8,16},{10,18},{12,20},{14,22},{16,8},... | collective-permute-start | bytes 196616 | tf_op jit(solution)/shard_map/ppermute | solution.py:318
  18.6 7.3 %collective-permute-start.15 = (bf16[4,2,32,128]{3,2,1,0:T(8,128)(2,1)S(1)}, bf16[4,2,32,128]{3,2,1,0:T(8,128)(2,1)S(1)}, u32[]{:S(2)}, u32[]{:S(2)}) collective-permute-start(bf16[4,2,32,128]{3,2,1,0:T(8,128)(2,1)S(1)} %fusion.2.left), channel_id=1, source_target_pairs={{0,24},{2,26},{4,28},{6,30},{8,16},{10,18},{12,20},{14,22},{16,8},... | collective-permute-start | bytes 196616 | tf_op jit(solution)/shard_map/ppermute | solution.py:318
  22.3 5.6 %collective-permute-start.7 = (bf16[4,2,32,128]{3,2,1,0:T(8,128)(2,1)S(1)}, bf16[4,2,32,128]{3,2,1,0:T(8,128)(2,1)S(1)}, u32[]{:S(2)}, u32[]{:S(2)}) collective-permute-start(bf16[4,2,32,128]{3,2,1,0:T(8,128)(2,1)S(1)} %whiten_sources.2.refs_0_), channel_id=1, source_target_pairs={{0,12},{2,14},{4,8},{6,10},{8,4},{10,6},{12,0},{14,2},{16,28},{18,... | collective-permute-start | bytes 196616 | tf_op jit(solution)/shard_map/ppermute | solution.py:318
  23.9 5.6 %collective-permute-start.6 = (bf16[4,2,32,128]{3,2,1,0:T(8,128)(2,1)S(1)}, bf16[4,2,32,128]{3,2,1,0:T(8,128)(2,1)S(1)}, u32[]{:S(2)}, u32[]{:S(2)}) collective-permute-start(bf16[4,2,32,128]{3,2,1,0:T(8,128)(2,1)S(1)} %whiten_sources.2.refs_0_), channel_id=1, source_target_pairs={{0,4},{2,6},{4,0},{6,2},{8,12},{10,14},{12,8},{14,10},{16,20},{18,... | collective-permute-start | bytes 196616 | tf_op jit(solution)/shard_map/ppermute | solution.py:318
  23.9 5.6 %collective-permute-start.5 = (bf16[4,2,32,128]{3,2,1,0:T(8,128)(2,1)S(1)}, bf16[4,2,32,128]{3,2,1,0:T(8,128)(2,1)S(1)}, u32[]{:S(2)}, u32[]{:S(2)}) collective-permute-start(bf16[4,2,32,128]{3,2,1,0:T(8,128)(2,1)S(1)} %whiten_sources.2.refs_0_), channel_id=1, source_target_pairs={{0,8},{2,10},{4,12},{6,14},{8,0},{10,2},{12,4},{14,6},{16,24},{18,... | collective-permute-start | bytes 196616 | tf_op jit(solution)/shard_map/ppermute | solution.py:318
  25.9 5.6 %collective-permute-start.18 = (bf16[4,2,32,128]{3,2,1,0:T(8,128)(2,1)S(1)}, bf16[4,2,32,128]{3,2,1,0:T(8,128)(2,1)S(1)}, u32[]{:S(2)}, u32[]{:S(2)}) collective-permute-start(bf16[4,2,32,128]{3,2,1,0:T(8,128)(2,1)S(1)} %whiten_sources.3.refs_0_), channel_id=1, source_target_pairs={{0,12},{2,14},{4,8},{6,10},{8,4},{10,6},{12,0},{14,2},{16,28},{18,... | collective-permute-start | bytes 196616 | tf_op jit(solution)/shard_map/ppermute | solution.py:318
  27.6 4.3 %collective-permute-start.17 = (bf16[4,2,32,128]{3,2,1,0:T(8,128)(2,1)S(1)}, bf16[4,2,32,128]{3,2,1,0:T(8,128)(2,1)S(1)}, u32[]{:S(2)}, u32[]{:S(2)}) collective-permute-start(bf16[4,2,32,128]{3,2,1,0:T(8,128)(2,1)S(1)} %whiten_sources.3.refs_0_), channel_id=1, source_target_pairs={{0,4},{2,6},{4,0},{6,2},{8,12},{10,14},{12,8},{14,10},{16,20},{18,... | collective-permute-start | bytes 196616 | tf_op jit(solution)/shard_map/ppermute | solution.py:318
  28.0 4.3 %collective-permute-start.16 = (bf16[4,2,32,128]{3,2,1,0:T(8,128)(2,1)S(1)}, bf16[4,2,32,128]{3,2,1,0:T(8,128)(2,1)S(1)}, u32[]{:S(2)}, u32[]{:S(2)}) collective-permute-start(bf16[4,2,32,128]{3,2,1,0:T(8,128)(2,1)S(1)} %whiten_sources.3.refs_0_), channel_id=1, source_target_pairs={{0,8},{2,10},{4,12},{6,14},{8,0},{10,2},{12,4},{14,6},{16,24},{18,... | collective-permute-start | bytes 196616 | tf_op jit(solution)/shard_map/ppermute | solution.py:318
  29.5 2.8 %collective-permute-start.8 = (bf16[4,4,2,32,128]{4,3,2,1,0:T(8,128)(2,1)S(1)}, bf16[4,4,2,32,128]{4,3,2,1,0:T(8,128)(2,1)S(1)}, u32[]{:S(2)}, u32[]{:S(2)}) collective-permute-start(bf16[4,4,2,32,128]{4,3,2,1,0:T(8,128)(2,1)S(1)} %stack.2.refs_0_), channel_id=1, source_target_pairs={{0,2},{2,0},{4,6},{6,4},{8,10},{10,8},{12,14},{14,12},{16,18},{18,... | collective-permute-start | bytes 786440 | tf_op jit(solution)/shard_map/ppermute | solution.py:318
  32.2 4.7 %collective-permute-start.19 = (bf16[4,4,2,32,128]{4,3,2,1,0:T(8,128)(2,1)S(1)}, bf16[4,4,2,32,128]{4,3,2,1,0:T(8,128)(2,1)S(1)}, u32[]{:S(2)}, u32[]{:S(2)}) collective-permute-start(bf16[4,4,2,32,128]{4,3,2,1,0:T(8,128)(2,1)S(1)} %stack.3.refs_0_), channel_id=1, source_target_pairs={{0,2},{2,0},{4,6},{6,4},{8,10},{10,8},{12,14},{14,12},{16,18},{18,... | collective-permute-start | bytes 786440 | tf_op jit(solution)/shard_map/ppermute | solution.py:318
  33.0 10.6 %collective-permute-start.9 = (bf16[56,1024]{1,0:T(8,128)(2,1)S(1)}, bf16[56,1024]{1,0:T(8,128)(2,1)S(1)}, u32[]{:S(2)}, u32[]{:S(2)}) collective-permute-start(bf16[56,1024]{1,0:T(8,128)(2,1)S(1)} %cross_coefficients.10), channel_id=1, source_target_pairs={{0,1},{1,0},{2,3},{3,2},{4,5},{5,4},{6,7},{7,6},{8,9},{9,8},{10,11... | collective-permute-start | bytes 344072 | tf_op jit(solution)/shard_map/ppermute | solution.py:374
  35.2 8.4 %collective-permute-start.10 = (bf16[56,1024]{1,0:T(8,128)(2,1)S(1)}, bf16[56,1024]{1,0:T(8,128)(2,1)S(1)}, u32[]{:S(2)}, u32[]{:S(2)}) collective-permute-start(bf16[56,1024]{1,0:T(8,128)(2,1)S(1)} %cross_coefficients.11), channel_id=1, source_target_pairs={{0,1},{1,0},{2,3},{3,2},{4,5},{5,4},{6,7},{7,6},{8,9},{9,8},{10,11... | collective-permute-start | bytes 344072 | tf_op jit(solution)/shard_map/ppermute | solution.py:374
  37.6 7.3 %collective-permute-start.20 = (bf16[56,1024]{1,0:T(8,128)(2,1)S(1)}, bf16[56,1024]{1,0:T(8,128)(2,1)S(1)}, u32[]{:S(2)}, u32[]{:S(2)}) collective-permute-start(bf16[56,1024]{1,0:T(8,128)(2,1)S(1)} %cross_coefficients.14), channel_id=1, source_target_pairs={{0,1},{1,0},{2,3},{3,2},{4,5},{5,4},{6,7},{7,6},{8,9},{9,8},{10,11... | collective-permute-start | bytes 344072 | tf_op jit(solution)/shard_map/ppermute | solution.py:374
  39.8 6.2 %collective-permute-start.21 = (bf16[56,1024]{1,0:T(8,128)(2,1)S(1)}, bf16[56,1024]{1,0:T(8,128)(2,1)S(1)}, u32[]{:S(2)}, u32[]{:S(2)}) collective-permute-start(bf16[56,1024]{1,0:T(8,128)(2,1)S(1)} %cross_coefficients.15), channel_id=1, source_target_pairs={{0,1},{1,0},{2,3},{3,2},{4,5},{5,4},{6,7},{7,6},{8,9},{9,8},{10,11... | collective-permute-start | bytes 344072 | tf_op jit(solution)/shard_map/ppermute | solution.py:374
  41.5 2.1 %copy-start.2 = (bf16[168,128]{1,0:T(8,128)(2,1)S(1)}, bf16[168,128]{1,0:T(8,128)(2,1)}, u32[]{:S(2)}) copy-start(bf16[168,128]{1,0:T(8,128)(2,1)} %constant.19.clone.refs_3_) | copy-start | bytes 129028
